TPU v7x, 32 devices: a whole 2x2x4 slice. The times are simulated.
32 devices in a mesh: batch: 8 (over z, core), ctx: 4 (over y, x).
Axes of the slice: x: 2, y: 2, z: 4, core: 2. Of those that a mesh axis runs over, the one named last changes fastest.
Arguments:
- queries: bfloat16 [16384, 1024], P(('batch', 'ctx')), parts along dimension 0, may hold values from -6 to 6
- keys: bfloat16 [16384, 1024], P(('batch', 'ctx')), parts along dimension 0, may hold values from -6 to 6
- values: bfloat16 [16384, 2048], P(('batch', 'ctx')), parts along dimension 0, may hold values from -6 to 6
- out_grad: bfloat16 [16384, 2048], P(('batch', 'ctx')), parts along dimension 0, may hold values from -6 to 6
Outputs:
- attended: bfloat16 [16384, 2048], P(('batch', 'ctx')), parts along dimension 0
- query_grad: bfloat16 [16384, 1024], P(('batch', 'ctx')), parts along dimension 0
- key_grad: bfloat16 [16384, 1024], P(('batch', 'ctx')), parts along dimension 0
- value_grad: bfloat16 [16384, 2048], P(('batch', 'ctx')), parts along dimension 0
There are 8 independent parts, one for each index of `batch`. A program takes and returns all parts, laid end to end along the dimension named above; each array names one. Nothing has to cross between parts.
All inputs are finite; a program needn't handle non-finite values.
Results may differ from a plain program's by a relative error of at most 0.0058.
Values sent between devices are 32-bit elements; how exact they have to be, the bound alone decides.
No kernel may reach another device: no remote copies, remote signals or barrier semaphores. Data moves between devices by JAX's collectives and lax.ppermute only.
A program may use at most 128 MiB of HBM per device.

v0:
```python
import jax
import jax.numpy as jnp
from jax import lax
from jax.sharding import PartitionSpec as P

H = 16
DK = 64
DV = 128


def prefix_2(array, axis, combine, identity, reverse):
    size, mine = (lax.axis_size(axis), lax.axis_index(axis))
    everything = lax.all_gather(array, axis)
    start = jnp.broadcast_to(jnp.asarray(identity, array.dtype), array.shape)

    def turn(k, before):
        at = size - 1 - k if reverse else k
        reached = at > mine if reverse else at < mine
        new = combine(before, everything[at])
        return jnp.where(reached, new, before)

    return lax.fori_loop(0, size, turn, start)


def add_states(earlier, later):
    return earlier + later


def local(queries, keys, values, out_grad):
    length = queries.shape[0]
    query_h = queries.reshape(length, H, DK)
    key_h = keys.reshape(length, H, DK)
    value_h = values.reshape(length, H, DV)
    grad_h = out_grad.reshape(length, H, DV)
    my_block = lax.axis_index("ctx")
    positions = (my_block * length + lax.iota(jnp.int32, length)).astype(jnp.float32)
    scales = 1.0 / jnp.sqrt(DK * (positions + 1.0))
    scaled_grad = (scales[:, None, None] * grad_h.astype(jnp.float32)).astype(jnp.bfloat16)
    key_value = jnp.einsum("thd,thc->hdc", key_h, value_h, preferred_element_type=jnp.float32)
    query_cot = jnp.einsum("thd,thc->hdc", query_h, scaled_grad, preferred_element_type=jnp.float32)
    prefix_sum = prefix_2(key_value, "ctx", add_states, jnp.zeros_like(key_value), False)
    suffix_sum = prefix_2(query_cot, "ctx", add_states, jnp.zeros_like(query_cot), True)
    causal = lax.iota(jnp.int32, length)[:, None] >= lax.iota(jnp.int32, length)[None, :]
    scores = jnp.einsum("thd,shd->hts", query_h, key_h, preferred_element_type=jnp.float32)
    scores_bf = jnp.where(causal[None], scores, 0.0).astype(jnp.bfloat16)
    grad_scores = jnp.einsum(
        "thc,shc->hts", scaled_grad, value_h, preferred_element_type=jnp.float32
    )
    grad_bf = jnp.where(causal[None], grad_scores, 0.0).astype(jnp.bfloat16)
    local_out = jnp.einsum("hts,shc->thc", scores_bf, value_h, preferred_element_type=jnp.float32)
    local_query = jnp.einsum("hts,shd->thd", grad_bf, key_h, preferred_element_type=jnp.float32)
    local_key = jnp.einsum("hts,thd->shd", grad_bf, query_h, preferred_element_type=jnp.float32)
    local_value = jnp.einsum(
        "hts,thc->shc", scores_bf, scaled_grad, preferred_element_type=jnp.float32
    )
    prefix = prefix_sum.astype(jnp.bfloat16)
    suffix = suffix_sum.astype(jnp.bfloat16)
    attended = local_out + jnp.einsum(
        "thd,hdc->thc", query_h, prefix, preferred_element_type=jnp.float32
    )
    attended = (attended * scales[:, None, None]).astype(jnp.bfloat16)
    query_grad = local_query + jnp.einsum(
        "thc,hdc->thd", scaled_grad, prefix, preferred_element_type=jnp.float32
    )
    key_grad = local_key + jnp.einsum(
        "shc,hdc->shd", value_h, suffix, preferred_element_type=jnp.float32
    )
    value_grad = local_value + jnp.einsum(
        "shd,hdc->shc", key_h, suffix, preferred_element_type=jnp.float32
    )
    return (
        attended.reshape(length, H * DV),
        query_grad.astype(jnp.bfloat16).reshape(length, H * DK),
        key_grad.astype(jnp.bfloat16).reshape(length, H * DK),
        value_grad.astype(jnp.bfloat16).reshape(length, H * DV),
    )


def solution(mesh):
    in_specs = (
        P(("batch", "ctx"), None),
        P(("batch", "ctx"), None),
        P(("batch", "ctx"), None),
        P(("batch", "ctx"), None),
    )
    out_specs = (
        P(("batch", "ctx"), None),
        P(("batch", "ctx"), None),
        P(("batch", "ctx"), None),
        P(("batch", "ctx"), None),
    )
    return jax.shard_map(local, mesh=mesh, in_specs=in_specs, out_specs=out_specs, check_vma=False)
```

profile of v0, /device:TPU:0, one launch (start us, length us, event | category | flops | bytes accessed | tf_op | source)
XLA Modules:
  0.0 144.7 jit_solution(7119004041571771415)
XLA Ops:
  7.2 0.0 copy-start
  7.2 0.0 all-gather.7.cloned.1.call-start
  7.2 1.6 %copy.42 = bf16[512,1024]{0,1:T(8,128)(2,1)S(1)} copy(bf16[512,1024]{1,0:T(8,128)(2,1)} %param.8) | data formatting | bytes 2097152 | tf_op args[0]
  8.9 0.0 copy-start.3
  8.9 4.5 %copy.46 = f32[512,2048]{0,1:T(8,128)} copy(bf16[512,2048]{1,0:T(8,128)(2,1)} %param.11) | data formatting | bytes 6291456 | tf_op jit(solution)/shard_map/convert_element_type | solution.py:38
  13.4 2.8 %multiply_convert_fusion = bf16[512,16,128]{0,2,1:T(8,128)(2,1)S(1)} fusion(f32[512,16,128]{0,2,1:T(8,128)} %bitcast.89, f32[512]{0:T(512)S(1)} %multiply_rsqrt_fusion), kind=kLoop, calls=%fused_computation.8 | loop fusion | flops 2097152 | bytes 6293504 | tf_op jit(solution)/shard_map/convert_element_type | solution.py:38
  16.2 0.0 copy-start.2
  16.2 1.3 copy-done.2
  17.5 1.6 %convolution_bitcast_fusion = f32[16,64,128]{2,1,0:T(8,128)} fusion(bf16[512,16,128]{0,2,1:T(8,128)(2,1)S(1)} %multiply_convert_fusion, bf16[512,16,64]{0,2,1:T(8,128)(2,1)S(1)} %bitcast.81), kind=kOutput, calls=%fused_computation.24 | convolution fusion | flops 134217728 | bytes 3670016 | tf_op jit(solution)/shard_map/thd,thc->hdc/dot_general | solution.py:40
  19.2 0.0 all-gather.7.cloned.1.call-update
  19.2 0.0 all-gather.5.cloned.1.call-start
  19.2 2.3 %copy.43 = bf16[512,1024]{0,1:T(8,128)(2,1)} copy(bf16[512,1024]{1,0:T(8,128)(2,1)} %param.9) | data formatting | bytes 2097152 | tf_op args[1]
  21.5 0.0 copy-done
  21.5 2.5 %fusion.7 = f32[16,64,128]{2,1,0:T(8,128)} fusion(bf16[512,16,64]{0,2,1:T(8,128)(2,1)} %bitcast.85, bf16[512,2048]{1,0:T(8,128)(2,1)S(1)} %copy-done), kind=kOutput, calls=%fused_computation.14 | convolution fusion | flops 134217728 | bytes 3670016 | tf_op jit(solution)/shard_map/thd,thc->hdc/dot_general | solution.py:39
  24.0 0.0 all-gather.5.cloned.1.call-update
  24.1 0.1 iota_compare_fusion
  24.2 0.0 copy-done.3
  24.2 6.9 %select_convert_fusion.1 = bf16[16,512,512]{2,1,0:T(8,128)(2,1)} fusion(bf16[512,16,64]{0,2,1:T(8,128)(2,1)S(1)} %bitcast.82, bf16[512,16,64]{0,2,1:T(8,128)(2,1)} %bitcast.86, pred[512,512]{1,0:T(8,128)(4,1)S(1)} %iota_compare_fusion), kind=kOutput, calls=%fused_computation.3 | convolution fusion | flops 545259520 | bytes 10747904 | tf_op jit(solution)/shard_map/thd,shd->hts/dot_general | solution.py:44
  31.1 7.5 %select_convert_fusion = bf16[16,512,512]{2,1,0:T(8,128)(2,1)} fusion(bf16[512,16,128]{0,2,1:T(8,128)(2,1)} %copy-done.2, pred[512,512]{1,0:T(8,128)(4,1)S(1)} %iota_compare_fusion, bf16[512,2048]{1,0:T(8,128)(2,1)S(1)} %copy-done), kind=kOutput, calls=%fused_computation.2 | convolution fusion | flops 1082130432 | bytes 12845056 | tf_op jit(solution)/shard_map/thc,shc->hts/dot_general | solution.py:46
  38.6 4.8 %fusion.2 = f32[16,512,128]{1,2,0:T(8,128)} fusion(bf16[16,512,512]{2,1,0:T(8,128)(2,1)S(1)} %copy-done.1, bf16[512,2048]{1,0:T(8,128)(2,1)S(1)} %copy-done), kind=kOutput, calls=%fused_computation.9 | convolution fusion | flops 1073741824 | bytes 14680064 | tf_op jit(solution)/shard_map/hts,shc->thc/dot_general | solution.py:50
  43.4 14.0 %all-gather.7.cloned.1.call-done = f32[64,64,128]{2,1,0:T(8,128)} async-done(((f32[16,64,128]{2,1,0:T(8,128)}), f32[64,64,128]{2,1,0:T(8,128)}) %all-gather.7.cloned.1.call-update) | async-done | bytes 2097168 | tf_op jit(solution)/shard_map/all_gather | solution.py:13
  57.4 5.0 %while.31 = (s32[]{:T(128)}, f32[16,64,128]{2,1,0:T(8,128)S(1)}, s32[]{:T(128)}, f32[4,16,64,128]{3,2,1,0:T(8,128)}, s32[]{:T(128)}, /*index=5*/s32[]{:T(128)}, s32[]{:T(128)}, s32[]{:T(128)}) while((s32[]{:T(128)}, f32[16,64,128]{2,1,0:T(8,128)S(1)}, s32[]{:T(128)}, f32[4,16,64,128]{3,2,1,0:T(8,128)}, s32[]{:T(128)}, ...), condition=%wide.region_3.4_spmd.clone, body=%wide.region_2.3_spmd.clone.sunk | while | flops 393224 | bytes 1573027 | solution.py:22
  57.4 1.2 add_select_fusion.5
  58.6 1.2 add_select_fusion.5
  59.9 1.2 add_select_fusion.5
  61.1 1.2 add_select_fusion.5
  62.4 0.0 copy-start.7
  62.4 2.2 %fusion.4 = f32[16,64,512]{2,1,0:T(8,128)} fusion(f32[16,64,128]{2,1,0:T(8,128)S(1)} %get-tuple-element.194, bf16[512,2048]{1,0:T(8,128)(2,1)S(1)} %copy-done), kind=kOutput, calls=%fused_computation.11 | convolution fusion | flops 134348800 | bytes 4718592 | tf_op jit(solution)/shard_map/shc,hdc->shd/dot_general | solution.py:65
  64.6 2.7 %fusion.15 = f32[16,128,512]{2,1,0:T(8,128)} fusion(bf16[512,16,64]{0,2,1:T(8,128)(2,1)S(1)} %bitcast.87, f32[16,64,128]{2,1,0:T(8,128)S(1)} %get-tuple-element.194), kind=kOutput, calls=%fused_computation.26 | convolution fusion | flops 134348800 | bytes 5767168 | tf_op jit(solution)/shard_map/shd,hdc->shc/dot_general | solution.py:68
  67.3 27.8 %all-gather.5.cloned.1.call-done = f32[64,64,128]{2,1,0:T(8,128)} async-done(((f32[16,64,128]{2,1,0:T(8,128)}), f32[64,64,128]{2,1,0:T(8,128)}) %all-gather.5.cloned.1.call-update) | async-done | bytes 2097168 | tf_op jit(solution)/shard_map/all_gather | solution.py:13
  95.1 5.2 %while.30 = (s32[]{:T(128)}, f32[16,64,128]{2,1,0:T(8,128)S(1)}, s32[]{:T(128)}, f32[4,16,64,128]{3,2,1,0:T(8,128)}, s32[]{:T(128)}, /*index=5*/s32[]{:T(128)}) while((s32[]{:T(128)}, f32[16,64,128]{2,1,0:T(8,128)S(1)}, s32[]{:T(128)}, f32[4,16,64,128]{3,2,1,0:T(8,128)}, s32[]{:T(128)}, /*index=5*/s32[]{:T(128)}) %tuple.84), condition=%wide.region_1.2_spmd.clone, body=%wide.region_0.1_spmd.clone.sunk | while | flops 393220 | bytes 1572965 | solution.py:22
  95.1 1.2 add_select_fusion.4
  96.4 1.2 add_select_fusion.4
  97.6 1.2 add_select_fusion.4
  98.9 1.2 add_select_fusion.4
  100.3 0.0 copy-start.5
  100.3 0.0 slice-start
  100.3 3.5 %fusion.18 = f32[16,64,512]{2,1,0:T(8,128)} fusion(bf16[512,16,128]{0,2,1:T(8,128)(2,1)} %copy-done.2, f32[16,64,128]{2,1,0:T(8,128)S(1)} %get-tuple-element.193), kind=kOutput, calls=%fused_computation.29 | convolution fusion | flops 134348800 | bytes 4718592 | tf_op jit(solution)/shard_map/thc,hdc->thd/dot_general | solution.py:62
  103.8 0.0 copy-done.5
  103.8 6.4 %fusion.9 = bf16[512,16,64]{0,2,1:T(8,128)(2,1)} fusion(f32[16,64,512]{2,1,0:T(8,128)S(1)} %copy-done.5, bf16[512,16,64]{0,2,1:T(8,128)(2,1)} %bitcast.83, bf16[16,512,512]{2,1,0:T(8,128)(2,1)} %select_convert_fusion), kind=kOutput, calls=%fused_computation.17 | convolution fusion | flops 537919488 | bytes 12582912 | tf_op jit(solution)/shard_map/hts,thd->shd/dot_general | solution.py:52
  110.2 0.0 slice-done.1
  110.2 5.2 %fusion.10 = bf16[512,16,64]{0,2,1:T(8,128)(2,1)} fusion(f32[16,64,512]{2,1,0:T(8,128)} %fusion.18, bf16[16,512,512]{2,1,0:T(8,128)(2,1)S(1)} %bitcast.80, bf16[512,16,64]{0,2,1:T(8,128)(2,1)S(1)} %bitcast.88), kind=kOutput, calls=%fused_computation.19 | convolution fusion | flops 537919488 | bytes 12582912 | tf_op jit(solution)/shard_map/hts,shd->thd/dot_general | solution.py:51
  115.4 2.3 %copy.53 = bf16[512,1024]{1,0:T(8,128)(2,1)} copy(bf16[512,1024]{0,1:T(8,128)(2,1)} %bitcast.93) | data formatting | bytes 2097152
  117.7 2.3 %copy.54 = bf16[512,1024]{1,0:T(8,128)(2,1)} copy(bf16[512,1024]{0,1:T(8,128)(2,1)} %bitcast.90) | data formatting | bytes 2097152
  119.9 8.0 %add_convert_fusion = bf16[16,128,512]{2,1,0:T(8,128)(2,1)} fusion(f32[16,128,512]{2,1,0:T(8,128)} %fusion.15, bf16[512,16,128]{0,2,1:T(8,128)(2,1)} %copy-done.2, bf16[16,512,512]{2,1,0:T(8,128)(2,1)} %select_convert_fusion.1), kind=kOutput, calls=%fused_computation.7 | convolution fusion | flops 1075838976 | bytes 16777216 | tf_op jit(solution)/shard_map/hts,thc->shc/dot_general | solution.py:53
  127.9 2.1 %fusion.1 = bf16[512,16,128]{0,2,1:T(8,128)(2,1)} fusion(f32[16,512,128]{1,2,0:T(8,128)S(1)} %copy-done.6, bf16[512,16,64]{0,2,1:T(8,128)(2,1)S(1)} %bitcast.84, f32[512]{0:T(512)S(1)} %multiply_rsqrt_fusion, f32[16,64,128]{2,1,0:T(8,128)S(1)} %get-tuple-element.193), kind=kOutput, calls=%fused_computation.6 | convolution fusion | flops 137494528 | bytes 7866368 | tf_op jit(solution)/shard_map/thd,hdc->thc/dot_general | solution.py:58
  130.0 3.9 %copy.52 = bf16[512,2048]{1,0:T(8,128)(2,1)} copy(bf16[512,2048]{0,1:T(8,128)(2,1)} %bitcast.91) | data formatting | bytes 4194304
  133.9 3.9 %copy.55 = bf16[512,2048]{1,0:T(8,128)(2,1)} copy(bf16[512,2048]{0,1:T(8,128)(2,1)} %bitcast.92) | data formatting | bytes 4194304
  (15 shorter events, 0.0 us)
Async XLA Ops:
  7.2 14.4 %copy-start = (bf16[512,2048]{1,0:T(8,128)(2,1)S(1)}, bf16[512,2048]{1,0:T(8,128)(2,1)}, u32[]{:S(2)}) copy-start(bf16[512,2048]{1,0:T(8,128)(2,1)} %param.10) | copy-start | bytes 6291460
  7.2 50.2 %all-gather.7.cloned.1.call-start = ((), (), s32[]{:S(2)}) async-start(), calls=%async_computation.1 | async-start | bytes 2621440 | tf_op jit(solution)/shard_map/all_gather | solution.py:13
  8.9 15.3 %copy-start.3 = (bf16[512,1024]{0,1:T(8,128)(2,1)}, bf16[512,1024]{0,1:T(8,128)(2,1)S(1)}, u32[]{:S(2)}) copy-start(bf16[512,1024]{0,1:T(8,128)(2,1)S(1)} %copy.42) | copy-start | bytes 3145732
  16.2 1.3 copy-start.2
  19.2 75.9 %all-gather.5.cloned.1.call-start = ((), (), s32[]{:S(2)}) async-start(), calls=%async_computation | async-start | bytes 2621440 | tf_op jit(solution)/shard_map/all_gather | solution.py:13
  31.1 7.5 %copy-start.1 = (bf16[16,512,512]{2,1,0:T(8,128)(2,1)S(1)}, bf16[16,512,512]{2,1,0:T(8,128)(2,1)}, u32[]{:S(2)}) copy-start(bf16[16,512,512]{2,1,0:T(8,128)(2,1)} %select_convert_fusion.1) | copy-start | bytes 25165828
  62.4 2.2 %copy-start.7 = (bf16[512,1024]{0,1:T(8,128)(2,1)S(1)}, bf16[512,1024]{0,1:T(8,128)(2,1)}, u32[]{:S(2)}) copy-start(bf16[512,1024]{0,1:T(8,128)(2,1)} %copy.43) | copy-start | bytes 3145732
  100.3 3.5 %copy-start.5 = (f32[16,64,512]{2,1,0:T(8,128)S(1)}, f32[16,64,512]{2,1,0:T(8,128)}, u32[]{:S(2)}) copy-start(f32[16,64,512]{2,1,0:T(8,128)} %fusion.4) | copy-start | bytes 6291460
  100.3 9.9 %slice-start = ((s8[8388608]{0:T(1024)(128)(4,1)}), s8[4194304]{0:T(1024)(128)(4,1)S(1)}, s32[]{:S(2)}) async-start(s8[8388608]{0:T(1024)(128)(4,1)} %bitcast.79), calls=%async_computation.2 | async-start | bytes 8388608
  103.8 6.4 %slice-start.1 = ((s8[8388608]{0:T(1024)(128)(4,1)}), s8[4194304]{0:T(1024)(128)(4,1)S(1)}, s32[]{:S(2)}) async-start(s8[8388608]{0:T(1024)(128)(4,1)} %bitcast.79), calls=%async_computation.3 | async-start | bytes 8388608
  103.8 6.4 %copy-start.8 = (bf16[512,1024]{0,1:T(8,128)(2,1)S(1)}, bf16[512,1024]{0,1:T(8,128)(2,1)}, u32[]{:S(2)}) copy-start(bf16[512,1024]{0,1:T(8,128)(2,1)} %copy.43) | copy-start | bytes 3145732
  119.9 8.0 %copy-start.4 = (bf16[512,1024]{0,1:T(8,128)(2,1)S(1)}, bf16[512,1024]{0,1:T(8,128)(2,1)}, u32[]{:S(2)}) copy-start(bf16[512,1024]{0,1:T(8,128)(2,1)} %copy-done.3) | copy-start | bytes 3145732
  119.9 8.0 %copy-start.6 = (f32[16,512,128]{1,2,0:T(8,128)S(1)}, f32[16,512,128]{1,2,0:T(8,128)}, u32[]{:S(2)}) copy-start(f32[16,512,128]{1,2,0:T(8,128)} %fusion.2) | copy-start | bytes 12582916
Sparse Core Ops, SparseCore 0:
  19.3 38.0 all-gather.6
  59.8 35.2 all-gather.4
where the time goes:
time: 146 us; the launch traced here: 145 us
  matrix products  53.4 us (37%)
  waiting for transfers between devices  41.8 us (29%)
  local copies, waits for them, and re-layouts  22.1 us (15%)
  between operations  14.2 us (10%)
  other arithmetic  12.7 us (9%)
    all_gather x2, waiting for transfers between devices, prefix_2(): everything = lax.all_gather(array, axis)  41.8 us
    unnamed x28, local copies, waits for them, and re-layouts  17.6 us
    select_n x8, other arithmetic, turn(): return jnp.where(reached, new, before)  9.83 us
    dot_general x1, matrix products, local(): jnp.einsum('hts,thc->shc', scores_bf, scaled_grad, preferred_element_type...  7.97 us
    dot_general x1, matrix products, local(): jnp.einsum('thc,shc->hts', scaled_grad, value_h, preferred_element_type=j...  7.48 us
    dot_general x1, matrix products, local(): jnp.einsum('thd,shd->hts', query_h, key_h, preferred_element_type=jnp.flo...  6.92 us
    dot_general x1, matrix products, local(): jnp.einsum('hts,thd->shd', grad_bf, query_h, preferred_element_type=jnp.f...  6.37 us
    dot_general x1, matrix products, local(): jnp.einsum('hts,shd->thd', grad_bf, key_h, preferred_element_type=jnp.flo...  5.2 us
  transfers between devices with their start and end apart: 2, of which 2 were waited for; matrix products, arithmetic and copies ran while one was open for 23% of the time, Pallas kernels for 0%

commit v1 on v0

v1 whole, which is shorter than its diff:
```python
import functools

import jax
import jax.numpy as jnp
from jax import lax
from jax.experimental import pallas as pl
from jax.experimental.pallas import tpu as pltpu
from jax.sharding import PartitionSpec as P

H = 16
DK = 64
DV = 128
PAIRS = H // 2
HALF = PAIRS // 2
XW = 2 * DK
YW = 2 * DV
CHUNKS = 2
VMEM_LIMIT = 12 * 1024 * 1024

NT = (((1,), (1,)), ((), ()))
TN = (((0,), (0,)), ((), ()))
NN = (((1,), (0,)), ((), ()))


def dot(a, b, dims=NN):
    return lax.dot_general(a, b, dims, preferred_element_type=jnp.float32)


def is_low():
    size = lax.axis_size("ctx")
    if size != 4:
        return lax.axis_index("ctx") >= 0
    return lax.axis_index("ctx") < size // 2


def is_inner():
    at = lax.axis_index("ctx")
    return (at == 1) | (at == 2)


def row_scales(rows, first, columns):
    at = lax.axis_index("ctx") * rows[1] + first + lax.broadcasted_iota(jnp.int32, (rows[0], columns), 0)
    return 1.0 / jnp.sqrt(DK * (at.astype(jnp.float32) + 1.0))


def diagonal(square):
    return jnp.concatenate([square[:DK, :DV], square[DK:, DV:]], axis=0)


def states_kernel(first, forward, q, k, v, do, x, y, state, chunk_state, sems):
    low = is_low()
    plain = low if forward else jnp.logical_not(low)
    length = x.shape[1]

    def copies(a, b, p):
        return (
            pltpu.make_async_copy(a.at[:, pl.ds((first + p) * XW, XW)], x.at[p], sems.at[0, p]),
            pltpu.make_async_copy(b.at[:, pl.ds((first + p) * YW, YW)], y.at[p], sems.at[1, p]),
        )

    def run(a, b, scaled):
        for p in range(HALF):
            for c in copies(a, b, p):
                c.start()
        if scaled:
            scales = row_scales((length, length), 0, YW)
        for p in range(HALF):
            for c in copies(a, b, p):
                c.wait()
            if scaled:
                y[p] = (y[p].astype(jnp.float32) * scales).astype(jnp.bfloat16)
            size = length // CHUNKS
            parts = [
                diagonal(dot(x[p, c * size : (c + 1) * size, :], y[p, c * size : (c + 1) * size, :], TN))
                for c in range(CHUNKS)
            ]
            state[p] = parts[0] + parts[1]
            chunk_state[p] = parts[1] if scaled else parts[0]

    @pl.when(plain)
    def _():
        run(k, v, False)

    @pl.when(jnp.logical_not(plain))
    def _():
        run(q, do, True)


def states(first, forward, q, k, v, do):
    length = q.shape[0]
    any_spec = pl.BlockSpec(memory_space=pltpu.HBM)
    vmem = pl.BlockSpec(memory_space=pltpu.VMEM)
    return pl.pallas_call(
        functools.partial(states_kernel, first, forward),
        in_specs=[any_spec] * 4,
        out_specs=[vmem, vmem, vmem, vmem],
        out_shape=[
            pltpu.VMEM((HALF, length, XW), jnp.bfloat16),
            pltpu.VMEM((HALF, length, YW), jnp.bfloat16),
            jax.ShapeDtypeStruct((HALF, XW, DV), jnp.float32),
            pltpu.VMEM((HALF, XW, DV), jnp.float32),
        ],
        scratch_shapes=[pltpu.SemaphoreType.DMA((2, HALF))],
        compiler_params=pltpu.CompilerParams(vmem_limit_bytes=VMEM_LIMIT),
        cost_estimate=pl.CostEstimate(flops=2 * HALF * length * XW * YW, bytes_accessed=HALF * length * (XW + YW) * 4, transcendentals=0),
        name="states",
    )(q, k, v, do)


def head_lanes(array):
    lane = lax.broadcasted_iota(jnp.int32, array.shape, 1)
    zero = jnp.zeros_like(array)
    return jnp.where(lane < DK, array, zero), jnp.where(lane >= DK, array, zero)


def block_diagonal(state):
    row = lax.broadcasted_iota(jnp.int32, state.shape, 0)
    zero = jnp.zeros_like(state)
    both = jnp.concatenate([jnp.where(row < DK, state, zero), jnp.where(row >= DK, state, zero)], axis=1)
    return both.astype(jnp.bfloat16)


def send_out(staged, first, p, width, sem, when_low, when_high, low):
    columns = pl.ds(pl.multiple_of((first + p) * width, width), width)
    to_low = pltpu.make_async_copy(staged.at[p], when_low.at[:, columns], sem.at[p])
    to_high = pltpu.make_async_copy(staged.at[p], when_high.at[:, columns], sem.at[p])

    @pl.when(low)
    def _():
        to_low.start()

    @pl.when(jnp.logical_not(low))
    def _():
        to_high.start()


def wait_out(staged, first, p, width, sem, when_low):
    columns = pl.ds(pl.multiple_of((first + p) * width, width), width)
    pltpu.make_async_copy(staged.at[p], when_low.at[:, columns], sem.at[p]).wait()


def local_kernel(first, *refs):
    xf, yf, xg, yg, fsel, near = refs[:6]
    att, qg, kg, vg, o2, o4, o1_out, o3_out, sem1, sem3 = refs[-10:]
    low = is_low()
    length = xf.shape[1]
    size = length // CHUNKS
    row = lax.broadcasted_iota(jnp.int32, (size, size), 0)
    col = lax.broadcasted_iota(jnp.int32, (size, size), 1)
    keep = jnp.where(low, row - col, col - row) >= 0
    has_near = is_inner()

    def body(p, carry):
        base = near[p]
        if lax.axis_size("ctx") == 4:
            base = jnp.where(has_near, base, 0.0)
        added = fsel[p]
        for c in range(CHUNKS):
            rows = pl.ds(c * size, size)
            takes = low if c == 1 else jnp.logical_not(low)
            bd = block_diagonal(base + jnp.where(takes, added, 0.0))
            xf_c, xg_c, yf_c, yg_c = xf[p, rows, :], xg[p, rows, :], yf[p, rows, :], yg[p, rows, :]
            xf_h, xg_h = head_lanes(xf_c), head_lanes(xg_c)
            o1 = dot(xg_c, bd)
            o3 = dot(yg_c, bd, NT)
            o4_c = None
            for h in range(2):
                lanes = slice(h * DV, (h + 1) * DV)
                m = jnp.where(keep, dot(xg_c, xf_h[h], NT), 0.0).astype(jnp.bfloat16)
                n = jnp.where(keep, dot(yg_c[:, lanes], yf_c[:, lanes], NT), 0.0).astype(jnp.bfloat16)
                o1_h = o1[:, lanes] + dot(m, yf_c[:, lanes])
                scale = jnp.where(low, row_scales((size, length), c * size, DV), 1.0)
                o1_out[p, rows, lanes] = (o1_h * scale).astype(jnp.bfloat16)
                o2[p, rows, lanes] = dot(m, yg_c[:, lanes], TN)
                o3 += dot(n, xf_h[h])
                part = dot(n, xg_h[h], TN)
                o4_c = part if o4_c is None else o4_c + part
            o3_out[p, rows, :] = o3.astype(jnp.bfloat16)
            o4[p, rows, :] = o4_c
        send_out(o1_out, first, p, YW, sem1, att, vg, low)
        send_out(o3_out, first, p, XW, sem3, qg, kg, low)
        return carry

    lax.fori_loop(0, HALF, body, 0)
    for p in range(HALF):
        wait_out(o1_out, first, p, YW, sem1, att)
        wait_out(o3_out, first, p, XW, sem3, qg)


def far_kernel(first, *refs):
    xf, yf, gsel, far1, far2, o2, o4 = refs[:7]
    att, qg, kg, vg, o2_out, o4_out, sem2, sem4 = refs[-8:]
    low = is_low()
    length = xf.shape[1]
    size = length // CHUNKS
    special = lax.axis_size("ctx") == 4
    first_half = first == 0

    def body(p, carry):
        base = far1[p]
        if special:
            if first_half:
                base += jnp.where(is_inner(), 0.0, far2[p])
            else:
                base += far2[p]
        added = gsel[p]
        for c in range(CHUNKS):
            rows = pl.ds(c * size, size)
            takes = low if c == 0 else jnp.logical_not(low)
            bd = block_diagonal(base + jnp.where(takes, added, 0.0))
            out2 = o2[p, rows, :] + dot(xf[p, rows, :], bd)
            scale = jnp.where(low, 1.0, row_scales((size, length), c * size, YW))
            o2_out[p, rows, :] = (out2 * scale).astype(jnp.bfloat16)
            out4 = o4[p, rows, :] + dot(yf[p, rows, :], bd, NT)
            o4_out[p, rows, :] = out4.astype(jnp.bfloat16)
        send_out(o2_out, first, p, YW, sem2, vg, att, low)
        send_out(o4_out, first, p, XW, sem4, kg, qg, low)
        return carry

    lax.fori_loop(0, HALF, body, 0)
    for p in range(HALF):
        wait_out(o2_out, first, p, YW, sem2, vg)
        wait_out(o4_out, first, p, XW, sem4, kg)


def in_vmem(array):
    return pltpu.with_memory_space_constraint(array, pltpu.VMEM)


ANY = pl.BlockSpec(memory_space=pltpu.HBM)
WHOLE = pl.BlockSpec(memory_space=pltpu.VMEM)


def out_shapes(length):
    wide = jax.ShapeDtypeStruct((length, H * DV), jnp.bfloat16)
    narrow = jax.ShapeDtypeStruct((length, H * DK), jnp.bfloat16)
    return [wide, narrow, narrow, wide]


def local_terms(first, f, g, near, outs):
    xf, yf, _, fsel = f
    xg, yg, _, _ = g
    length = xf.shape[1]
    scratch = [
        pltpu.VMEM((HALF, length, YW), jnp.bfloat16),
        pltpu.VMEM((HALF, length, XW), jnp.bfloat16),
        pltpu.SemaphoreType.DMA((HALF,)),
        pltpu.SemaphoreType.DMA((HALF,)),
    ]
    ins = [in_vmem(xf), in_vmem(yf), in_vmem(xg), in_vmem(yg), in_vmem(fsel), near]
    return pl.pallas_call(
        functools.partial(local_kernel, first),
        in_specs=[WHOLE] * 6 + [ANY] * len(outs),
        out_specs=[ANY] * 4 + [WHOLE] * 2,
        out_shape=out_shapes(length)
        + [pltpu.VMEM((HALF, length, YW), jnp.float32), pltpu.VMEM((HALF, length, XW), jnp.float32)],
        input_output_aliases={6 + i: i for i in range(len(outs))},
        scratch_shapes=scratch,
        compiler_params=pltpu.CompilerParams(vmem_limit_bytes=VMEM_LIMIT),
        cost_estimate=pl.CostEstimate(flops=HALF * 2 * 12 * 2 * 256**3 // 2, bytes_accessed=4 * 1024 * 1024, transcendentals=0),
        name="local",
    )(*ins, *outs)


def far_terms(first, f, g, far1, far2, o2, o4, outs):
    xf, yf, _, _ = f
    gsel = g[3]
    length = xf.shape[1]
    scratch = [
        pltpu.VMEM((HALF, length, YW), jnp.bfloat16),
        pltpu.VMEM((HALF, length, XW), jnp.bfloat16),
        pltpu.SemaphoreType.DMA((HALF,)),
        pltpu.SemaphoreType.DMA((HALF,)),
    ]
    ins = [in_vmem(xf), in_vmem(yf), in_vmem(gsel), far1, far2, in_vmem(o2), in_vmem(o4)]
    return pl.pallas_call(
        functools.partial(far_kernel, first),
        in_specs=[WHOLE] * 7 + [ANY] * 4,
        out_specs=[ANY] * 4,
        out_shape=out_shapes(length),
        input_output_aliases={7 + i: i for i in range(4)},
        scratch_shapes=scratch,
        compiler_params=pltpu.CompilerParams(vmem_limit_bytes=VMEM_LIMIT),
        cost_estimate=pl.CostEstimate(flops=HALF * 4 * 2 * 256**3 // 2, bytes_accessed=2 * 1024 * 1024, transcendentals=0),
        name="far",
    )(*ins, *outs)


def scan_sum(state, size, reverse):
    step, total = 1, state
    sign = -1 if reverse else 1
    before = lax.ppermute(state, "ctx", [(i, i + sign) for i in range(size) if 0 <= i + sign < size])
    total = before
    while step < size:
        moved = [(i, i + sign * step) for i in range(size) if 0 <= i + sign * step < size]
        total = total + lax.ppermute(total, "ctx", moved)
        step *= 2
    return total


def local(queries, keys, values, out_grad):
    args = [pltpu.with_memory_space_constraint(a, pltpu.HBM) for a in (queries, keys, values, out_grad)]
    size = lax.axis_size("ctx")
    fa = states(0, True, *args)
    fb = states(HALF, True, *args)
    ga = states(0, False, *args)
    gb = states(HALF, False, *args)
    if size == 4:
        swap_x = [(0, 1), (1, 0), (2, 3), (3, 2)]
        swap_y = [(0, 2), (2, 0), (1, 3), (3, 1)]
        inner = is_inner()
        got_xa = lax.ppermute(fa[2], "ctx", swap_x)
        got_y1 = lax.ppermute(fb[2], "ctx", swap_y)
        got_xb = lax.ppermute(jnp.where(inner, ga[2], fb[2]), "ctx", swap_x)
        got_y2 = lax.ppermute(fa[2] + got_xa, "ctx", swap_y)
        got_x2 = lax.ppermute(got_y1 + jnp.where(inner, gb[2], 0.0), "ctx", swap_x)
        near_a, near_b = got_xa, got_xb
        far_a, far_b = (got_y2, got_xb), (got_y1, got_x2)
    else:
        near_a, near_b = scan_sum(fa[2], size, False), scan_sum(fb[2], size, False)
        far_a, far_b = [scan_sum(ga[2], size, True)] * 2, [scan_sum(gb[2], size, True)] * 2
    *outs, o2a, o4a = local_terms(0, fa, ga, near_a, [])
    *outs, o2b, o4b = local_terms(HALF, fb, gb, near_b, outs)
    outs = far_terms(0, fa, ga, *far_a, o2a, o4a, outs)
    outs = far_terms(HALF, fb, gb, *far_b, o2b, o4b, outs)
    return tuple(outs)


def solution(mesh):
    spec = P(("batch", "ctx"), None)
    return jax.shard_map(local, mesh=mesh, in_specs=(spec,) * 4, out_specs=(spec,) * 4, check_vma=False)
```

time: 146 us -> 42.8 us (0.29)
  matrix products: 53.4 us -> 0 us
  waiting for transfers between devices: 41.8 us -> 0.01 us
  Pallas kernels: 0 us -> 28.5 us
  local copies, waits for them, and re-layouts: 22.1 us -> 3.89 us
  between operations: 14.2 us -> 0.82 us
  other arithmetic: 12.7 us -> 2.07 us
  starting transfers between devices: 0.08 us -> 7.25 us
    dot_general x12 -> x0, matrix products: 53.4 us -> none  [the longest x1 7.97 us: local(): jnp.einsum('hts,thc->shc', scores_bf, scaled_grad, preferred_element_type...]
    all_gather x2 -> x0, waiting for transfers between devices: 41.8 us -> none  [prefix_2(): everything = lax.all_gather(array, axis)]
    pallas_call x0 -> x8, Pallas kernels: none -> 28.5 us  [the longest x2 15.1 us: local_terms(): pl.pallas_call(functools.partial(local_kernel, first), in_specs=[WHOLE] *...]
    unnamed x28 -> x22, local copies, waits for them, and re-layouts: 17.6 us -> 3.89 us
    select_n x8 -> x1, other arithmetic: 9.83 us -> 0.98 us  [local(): got_xb = lax.ppermute(jnp.where(inner, ga[2], fb[2]), 'ctx', swap_x)]
    ppermute x0 -> x5, starting transfers between devices: none -> 7.25 us  [the longest x1 3.04 us: local(): got_y1 = lax.ppermute(fb[2], 'ctx', swap_y)]
    convert_element_type x1 -> x0, local copies, waits for them, and re-layouts: 4.53 us -> none  [local(): grad_h.astype(jnp.float32)]
    convert_element_type x1 -> x0, other arithmetic: 2.78 us -> none  [local(): (scales[:, None, None] * grad_h.astype(jnp.float32)).astype(jnp.bfloat16)]
  transfers between devices with their start and end apart: 2 -> 5, of which waited for: 2 -> 0; matrix products, arithmetic and copies ran while one was open for 23% -> 5% of each run, Pallas kernels for 0% -> 56%
where the time goes in v1:
time: 42.8 us; the launch traced here: 42.5 us
  Pallas kernels  28.5 us (67%)
  starting transfers between devices  7.25 us (17%)
  local copies, waits for them, and re-layouts  3.89 us (9%)
  other arithmetic  2.07 us (5%)
  between operations  0.82 us (2%)
    pallas_call x2, Pallas kernels, local_terms(): pl.pallas_call(functools.partial(local_kernel, first), in_specs=[WHOLE] *...  15.1 us
    pallas_call x4, Pallas kernels, states(): pl.pallas_call(functools.partial(states_kernel, first, forward), in_specs...  9.48 us
    pallas_call x2, Pallas kernels, far_terms(): pl.pallas_call(functools.partial(far_kernel, first), in_specs=[WHOLE] * 7...  3.94 us
    unnamed x22, local copies, waits for them, and re-layouts  3.89 us
    ppermute x1, starting transfers between devices, local(): got_y1 = lax.ppermute(fb[2], 'ctx', swap_y)  3.04 us
    ppermute x1, starting transfers between devices, local(): got_x2 = lax.ppermute(got_y1 + jnp.where(inner, gb[2], 0.0), 'ctx', swap_x)  1.55 us
    ppermute x1, starting transfers between devices, local(): got_xa = lax.ppermute(fa[2], 'ctx', swap_x)  1.49 us
    add x1, other arithmetic, local(): got_y2 = lax.ppermute(fa[2] + got_xa, 'ctx', swap_y)  1.06 us
  transfers between devices with their start and end apart: 5, of which 0 were waited for; matrix products, arithmetic and copies ran while one was open for 5% of the time, Pallas kernels for 56%

profile of v1, /device:TPU:0, one launch (start us, length us, event | category | flops | bytes accessed | tf_op | source)
XLA Modules:
  0.0 42.5 jit_solution(99428352797936303)
XLA Ops:
  0.6 2.7 %states.4 = (bf16[4,512,128]{2,1,0:T(8,128)(2,1)S(1)}, bf16[4,512,256]{2,1,0:T(8,128)(2,1)S(1)}, f32[4,128,128]{2,1,0:T(8,128)}, f32[4,128,128]{2,1,0:T(8,128)S(1)}) custom-call(bf16[512,1024]{1,0:T(8,128)(2,1)} %q.7, bf16[512,1024]{1,0:T(8,128)(2,1)} %k.7, bf16[512,2048]{1,0:T(8,128)(2,1)} %v.7, bf16[512,2048]{1,0:T(8,128)(2,1)} %do.7), custom_call_target="tpu_custom_call" | custom-call | flops 134217728 | bytes 3145728 | tf_op jit(solution)/shard_map/states/pallas_call | solution.py:93
  3.4 0.0 copy-start
  3.4 3.0 %collective-permute-start = (f32[4,128,128]{2,1,0:T(8,128)}, f32[4,128,128]{2,1,0:T(8,128)S(1)}, u32[]{:S(2)}, u32[]{:S(2)}) collective-permute-start(f32[4,128,128]{2,1,0:T(8,128)} %get-tuple-element.39), channel_id=1, source_target_pairs={{0,2},{2,0},{1,3},{3,1},{4,6},{6,4},{5,7},{7,5},{8,10},{10,8},{9,1... | collective-permute-start | bytes 786440 | tf_op jit(solution)/shard_map/ppermute | solution.py:313
  6.4 2.7 %states.7 = (bf16[4,512,128]{2,1,0:T(8,128)(2,1)S(1)}, bf16[4,512,256]{2,1,0:T(8,128)(2,1)S(1)}, f32[4,128,128]{2,1,0:T(8,128)}, f32[4,128,128]{2,1,0:T(8,128)S(1)}) custom-call(bf16[512,1024]{1,0:T(8,128)(2,1)} %q.7, bf16[512,1024]{1,0:T(8,128)(2,1)} %k.7, bf16[512,2048]{1,0:T(8,128)(2,1)} %v.7, bf16[512,2048]{1,0:T(8,128)(2,1)} %do.7), custom_call_target="tpu_custom_call" | custom-call | flops 134217728 | bytes 3145728 | tf_op jit(solution)/shard_map/states/pallas_call | solution.py:93
  9.1 0.0 copy-done
  9.1 0.0 copy-start.9
  9.2 0.7 %copy-done.9 = f32[4,128,128]{2,1,0:T(8,128)} copy-done((f32[4,128,128]{2,1,0:T(8,128)}, f32[4,128,128]{2,1,0:T(8,128)S(1)}, u32[]{:S(2)}) %copy-start.9) | copy-done | bytes 262168
  9.9 1.5 %collective-permute-start.3 = (f32[4,128,128]{2,1,0:T(8,128)}, f32[4,128,128]{2,1,0:T(8,128)}, u32[]{:S(2)}, u32[]{:S(2)}) collective-permute-start(f32[4,128,128]{2,1,0:T(8,128)} %get-tuple-element.50), channel_id=1, source_target_pairs={{0,1},{1,0},{2,3},{3,2},{4,5},{5,4},{6,7},{7,6},{8,9},{9,8},{10,11... | collective-permute-start | bytes 786440 | tf_op jit(solution)/shard_map/ppermute | solution.py:312
  11.3 2.0 %states.6 = (bf16[4,512,128]{2,1,0:T(8,128)(2,1)S(1)}, bf16[4,512,256]{2,1,0:T(8,128)(2,1)S(1)}, f32[4,128,128]{2,1,0:T(8,128)S(1)}, f32[4,128,128]{2,1,0:T(8,128)S(1)}) custom-call(bf16[512,1024]{1,0:T(8,128)(2,1)} %q.7, bf16[512,1024]{1,0:T(8,128)(2,1)} %k.7, bf16[512,2048]{1,0:T(8,128)(2,1)} %v.7, bf16[512,2048]{1,0:T(8,128)(2,1)} %do.7), custom_call_target="tpu_custom_call" | custom-call | flops 134217728 | bytes 3145728 | tf_op jit(solution)/shard_map/states/pallas_call | solution.py:93
  13.4 0.0 copy-start.2
  13.4 0.7 %copy-done.2 = f32[4,128,128]{2,1,0:T(8,128)} copy-done((f32[4,128,128]{2,1,0:T(8,128)}, f32[4,128,128]{2,1,0:T(8,128)S(1)}, u32[]{:S(2)}) %copy-start.2) | copy-done | bytes 262168
  14.1 0.0 copy-start.4
  14.1 0.7 %copy-done.4 = f32[4,128,128]{2,1,0:T(8,128)} copy-done((f32[4,128,128]{2,1,0:T(8,128)}, f32[4,128,128]{2,1,0:T(8,128)S(1)}, u32[]{:S(2)}) %copy-start.4) | copy-done | bytes 262168
  14.8 0.0 copy-start.5
  14.8 1.0 %copy-done.5 = bf16[4,512,256]{2,1,0:T(8,128)(2,1)} copy-done((bf16[4,512,256]{2,1,0:T(8,128)(2,1)}, bf16[4,512,256]{2,1,0:T(8,128)(2,1)S(1)}, u32[]{:S(2)}) %copy-start.5) | copy-done | bytes 1048600
  15.8 0.0 copy-start.7
  15.8 0.8 %copy-done.7 = bf16[4,512,128]{2,1,0:T(8,128)(2,1)} copy-done((bf16[4,512,128]{2,1,0:T(8,128)(2,1)}, bf16[4,512,128]{2,1,0:T(8,128)(2,1)S(1)}, u32[]{:S(2)}) %copy-start.7) | copy-done | bytes 524312
  16.5 1.0 %broadcast_select_fusion = f32[4,128,128]{2,1,0:T(8,128)S(1)} fusion(f32[4,128,128]{2,1,0:T(8,128)} %copy-done.4, f32[4,128,128]{2,1,0:T(8,128)} %get-tuple-element.39, pred[]{:T(512)S(6)} %or.3), kind=kLoop, calls=%fused_computation.1 | loop fusion | flops 65536 | bytes 786433 | tf_op jit(solution)/shard_map/jit(_where)/select_n | solution.py:314
  17.5 0.0 copy-start.6
  17.5 0.0 copy-start.8
  17.6 0.0 copy-start.10
  17.6 0.6 %collective-permute-start.2 = (f32[4,128,128]{2,1,0:T(8,128)S(1)}, f32[4,128,128]{2,1,0:T(8,128)S(1)}, u32[]{:S(2)}, u32[]{:S(2)}) collective-permute-start(f32[4,128,128]{2,1,0:T(8,128)S(1)} %broadcast_select_fusion), channel_id=1, source_target_pairs={{0,1},{1,0},{2,3},{3,2},{4,5},{5,4},{6,7},{7,6},{8,9},{9,8},{10,11... | collective-permute-start | bytes 786440 | tf_op jit(solution)/shard_map/ppermute | solution.py:314
  18.2 2.0 %states.5 = (bf16[4,512,128]{2,1,0:T(8,128)(2,1)S(1)}, bf16[4,512,256]{2,1,0:T(8,128)(2,1)S(1)}, f32[4,128,128]{2,1,0:T(8,128)S(1)}, f32[4,128,128]{2,1,0:T(8,128)S(1)}) custom-call(bf16[512,1024]{1,0:T(8,128)(2,1)} %q.7, bf16[512,1024]{1,0:T(8,128)(2,1)} %k.7, bf16[512,2048]{1,0:T(8,128)(2,1)} %v.7, bf16[512,2048]{1,0:T(8,128)(2,1)} %do.7), custom_call_target="tpu_custom_call" | custom-call | flops 134217728 | bytes 3145728 | tf_op jit(solution)/shard_map/states/pallas_call | solution.py:93
  20.2 0.0 collective-permute-done.refs_3_
  20.2 1.6 %collective-permute-start.1 = (f32[4,128,128]{2,1,0:T(8,128)S(1)}, f32[4,128,128]{2,1,0:T(8,128)S(1)}, u32[]{:S(2)}, u32[]{:S(2)}) collective-permute-start(f32[4,128,128]{2,1,0:T(8,128)S(1)} %select_add_fusion), channel_id=1, source_target_pairs={{0,1},{1,0},{2,3},{3,2},{4,5},{5,4},{6,7},{7,6},{8,9},{9,8},{10,11... | collective-permute-start | bytes 786440 | tf_op jit(solution)/shard_map/ppermute | solution.py:316
  21.8 0.0 collective-permute-done.3.refs_5_
  21.8 1.1 %add.7 = f32[4,128,128]{2,1,0:T(8,128)S(1)} add(f32[4,128,128]{2,1,0:T(8,128)} %get-tuple-element.50, f32[4,128,128]{2,1,0:T(8,128)} %collective-permute-done.3.refs_5_) | non-fusion elementwise | flops 65536 | bytes 786432 | tf_op jit(solution)/shard_map/add | solution.py:315
  22.9 0.6 %collective-permute-start.4 = (f32[4,128,128]{2,1,0:T(8,128)S(1)}, f32[4,128,128]{2,1,0:T(8,128)S(1)}, u32[]{:S(2)}, u32[]{:S(2)}) collective-permute-start(f32[4,128,128]{2,1,0:T(8,128)S(1)} %add.7), channel_id=1, source_target_pairs={{0,2},{2,0},{1,3},{3,1},{4,6},{6,4},{5,7},{7,5},{8,10},{10,8},{9,1... | collective-permute-start | bytes 786440 | tf_op jit(solution)/shard_map/ppermute | solution.py:315
  23.4 0.0 copy-done.6
  23.4 0.0 copy-done.8
  23.4 0.0 copy-done.10
  23.4 0.0 copy-start.1
  23.4 8.0 %local.2 = (bf16[512,2048]{1,0:T(8,128)(2,1)}, bf16[512,1024]{1,0:T(8,128)(2,1)}, bf16[512,1024]{1,0:T(8,128)(2,1)}, bf16[512,2048]{1,0:T(8,128)(2,1)}, f32[4,51...) custom-call(bf16[4,512,128]{2,1,0:T(8,128)(2,1)S(1)} %get-tuple-element.45.refs_0_, ...), custom_call_target="tpu_custom_call" | custom-call | flops 1610612736 | bytes 4194304 | tf_op jit(solution)/shard_map/local/pallas_call | solution.py:251
  31.4 0.0 collective-permute-done.2.refs_5_.refs_4_
  31.4 0.0 copy-done.1
  31.5 0.0 copy-start.3
  31.5 7.1 %local.3 = (bf16[512,2048]{1,0:T(8,128)(2,1)}, bf16[512,1024]{1,0:T(8,128)(2,1)}, bf16[512,1024]{1,0:T(8,128)(2,1)}, bf16[512,2048]{1,0:T(8,128)(2,1)}, f32[4,51...) custom-call(bf16[4,512,128]{2,1,0:T(8,128)(2,1)S(1)} %get-tuple-elem, ...), custom_call_target="tpu_custom_call", output_to_operand_aliasing={{0}: (6, {}), {1}: (7, {}), {2}: (8, {}), {3}: (9, {})} | custom-call | flops 1610612736 | bytes 4194304 | tf_op jit(solution)/shard_map/local/pallas_call | solution.py:251
  38.5 0.0 collective-permute-done.4.refs_3_
  38.5 0.0 copy-done.3
  38.6 2.0 %far.2 = (bf16[512,2048]{1,0:T(8,128)(2,1)}, bf16[512,1024]{1,0:T(8,128)(2,1)}, bf16[512,1024]{1,0:T(8,128)(2,1)}, bf16[512,2048]{1,0:T(8,128)(2,1)}) custom-call(bf16[4,512,128]{2,1,0:T(8,128)(2,1)S(1)} %get-tuple-element.45.refs_0_, ...), custom_call_target="tpu_custom_call", output_to_operand_aliasing={{0}: (7, {}), {1}: (8, {}), {2}: (9, {}), {3}: (10, {})} | custom-call | flops 268435456 | bytes 2097152 | tf_op jit(solution)/shard_map/far/pallas_call | solution.py:276
  40.5 0.0 collective-permute-done.1.refs_4_
  40.5 2.0 %far.3 = (bf16[512,2048]{1,0:T(8,128)(2,1)}, bf16[512,1024]{1,0:T(8,128)(2,1)}, bf16[512,1024]{1,0:T(8,128)(2,1)}, bf16[512,2048]{1,0:T(8,128)(2,1)}) custom-call(bf16[4,512,128]{2,1,0:T(8,128)(2,1)S(1)} %get-tuple-element.36.refs_0_, ...), custom_call_target="tpu_custom_call", output_to_operand_aliasing={{0}: (7, {}), {1}: (8, {}), {2}: (9, {}), {3}: (10, {})} | custom-call | flops 268435456 | bytes 2097152 | tf_op jit(solution)/shard_map/far/pallas_call | solution.py:276
  (1 shorter events, 0.0 us)
Async XLA Ops:
  3.4 5.8 %copy-start = (f32[4,128,128]{2,1,0:T(8,128)}, f32[4,128,128]{2,1,0:T(8,128)S(1)}, u32[]{:S(2)}) copy-start(f32[4,128,128]{2,1,0:T(8,128)S(1)} %get-tuple-element.43.refs_4_) | copy-start | bytes 786436
  3.4 16.8 %collective-permute-start = (f32[4,128,128]{2,1,0:T(8,128)}, f32[4,128,128]{2,1,0:T(8,128)S(1)}, u32[]{:S(2)}, u32[]{:S(2)}) collective-permute-start(f32[4,128,128]{2,1,0:T(8,128)} %get-tuple-element.39), channel_id=1, source_target_pairs={{0,2},{2,0},{1,3},{3,1},{4,6},{6,4},{5,7},{7,5},{8,10},{10,8},{9,1... | collective-permute-start | bytes 786440 | tf_op jit(solution)/shard_map/ppermute | solution.py:313
  9.1 0.7 %copy-start.9 = (f32[4,128,128]{2,1,0:T(8,128)}, f32[4,128,128]{2,1,0:T(8,128)S(1)}, u32[]{:S(2)}) copy-start(f32[4,128,128]{2,1,0:T(8,128)S(1)} %get-tuple-element.49.refs_4_) | copy-start | bytes 786436
  9.9 11.9 %collective-permute-start.3 = (f32[4,128,128]{2,1,0:T(8,128)}, f32[4,128,128]{2,1,0:T(8,128)}, u32[]{:S(2)}, u32[]{:S(2)}) collective-permute-start(f32[4,128,128]{2,1,0:T(8,128)} %get-tuple-element.50), channel_id=1, source_target_pairs={{0,1},{1,0},{2,3},{3,2},{4,5},{5,4},{6,7},{7,6},{8,9},{9,8},{10,11... | collective-permute-start | bytes 786440 | tf_op jit(solution)/shard_map/ppermute | solution.py:312
  13.4 0.7 %copy-start.2 = (f32[4,128,128]{2,1,0:T(8,128)}, f32[4,128,128]{2,1,0:T(8,128)S(1)}, u32[]{:S(2)}) copy-start(f32[4,128,128]{2,1,0:T(8,128)S(1)} %get-tuple-element.57.refs_2_) | copy-start | bytes 786436
  14.1 0.7 %copy-start.4 = (f32[4,128,128]{2,1,0:T(8,128)}, f32[4,128,128]{2,1,0:T(8,128)S(1)}, u32[]{:S(2)}) copy-start(f32[4,128,128]{2,1,0:T(8,128)S(1)} %get-tuple-element.44) | copy-start | bytes 786436
  14.8 1.0 %copy-start.5 = (bf16[4,512,256]{2,1,0:T(8,128)(2,1)}, bf16[4,512,256]{2,1,0:T(8,128)(2,1)S(1)}, u32[]{:S(2)}) copy-start(bf16[4,512,256]{2,1,0:T(8,128)(2,1)S(1)} %get-tuple-element.48.refs_3_) | copy-start | bytes 3145732
  15.8 0.8 %copy-start.7 = (bf16[4,512,128]{2,1,0:T(8,128)(2,1)}, bf16[4,512,128]{2,1,0:T(8,128)(2,1)S(1)}, u32[]{:S(2)}) copy-start(bf16[4,512,128]{2,1,0:T(8,128)(2,1)S(1)} %get-tuple-element.47.refs_2_) | copy-start | bytes 1572868
  17.5 5.9 %copy-start.6 = (bf16[4,512,256]{2,1,0:T(8,128)(2,1)S(1)}, bf16[4,512,256]{2,1,0:T(8,128)(2,1)}, u32[]{:S(2)}) copy-start(bf16[4,512,256]{2,1,0:T(8,128)(2,1)} %copy-done.5) | copy-start | bytes 3145732
  17.5 5.9 %copy-start.8 = (bf16[4,512,128]{2,1,0:T(8,128)(2,1)S(1)}, bf16[4,512,128]{2,1,0:T(8,128)(2,1)}, u32[]{:S(2)}) copy-start(bf16[4,512,128]{2,1,0:T(8,128)(2,1)} %copy-done.7) | copy-start | bytes 1572868
  17.6 5.9 %copy-start.10 = (f32[4,128,128]{2,1,0:T(8,128)S(1)}, f32[4,128,128]{2,1,0:T(8,128)}, u32[]{:S(2)}) copy-start(f32[4,128,128]{2,1,0:T(8,128)} %copy-done.9) | copy-start | bytes 786436
  17.6 13.9 %collective-permute-start.2 = (f32[4,128,128]{2,1,0:T(8,128)S(1)}, f32[4,128,128]{2,1,0:T(8,128)S(1)}, u32[]{:S(2)}, u32[]{:S(2)}) collective-permute-start(f32[4,128,128]{2,1,0:T(8,128)S(1)} %broadcast_select_fusion), channel_id=1, source_target_pairs={{0,1},{1,0},{2,3},{3,2},{4,5},{5,4},{6,7},{7,6},{8,9},{9,8},{10,11... | collective-permute-start | bytes 786440 | tf_op jit(solution)/shard_map/ppermute | solution.py:314
  20.2 20.3 %collective-permute-start.1 = (f32[4,128,128]{2,1,0:T(8,128)S(1)}, f32[4,128,128]{2,1,0:T(8,128)S(1)}, u32[]{:S(2)}, u32[]{:S(2)}) collective-permute-start(f32[4,128,128]{2,1,0:T(8,128)S(1)} %select_add_fusion), channel_id=1, source_target_pairs={{0,1},{1,0},{2,3},{3,2},{4,5},{5,4},{6,7},{7,6},{8,9},{9,8},{10,11... | collective-permute-start | bytes 786440 | tf_op jit(solution)/shard_map/ppermute | solution.py:316
  22.9 15.7 %collective-permute-start.4 = (f32[4,128,128]{2,1,0:T(8,128)S(1)}, f32[4,128,128]{2,1,0:T(8,128)S(1)}, u32[]{:S(2)}, u32[]{:S(2)}) collective-permute-start(f32[4,128,128]{2,1,0:T(8,128)S(1)} %add.7), channel_id=1, source_target_pairs={{0,2},{2,0},{1,3},{3,1},{4,6},{6,4},{5,7},{7,5},{8,10},{10,8},{9,1... | collective-permute-start | bytes 786440 | tf_op jit(solution)/shard_map/ppermute | solution.py:315
  23.4 8.0 %copy-start.1 = (f32[4,128,128]{2,1,0:T(8,128)S(1)}, f32[4,128,128]{2,1,0:T(8,128)}, u32[]{:S(2)}) copy-start(f32[4,128,128]{2,1,0:T(8,128)} %copy-done) | copy-start | bytes 786436
  31.5 7.1 %copy-start.3 = (f32[4,128,128]{2,1,0:T(8,128)S(1)}, f32[4,128,128]{2,1,0:T(8,128)}, u32[]{:S(2)}) copy-start(f32[4,128,128]{2,1,0:T(8,128)} %copy-done.2) | copy-start | bytes 786436

commit v2 on v0

v2 whole, which is shorter than its diff:
```python
import functools

import jax
import jax.numpy as jnp
from jax import lax
from jax.experimental import pallas as pl
from jax.experimental.pallas import tpu as pltpu
from jax.sharding import PartitionSpec as P


H = 16
DK = 64
DV = 128
PAIRS = H // 2
HALF = PAIRS // 2
XW = 2 * DK
YW = 2 * DV
CHUNK = 128
SPLIT = 2
VMEM_LIMIT = 12 * 1024 * 1024

NN = (((1,), (0,)), ((), ()))
NT = (((1,), (1,)), ((), ()))
TN = (((0,), (0,)), ((), ()))
F32 = jnp.float32
BF16 = jnp.bfloat16

HBM = pl.BlockSpec(memory_space=pltpu.HBM)
VMEM = pl.BlockSpec(memory_space=pltpu.VMEM)


def dot(a, b, dims=NN):
    return lax.dot_general(a, b, dims, preferred_element_type=F32)


def is_low():
    size = lax.axis_size("ctx")
    return lax.axis_index("ctx") < (size // 2 if size == 4 else size)


def is_inner():
    at = lax.axis_index("ctx")
    return (at == 1) | (at == 2) if lax.axis_size("ctx") == 4 else at >= 0


def in_vmem(array):
    return pltpu.with_memory_space_constraint(array, pltpu.VMEM)


def in_hbm(array):
    return pltpu.with_memory_space_constraint(array, pltpu.HBM)


def x_shape(length, dtype=BF16):
    return pltpu.VMEM((HALF, length, XW), dtype)


def y_shape(length, dtype=BF16):
    return pltpu.VMEM((HALF, length, YW), dtype)


STATE = pltpu.VMEM((HALF, XW, DV), F32)


def steps_shape(length):
    return pltpu.VMEM((HALF, length // CHUNK, XW, DV), F32)


def params():
    return pltpu.CompilerParams(vmem_limit_bytes=VMEM_LIMIT)


def diagonal(square):
    return jnp.concatenate([square[:DK, :DV], square[DK:, DV:]], axis=0)


def pair_states(x, y, scaled, scale, backward, steps):
    count = y.shape[0] // CHUNK
    parts = []
    for c in range(count):
        rows = slice(c * CHUNK, (c + 1) * CHUNK)
        s = scale[rows, :]
        new = (y[rows, :].astype(F32) * jnp.concatenate([s, s], axis=1)).astype(BF16)
        scaled[rows, :] = new
        parts.append(diagonal(dot(x[rows, :], new, TN)))
    before, after = [jnp.zeros_like(parts[0])], [jnp.zeros_like(parts[0])]
    for c in range(count - 1):
        before.append(before[-1] + parts[c])
        after.append(after[-1] + parts[count - 1 - c])
    for c in range(count):
        steps[c] = jnp.where(backward, after[count - 1 - c], before[c])
    return before[-1] + parts[-1]


def load_kernel(q, k, v, do, xfa, yfa, xfb, yfb, xga, yga, xgb, ygb, scale_low, scale_high, state, steps, raw, sems):
    low = is_low()
    length = q.shape[0]

    def copies(a, b, x, y, first, at):
        return [
            copy
            for p in range(HALF)
            for copy in (
                pltpu.make_async_copy(a.at[:, pl.ds((first + p) * XW, XW)], x.at[p], sems.at[at, 0, p]),
                pltpu.make_async_copy(b.at[:, pl.ds((first + p) * YW, YW)], y.at[p], sems.at[at, 1, p]),
            )
        ]

    def start(f, g):
        for a, b, x, y, first, at in (
            (*f, xfa, raw, 0, 0),
            (*f, xfb, yfb, HALF, 1),
            (*g, xga, yga, 0, 2),
            (*g, xgb, ygb, HALF, 3),
        ):
            for copy in copies(a, b, x, y, first, at):
                copy.start()

    @pl.when(low)
    def _():
        start((k, v), (q, do))

    @pl.when(jnp.logical_not(low))
    def _():
        start((q, do), (k, v))

    at = lax.axis_index("ctx") * length + lax.broadcasted_iota(jnp.int32, (length, DV), 0)
    scale = 1.0 / jnp.sqrt(DK * (at.astype(F32) + 1.0))
    scale_low[...] = jnp.where(low, scale, 1.0)
    scale_high[...] = jnp.where(low, 1.0, scale)
    first = copies(k, v, xfa, raw, 0, 0)
    for p in range(HALF):
        first[2 * p].wait()
        first[2 * p + 1].wait()
        state[p] = pair_states(xfa.at[p], raw.at[p], yfa.at[p], scale_high, jnp.logical_not(low), steps.at[p])
    for x, y, at in ((xfb, yfb, 1), (xga, yga, 2), (xgb, ygb, 3)):
        for copy in copies(k, v, x, y, 0, at):
            copy.wait()


def load(q, k, v, do):
    length = q.shape[0]
    x, y = x_shape(length), y_shape(length)
    scale = pltpu.VMEM((length, DV), F32)
    return pl.pallas_call(
        load_kernel,
        in_specs=[HBM] * 4,
        out_specs=[VMEM] * 12,
        out_shape=[x, y, x, y, x, y, x, y, scale, scale, STATE, steps_shape(length)],
        scratch_shapes=[y, pltpu.SemaphoreType.DMA((4, 2, HALF))],
        compiler_params=params(),
        name="load",
    )(q, k, v, do)


def f_kernel(x, y, scale, scaled, state, steps):
    high = jnp.logical_not(is_low())
    for p in range(HALF):
        state[p] = pair_states(x.at[p], y.at[p], scaled.at[p], scale, high, steps.at[p])


def f_states(x, y, scale):
    length = x.shape[1]
    return pl.pallas_call(
        f_kernel,
        in_specs=[VMEM] * 3,
        out_specs=[VMEM] * 3,
        out_shape=[y_shape(length), STATE, steps_shape(length)],
        compiler_params=params(),
        name="f_states",
    )(in_vmem(x), in_vmem(y), in_vmem(scale))


def g_kernel(xa, ya, xb, yb, scale, fb, scaled_a, scaled_b, steps_a, steps_b, mixed, inner_b):
    low = is_low()
    inner = is_inner()
    for p in range(HALF):
        state = pair_states(xa.at[p], ya.at[p], scaled_a.at[p], scale, low, steps_a.at[p])
        mixed[p] = jnp.where(inner, state, fb[p])
    for p in range(HALF):
        state = pair_states(xb.at[p], yb.at[p], scaled_b.at[p], scale, low, steps_b.at[p])
        inner_b[p] = jnp.where(inner, state, 0.0)


def g_states(xa, ya, xb, yb, scale, fb):
    length = xa.shape[1]
    y, steps = y_shape(length), steps_shape(length)
    return pl.pallas_call(
        g_kernel,
        in_specs=[VMEM] * 6,
        out_specs=[VMEM] * 6,
        out_shape=[y, y, steps, steps, STATE, STATE],
        compiler_params=params(),
        name="g_states",
    )(*map(in_vmem, (xa, ya, xb, yb, scale, fb)))


def add(a, b, parts, after=()):
    shape = pltpu.VMEM((HALF // parts, XW, DV), F32)
    return pl.pallas_call(
        functools.partial(add_parts_kernel, parts),
        in_specs=[VMEM] * 2 + [HBM] * len(after),
        out_specs=[VMEM] * parts,
        out_shape=[shape] * parts,
        compiler_params=params(),
        name="add",
    )(a, b, *after)


def add_parts_kernel(parts, a, b, *refs):
    outs = refs[-parts:]
    count = a.shape[0] // parts
    for i, out in enumerate(outs):
        for p in range(count):
            out[p] = a[i * count + p] + b[i * count + p]


def head_rows(x):
    lane = lax.broadcasted_iota(jnp.int32, x.shape, 1)
    zero = jnp.zeros_like(x)
    return jnp.concatenate([jnp.where(lane < DK, x, zero), jnp.where(lane >= DK, x, zero)], axis=0)


def head_blocks(y):
    zero = jnp.zeros_like(y[:, :DV])
    top = jnp.concatenate([y[:, :DV], zero], axis=1)
    return jnp.concatenate([top, jnp.concatenate([zero, y[:, DV:]], axis=1)], axis=0)


def state_blocks(state):
    row = lax.broadcasted_iota(jnp.int32, state.shape, 0)
    zero = jnp.zeros_like(state)
    both = jnp.concatenate([jnp.where(row < DK, state, zero), jnp.where(row >= DK, state, zero)], axis=1)
    return both.astype(BF16)


def turned(scores):
    return jnp.concatenate([scores[:, :CHUNK].T, scores[:, CHUNK:].T], axis=1)


def send(staged, p, when_low, when_high, columns, sem, low):
    to_low = pltpu.make_async_copy(staged.at[p], when_low.at[:, columns], sem.at[p])
    to_high = pltpu.make_async_copy(staged.at[p], when_high.at[:, columns], sem.at[p])

    @pl.when(low)
    def _():
        to_low.start()

    @pl.when(jnp.logical_not(low))
    def _():
        to_high.start()


def local_kernel(first, xf, yf, xg, yg, steps, near, scale, *refs):
    att, qg, kg, vg, o2, o4, o1_out, o3_out, sem1, sem3 = refs[-10:]
    low = is_low()
    inner = is_inner()
    row = lax.broadcasted_iota(jnp.int32, (CHUNK, 2 * CHUNK), 0)
    col = lax.rem(lax.broadcasted_iota(jnp.int32, (CHUNK, 2 * CHUNK), 1), CHUNK)
    keep = jnp.where(low, row - col, col - row) >= 0
    chunks = [slice(c, c + CHUNK) for c in range(0, xf.shape[1], CHUNK)]
    for p in range(HALF):
        base = jnp.where(inner, near[p], 0.0)
        parts, scores = [], []
        for c, rows in enumerate(chunks):
            x1, y1, x2, y2 = xf[p, rows, :], yf[p, rows, :], xg[p, rows, :], yg[p, rows, :]
            s = scale[rows, :]
            blocks = state_blocks(base + steps[p, c])
            parts.append((head_rows(x1), head_blocks(y1), x2, y2, jnp.concatenate([s, s], axis=1), blocks))
        for x1s, y1s, x2, y2, _, _ in parts:
            m = jnp.where(keep, dot(x2, x1s, NT), 0.0).astype(BF16)
            n = jnp.where(keep, dot(y2, y1s, NT), 0.0).astype(BF16)
            scores.append((m, n))
        for rows, (x1s, y1s, x2, y2, s, blocks), (m, n) in zip(chunks, parts, scores):
            o1_out[p, rows, :] = ((dot(m, y1s) + dot(x2, blocks)) * s).astype(BF16)
            o3_out[p, rows, :] = (dot(n, x1s) + dot(y2, blocks, NT)).astype(BF16)
            o2[p, rows, :] = dot(turned(m), head_blocks(y2))
            o4[p, rows, :] = dot(turned(n), head_rows(x2))
        send(o1_out, p, att, vg, pl.ds((first + p) * YW, YW), sem1, low)
        send(o3_out, p, qg, kg, pl.ds((first + p) * XW, XW), sem3, low)
    for p in range(HALF):
        pltpu.make_async_copy(o1_out.at[p], att.at[:, pl.ds((first + p) * YW, YW)], sem1.at[p]).wait()
        pltpu.make_async_copy(o3_out.at[p], qg.at[:, pl.ds((first + p) * XW, XW)], sem3.at[p]).wait()


def out_shapes(length):
    wide = jax.ShapeDtypeStruct((length, H * DV), BF16)
    narrow = jax.ShapeDtypeStruct((length, H * DK), BF16)
    return [wide, narrow, narrow, wide]


def local_terms(first, xf, yf, xg, yg, steps, near, scale, outs, after):
    length = xf.shape[1]
    ins = [*map(in_vmem, (xf, yf, xg, yg, steps)), near, in_vmem(scale)]
    return pl.pallas_call(
        functools.partial(local_kernel, first),
        in_specs=[VMEM] * 7 + [HBM] * (len(outs) + len(after)),
        out_specs=[HBM] * 4 + [VMEM] * 2,
        out_shape=out_shapes(length) + [y_shape(length, F32), x_shape(length, F32)],
        input_output_aliases={7 + i: i for i in range(len(outs))},
        scratch_shapes=[
            y_shape(length),
            x_shape(length),
            pltpu.SemaphoreType.DMA((HALF,)),
            pltpu.SemaphoreType.DMA((HALF,)),
        ],
        compiler_params=params(),
        name="local",
    )(*ins, *outs, *after)


def far_kernel(first, offset, count, mask_second, xf, yf, steps, far1, far2, o2, o4, scale, *refs):
    att, qg, kg, vg, o2_out, o4_out, sem2, sem4 = refs[-8:]
    low = is_low()
    inner = is_inner()
    chunks = [slice(c, c + CHUNK) for c in range(0, xf.shape[1], CHUNK)]
    for i in range(count):
        p = offset + i
        second = far2[i]
        base = far1[p] + (jnp.where(inner, 0.0, second) if mask_second else second)
        blocks = [state_blocks(base + steps[p, c]) for c in range(len(chunks))]
        wide = [dot(xf[p, rows, :], b) for rows, b in zip(chunks, blocks)]
        narrow = [dot(yf[p, rows, :], b, NT) for rows, b in zip(chunks, blocks)]
        for rows, a in zip(chunks, wide):
            s = scale[rows, :]
            o2_out[i, rows, :] = ((o2[p, rows, :] + a) * jnp.concatenate([s, s], axis=1)).astype(BF16)
        send(o2_out, i, vg, att, pl.ds((first + p) * YW, YW), sem2, low)
        for rows, a in zip(chunks, narrow):
            o4_out[i, rows, :] = (o4[p, rows, :] + a).astype(BF16)
        send(o4_out, i, kg, qg, pl.ds((first + p) * XW, XW), sem4, low)
    for i in range(count):
        p = offset + i
        pltpu.make_async_copy(o2_out.at[i], vg.at[:, pl.ds((first + p) * YW, YW)], sem2.at[i]).wait()
        pltpu.make_async_copy(o4_out.at[i], kg.at[:, pl.ds((first + p) * XW, XW)], sem4.at[i]).wait()


def far_terms(first, offset, count, mask_second, xf, yf, steps, far1, far2, o2, o4, scale, outs):
    length = xf.shape[1]
    ins = [*map(in_vmem, (xf, yf, steps)), far1, far2, *map(in_vmem, (o2, o4, scale))]
    return pl.pallas_call(
        functools.partial(far_kernel, first, offset, count, mask_second),
        in_specs=[VMEM] * 8 + [HBM] * 4,
        out_specs=[HBM] * 4,
        out_shape=out_shapes(length),
        input_output_aliases={8 + i: i for i in range(4)},
        scratch_shapes=[
            pltpu.VMEM((count, length, YW), BF16),
            pltpu.VMEM((count, length, XW), BF16),
            pltpu.SemaphoreType.DMA((count,)),
            pltpu.SemaphoreType.DMA((count,)),
        ],
        compiler_params=params(),
        name="far",
    )(*ins, *outs)


def scan_sum(state, size, sign):
    def moved(array, step):
        return lax.ppermute(array, "ctx", [(i, i + sign * step) for i in range(size) if 0 <= i + sign * step < size])

    total, step = moved(state, 1), 1
    while step < size:
        total, step = total + moved(total, step), 2 * step
    return total


def local(queries, keys, values, out_grad):
    size = lax.axis_size("ctx")
    xfa, yfa, xfb, yfb, xga, yga, xgb, ygb, scale_low, scale_high, fa, fa_steps = load(
        *map(in_hbm, (queries, keys, values, out_grad))
    )
    swap_x = [(0, 1), (1, 0), (2, 3), (3, 2)]
    swap_y = [(0, 2), (2, 0), (1, 3), (3, 1)]
    if size == 4:
        got_xa = lax.ppermute(fa, "ctx", swap_x)
    yfb, fb, fb_steps = f_states(xfb, yfb, scale_high)
    if size == 4:
        got_y1 = lax.ppermute(fb, "ctx", swap_y)
    yga, ygb, ga_steps, gb_steps, mixed, inner_b = g_states(xga, yga, xgb, ygb, scale_low, fb)
    if size == 4:
        got_xb = lax.ppermute(mixed, "ctx", swap_x)
        (sum_a,) = add(fa, got_xa, 1)
        got_y2 = lax.ppermute(sum_a, "ctx", swap_y)
        near_a, near_b, first_token = got_xa, got_xb, [sum_a]
        far_a, far_b = (got_y2, got_xb), got_y1
    else:
        near_a, near_b, first_token = scan_sum(fa, size, 1), scan_sum(fb, size, 1), []
        far_a, far_b = (scan_sum(mixed, size, -1), mixed), scan_sum(inner_b, size, -1)
    *outs, o2a, o4a = local_terms(0, xfa, yfa, xga, yga, fa_steps, near_a, scale_low, [], first_token)
    if size == 4:
        sums = add(got_y1, inner_b, SPLIT, [outs[1]])
        far_last = [lax.ppermute(s, "ctx", swap_x) for s in sums]
        second_token = list(sums)
    else:
        far_last, second_token = [jnp.zeros((HALF // SPLIT, XW, DV), F32)] * SPLIT, []
    *outs, o2b, o4b = local_terms(HALF, xfb, yfb, xgb, ygb, fb_steps, near_b, scale_low, outs, second_token)
    outs = far_terms(0, 0, HALF, True, xfa, yfa, ga_steps, *far_a, o2a, o4a, scale_high, outs)
    count = HALF // SPLIT
    for i in range(SPLIT):
        outs = far_terms(
            HALF, i * count, count, False, xfb, yfb, gb_steps, far_b, far_last[i], o2b, o4b, scale_high, outs
        )
    return tuple(outs)


def solution(mesh):
    spec = P(("batch", "ctx"), None)
    return jax.shard_map(local, mesh=mesh, in_specs=(spec,) * 4, out_specs=(spec,) * 4, check_vma=False)
```

time: 146 us -> 30.4 us (0.21)
  matrix products: 53.4 us -> 0 us
  waiting for transfers between devices: 41.8 us -> 3.64 us
  local copies, waits for them, and re-layouts: 22.1 us -> 1.22 us
  Pallas kernels: 0 us -> 15.2 us
  between operations: 14.2 us -> 0.74 us
  other arithmetic: 12.7 us -> 0 us
  starting transfers between devices: 0.08 us -> 9.44 us
    dot_general x12 -> x0, matrix products: 53.4 us -> none  [the longest x1 7.97 us: local(): jnp.einsum('hts,thc->shc', scores_bf, scaled_grad, preferred_element_type...]
    all_gather x2 -> x0, waiting for transfers between devices: 41.8 us -> none  [prefix_2(): everything = lax.all_gather(array, axis)]
    unnamed x28 -> x2, local copies, waits for them, and re-layouts: 17.6 us -> 1.22 us
    pallas_call x0 -> x10, Pallas kernels: none -> 15.2 us  [the longest x2 6.92 us: local_terms(): pl.pallas_call(functools.partial(local_kernel, first), in_specs=[VMEM] *...]
    select_n x8 -> x0, other arithmetic: 9.83 us -> none  [turn(): return jnp.where(reached, new, before)]
    ppermute x0 -> x6, starting transfers between devices: none -> 9.44 us  [the longest x1 3 us: local(): got_xa = lax.ppermute(fa, 'ctx', swap_x)]
    convert_element_type x1 -> x0, local copies, waits for them, and re-layouts: 4.53 us -> none  [local(): grad_h.astype(jnp.float32)]
    ppermute x0 -> x6, waiting for transfers between devices: none -> 3.64 us  [the longest x1 3.63 us: local(): got_xa = lax.ppermute(fa, 'ctx', swap_x)]
  transfers between devices with their start and end apart: 2 -> 6, of which waited for: 2 -> 1; matrix products, arithmetic and copies ran while one was open for 23% -> 0% of each run, Pallas kernels for 0% -> 36%
where the time goes in v2:
time: 30.4 us; the launch traced here: 30.3 us
  Pallas kernels  15.2 us (50%)
  starting transfers between devices  9.44 us (31%)
  waiting for transfers between devices  3.64 us (12%)
  local copies, waits for them, and re-layouts  1.22 us (4%)
  between operations  0.74 us (2%)
    pallas_call x2, Pallas kernels, local_terms(): pl.pallas_call(functools.partial(local_kernel, first), in_specs=[VMEM] *...  6.92 us
    pallas_call x3, Pallas kernels, far_terms(): pl.pallas_call(functools.partial(far_kernel, first, offset, count, mask_s...  3.74 us
    ppermute x1, waiting for transfers between devices, local(): got_xa = lax.ppermute(fa, 'ctx', swap_x)  3.63 us
    pallas_call x1, Pallas kernels, load(): pl.pallas_call(load_kernel, in_specs=[HBM] * 4, out_specs=[VMEM] * 12, ou...  3.23 us
    ppermute x1, starting transfers between devices, local(): got_xa = lax.ppermute(fa, 'ctx', swap_x)  3 us
    ppermute x1, starting transfers between devices, local(): got_y2 = lax.ppermute(sum_a, 'ctx', swap_y)  2.16 us
    ppermute x2, starting transfers between devices, local(): far_last = [lax.ppermute(s, 'ctx', swap_x) for s in sums]  2.09 us
    ppermute x1, starting transfers between devices, local(): got_y1 = lax.ppermute(fb, 'ctx', swap_y)  1.59 us
  transfers between devices with their start and end apart: 6, of which 1 were waited for; matrix products, arithmetic and copies ran while one was open for 0% of the time, Pallas kernels for 36%

profile of v2, /device:TPU:0, one launch (start us, length us, event | category | flops | bytes accessed | tf_op | source)
XLA Modules:
  0.0 30.3 jit_solution(1265227771468705435)
XLA Ops:
  0.6 3.2 %load.1 = (bf16[4,512,128]{2,1,0:T(8,128)(2,1)S(1)}, bf16[4,512,256]{2,1,0:T(8,128)(2,1)S(1)}, bf16[4,512,128]{2,1,0:T(8,128)(2,1)S(1)}, bf16[4,512,256]{2,1,0:T...) custom-call(bf16[512,1024]{1,0:T(8,128)(2,1)} %q.1, ...), custom_call_target="tpu_custom_call" | custom-call | tf_op jit(solution)/shard_map/load/pallas_call | solution.py:145
  3.9 3.0 %collective-permute-start.1 = (f32[4,128,128]{2,1,0:T(8,128)S(1)}, f32[4,128,128]{2,1,0:T(8,128)S(1)}, u32[]{:S(2)}, u32[]{:S(2)}) collective-permute-start(f32[4,128,128]{2,1,0:T(8,128)S(1)} %get-tuple-element.63.a), channel_id=1, source_target_pairs={{0,1},{1,0},{2,3},{3,2},{4,5},{5,4},{6,7},{7,6},{8,9},{9,8},{10,11... | collective-permute-start | bytes 786440 | tf_op jit(solution)/shard_map/ppermute | solution.py:375
  6.9 0.5 %f_states.1 = (bf16[4,512,256]{2,1,0:T(8,128)(2,1)S(1)}, f32[4,128,128]{2,1,0:T(8,128)S(1)}, f32[4,4,128,128]{3,2,1,0:T(8,128)S(1)}) custom-call(bf16[4,512,128]{2,1,0:T(8,128)(2,1)S(1)} %get-tuple-element.47.x.xf, bf16[4,512,256]{2,1,0:T(8,128)(2,1)S(1)} %get-tuple-element.48.y, f32[512,128]{1,0:T(8,128)S(1)} %get-tuple-element.49.scale), custom_call_target="tpu_custom_call" | custom-call | tf_op jit(solution)/shard_map/f_states/pallas_call | solution.py:164
  7.4 1.6 %collective-permute-start = (f32[4,128,128]{2,1,0:T(8,128)S(1)}, f32[4,128,128]{2,1,0:T(8,128)S(1)}, u32[]{:S(2)}, u32[]{:S(2)}) collective-permute-start(f32[4,128,128]{2,1,0:T(8,128)S(1)} %get-tuple-element.56.fb), channel_id=1, source_target_pairs={{0,2},{2,0},{1,3},{3,1},{4,6},{6,4},{5,7},{7,5},{8,10},{10,8},{9,1... | collective-permute-start | bytes 786440 | tf_op jit(solution)/shard_map/ppermute | solution.py:378
  9.0 0.8 %g_states.1 = (bf16[4,512,256]{2,1,0:T(8,128)(2,1)S(1)}, bf16[4,512,256]{2,1,0:T(8,128)(2,1)S(1)}, f32[4,4,128,128]{3,2,1,0:T(8,128)S(1)}, f32[4,4,128,128]{3,2,...) custom-call(bf16[4,512,128]{2,1,0:T(8,128)(2,1)S(1)} %get-tuple-element.51.xa.xg, ...), custom_call_target="tpu_custom_call" | custom-call | tf_op jit(solution)/shard_map/g_states/pallas_call | solution.py:188
  9.8 0.6 %collective-permute-start.3 = (f32[4,128,128]{2,1,0:T(8,128)S(1)}, f32[4,128,128]{2,1,0:T(8,128)S(1)}, u32[]{:S(2)}, u32[]{:S(2)}) collective-permute-start(f32[4,128,128]{2,1,0:T(8,128)S(1)} %get-tuple-element.68), channel_id=1, source_target_pairs={{0,1},{1,0},{2,3},{3,2},{4,5},{5,4},{6,7},{7,6},{8,9},{9,8},{10,11... | collective-permute-start | bytes 786440 | tf_op jit(solution)/shard_map/ppermute | solution.py:381
  10.4 3.6 %collective-permute-done.1.b.near = f32[4,128,128]{2,1,0:T(8,128)S(1)} collective-permute-done((f32[4,128,128]{2,1,0:T(8,128)S(1)}, f32[4,128,128]{2,1,0:T(8,128)S(1)}, u32[]{:S(2)}, u32[]{:S(2)}) %collective-permute-start.1) | collective-permute-done | bytes 262176 | tf_op jit(solution)/shard_map/ppermute | solution.py:375
  14.0 2.2 %collective-permute-start.5 = (f32[4,128,128]{2,1,0:T(8,128)S(1)}, f32[4,128,128]{2,1,0:T(8,128)S(1)}, u32[]{:S(2)}, u32[]{:S(2)}) collective-permute-start(f32[4,128,128]{2,1,0:T(8,128)S(1)} %add.2.refs_0_), channel_id=1, source_target_pairs={{0,2},{2,0},{1,3},{3,1},{4,6},{6,4},{5,7},{7,5},{8,10},{10,8},{9,1... | collective-permute-start | bytes 786440 | tf_op jit(solution)/shard_map/ppermute | solution.py:383
  16.2 3.5 %local.2 = (bf16[512,2048]{1,0:T(8,128)(2,1)}, bf16[512,1024]{1,0:T(8,128)(2,1)}, bf16[512,1024]{1,0:T(8,128)(2,1)}, bf16[512,2048]{1,0:T(8,128)(2,1)}, f32[4,51...) custom-call(bf16[4,512,128]{2,1,0:T(8,128)(2,1)S(1)} %get-tuple-element.59.xf, ...), custom_call_target="tpu_custom_call" | custom-call | tf_op jit(solution)/shard_map/local/pallas_call | solution.py:295
  19.7 0.0 collective-permute-done.a.far1
  19.7 0.0 copy-start
  19.7 1.2 %copy-done = bf16[512,1024]{1,0:T(8,128)(2,1)S(1)} copy-done((bf16[512,1024]{1,0:T(8,128)(2,1)S(1)}, bf16[512,1024]{1,0:T(8,128)(2,1)}, u32[]{:S(2)}) %copy-start) | copy-done | bytes 1048600
  20.9 1.6 %collective-permute-start.4 = (f32[2,128,128]{2,1,0:T(8,128)S(1)}, f32[2,128,128]{2,1,0:T(8,128)S(1)}, u32[]{:S(2)}, u32[]{:S(2)}) collective-permute-start(f32[2,128,128]{2,1,0:T(8,128)S(1)} %get-tuple-element.72.refs_4_), channel_id=1, source_target_pairs={{0,1},{1,0},{2,3},{3,2},{4,5},{5,4},{6,7},{7,6},{8,9},{9,8},{10,11... | collective-permute-start | bytes 393224 | tf_op jit(solution)/shard_map/ppermute | solution.py:392
  22.5 0.5 %collective-permute-start.2 = (f32[2,128,128]{2,1,0:T(8,128)S(1)}, f32[2,128,128]{2,1,0:T(8,128)S(1)}, u32[]{:S(2)}, u32[]{:S(2)}) collective-permute-start(f32[2,128,128]{2,1,0:T(8,128)S(1)} %get-tuple-element.65.refs_5_), channel_id=1, source_target_pairs={{0,1},{1,0},{2,3},{3,2},{4,5},{5,4},{6,7},{7,6},{8,9},{9,8},{10,11... | collective-permute-start | bytes 393224 | tf_op jit(solution)/shard_map/ppermute | solution.py:392
  23.0 0.0 collective-permute-done.3.near.far2
  23.0 3.5 %local.3 = (bf16[512,2048]{1,0:T(8,128)(2,1)}, bf16[512,1024]{1,0:T(8,128)(2,1)}, bf16[512,1024]{1,0:T(8,128)(2,1)}, bf16[512,2048]{1,0:T(8,128)(2,1)}, f32[4,51...) custom-call(bf16[4,512,128]{2,1,0:T(8,128)(2,1)S(1)} %get-tuple-elem, ...), custom_call_target="tpu_custom_call", output_to_operand_aliasing={{0}: (7, {}), {1}: (8, {}), {2}: (9, {}), {3}: (10, {})} | custom-call | tf_op jit(solution)/shard_map/local/pallas_call | solution.py:295
  26.5 0.0 collective-permute-done.5.far1
  26.5 1.5 %far.3 = (bf16[512,2048]{1,0:T(8,128)(2,1)}, bf16[512,1024]{1,0:T(8,128)(2,1)}, bf16[512,1024]{1,0:T(8,128)(2,1)}, bf16[512,2048]{1,0:T(8,128)(2,1)}) custom-call(bf16[4,512,128]{2,1,0:T(8,128)(2,1)S(1)} %get-tuple-element.59.xf, ...), custom_call_target="tpu_custom_call", output_to_operand_aliasing={{0}: (8, {}), {1}: (9, {}), {2}: (10, {}), {3}: (11, {})} | custom-call | tf_op jit(solution)/shard_map/far/pallas_call | solution.py:340
  28.0 0.0 collective-permute-done.4.far2
  28.0 1.1 %far.4 = (bf16[512,2048]{1,0:T(8,128)(2,1)}, bf16[512,1024]{1,0:T(8,128)(2,1)}, bf16[512,1024]{1,0:T(8,128)(2,1)}, bf16[512,2048]{1,0:T(8,128)(2,1)}) custom-call(bf16[4,512,128]{2,1,0:T(8,128)(2,1)S(1)} %get-tuple-element.47.x.xf, ...), custom_call_target="tpu_custom_call", output_to_operand_aliasing={{0}: (8, {}), {1}: (9, {}), {2}: (10, {}), {3}: (11, {})} | custom-call | tf_op jit(solution)/shard_map/far/pallas_call | solution.py:340
  29.1 0.0 collective-permute-done.2.far2
  29.1 1.1 %far.5 = (bf16[512,2048]{1,0:T(8,128)(2,1)}, bf16[512,1024]{1,0:T(8,128)(2,1)}, bf16[512,1024]{1,0:T(8,128)(2,1)}, bf16[512,2048]{1,0:T(8,128)(2,1)}) custom-call(bf16[4,512,128]{2,1,0:T(8,128)(2,1)S(1)} %get-tuple-element.47.x.xf, ...), custom_call_target="tpu_custom_call", output_to_operand_aliasing={{0}: (8, {}), {1}: (9, {}), {2}: (10, {}), {3}: (11, {})} | custom-call | tf_op jit(solution)/shard_map/far/pallas_call | solution.py:340
  (2 shorter events, 0.1 us)
Async XLA Ops:
  3.9 10.1 %collective-permute-start.1 = (f32[4,128,128]{2,1,0:T(8,128)S(1)}, f32[4,128,128]{2,1,0:T(8,128)S(1)}, u32[]{:S(2)}, u32[]{:S(2)}) collective-permute-start(f32[4,128,128]{2,1,0:T(8,128)S(1)} %get-tuple-element.63.a), channel_id=1, source_target_pairs={{0,1},{1,0},{2,3},{3,2},{4,5},{5,4},{6,7},{7,6},{8,9},{9,8},{10,11... | collective-permute-start | bytes 786440 | tf_op jit(solution)/shard_map/ppermute | solution.py:375
  7.4 12.3 %collective-permute-start = (f32[4,128,128]{2,1,0:T(8,128)S(1)}, f32[4,128,128]{2,1,0:T(8,128)S(1)}, u32[]{:S(2)}, u32[]{:S(2)}) collective-permute-start(f32[4,128,128]{2,1,0:T(8,128)S(1)} %get-tuple-element.56.fb), channel_id=1, source_target_pairs={{0,2},{2,0},{1,3},{3,1},{4,6},{6,4},{5,7},{7,5},{8,10},{10,8},{9,1... | collective-permute-start | bytes 786440 | tf_op jit(solution)/shard_map/ppermute | solution.py:378
  9.8 13.2 %collective-permute-start.3 = (f32[4,128,128]{2,1,0:T(8,128)S(1)}, f32[4,128,128]{2,1,0:T(8,128)S(1)}, u32[]{:S(2)}, u32[]{:S(2)}) collective-permute-start(f32[4,128,128]{2,1,0:T(8,128)S(1)} %get-tuple-element.68), channel_id=1, source_target_pairs={{0,1},{1,0},{2,3},{3,2},{4,5},{5,4},{6,7},{7,6},{8,9},{9,8},{10,11... | collective-permute-start | bytes 786440 | tf_op jit(solution)/shard_map/ppermute | solution.py:381
  14.0 12.5 %collective-permute-start.5 = (f32[4,128,128]{2,1,0:T(8,128)S(1)}, f32[4,128,128]{2,1,0:T(8,128)S(1)}, u32[]{:S(2)}, u32[]{:S(2)}) collective-permute-start(f32[4,128,128]{2,1,0:T(8,128)S(1)} %add.2.refs_0_), channel_id=1, source_target_pairs={{0,2},{2,0},{1,3},{3,1},{4,6},{6,4},{5,7},{7,5},{8,10},{10,8},{9,1... | collective-permute-start | bytes 786440 | tf_op jit(solution)/shard_map/ppermute | solution.py:383
  19.7 1.2 %copy-start = (bf16[512,1024]{1,0:T(8,128)(2,1)S(1)}, bf16[512,1024]{1,0:T(8,128)(2,1)}, u32[]{:S(2)}) copy-start(bf16[512,1024]{1,0:T(8,128)(2,1)} %get-tuple-element.64.refs_0_.refs_1_) | copy-start | bytes 3145732
  20.9 7.0 %collective-permute-start.4 = (f32[2,128,128]{2,1,0:T(8,128)S(1)}, f32[2,128,128]{2,1,0:T(8,128)S(1)}, u32[]{:S(2)}, u32[]{:S(2)}) collective-permute-start(f32[2,128,128]{2,1,0:T(8,128)S(1)} %get-tuple-element.72.refs_4_), channel_id=1, source_target_pairs={{0,1},{1,0},{2,3},{3,2},{4,5},{5,4},{6,7},{7,6},{8,9},{9,8},{10,11... | collective-permute-start | bytes 393224 | tf_op jit(solution)/shard_map/ppermute | solution.py:392
  22.5 6.6 %collective-permute-start.2 = (f32[2,128,128]{2,1,0:T(8,128)S(1)}, f32[2,128,128]{2,1,0:T(8,128)S(1)}, u32[]{:S(2)}, u32[]{:S(2)}) collective-permute-start(f32[2,128,128]{2,1,0:T(8,128)S(1)} %get-tuple-element.65.refs_5_), channel_id=1, source_target_pairs={{0,1},{1,0},{2,3},{3,2},{4,5},{5,4},{6,7},{7,6},{8,9},{9,8},{10,11... | collective-permute-start | bytes 393224 | tf_op jit(solution)/shard_map/ppermute | solution.py:392

commit v3 on v2

v3 whole, which is shorter than its diff:
```python
import functools

import jax
import jax.numpy as jnp
from jax import lax
from jax.experimental import pallas as pl
from jax.experimental.pallas import tpu as pltpu
from jax.sharding import PartitionSpec as P


H = 16
DK = 64
DV = 128
PAIRS = H // 2
HALF = PAIRS // 2
XW = 2 * DK
YW = 2 * DV
CHUNK = 128
SPLIT = 2
VMEM_LIMIT = 12 * 1024 * 1024

NN = (((1,), (0,)), ((), ()))
NT = (((1,), (1,)), ((), ()))
TN = (((0,), (0,)), ((), ()))
F32 = jnp.float32
BF16 = jnp.bfloat16

HBM = pl.BlockSpec(memory_space=pltpu.HBM)
VMEM = pl.BlockSpec(memory_space=pltpu.VMEM)


def dot(a, b, dims=NN):
    return lax.dot_general(a, b, dims, preferred_element_type=F32)


def is_low():
    size = lax.axis_size("ctx")
    return lax.axis_index("ctx") < (size // 2 if size == 4 else size)


def is_inner():
    at = lax.axis_index("ctx")
    return (at == 1) | (at == 2) if lax.axis_size("ctx") == 4 else at >= 0


def in_vmem(array):
    return pltpu.with_memory_space_constraint(array, pltpu.VMEM)


def in_hbm(array):
    return pltpu.with_memory_space_constraint(array, pltpu.HBM)


def x_shape(length, dtype=BF16):
    return pltpu.VMEM((length, HALF * XW), dtype)


def y_shape(length, dtype=BF16):
    return pltpu.VMEM((length, HALF * YW), dtype)


STATE = pltpu.VMEM((HALF, XW, DV), F32)


def steps_shape(length):
    return pltpu.VMEM((HALF, length // CHUNK, XW, DV), F32)


def params():
    return pltpu.CompilerParams(vmem_limit_bytes=VMEM_LIMIT)


def diagonal(square):
    return jnp.concatenate([square[:DK, :DV], square[DK:, DV:]], axis=0)


def xs(p):
    return slice(p * XW, (p + 1) * XW)


def ys(p):
    return slice(p * YW, (p + 1) * YW)


def chunks_of(array):
    return [slice(c, c + CHUNK) for c in range(0, array.shape[0], CHUNK)]


def twice(scale):
    return jnp.concatenate([scale, scale], axis=1)


def chunk_states(x, y, scaled, scale, rows):
    s = twice(scale[rows, :])
    states = []
    for p in range(HALF):
        new = (y[rows, ys(p)].astype(F32) * s).astype(BF16)
        scaled[rows, ys(p)] = new
        states.append(diagonal(dot(x[rows, xs(p)], new, TN)))
    return states


def block_states(parts, backward, steps):
    count = len(parts)
    states = []
    for p in range(HALF):
        zero = jnp.zeros_like(parts[0][p])
        before, after = [zero], [zero]
        for c in range(count - 1):
            before.append(before[-1] + parts[c][p])
            after.append(after[-1] + parts[count - 1 - c][p])
        for c in range(count):
            steps[p, c] = jnp.where(backward, after[count - 1 - c], before[c])
        states.append(before[-1] + parts[-1][p])
    return states


def load_kernel(q, k, v, do, xfa, yfa, xfb, yfb, xga, yga, xgb, ygb, scale_low, scale_high, state, steps, raw, sems):
    low = is_low()
    length = q.shape[0]
    chunks = chunks_of(q)

    def copies(a, b, x, y, half, at):
        wide, narrow = pl.ds(half * HALF * YW, HALF * YW), pl.ds(half * HALF * XW, HALF * XW)
        return [
            (
                pltpu.make_async_copy(a.at[rows, narrow], x.at[rows, :], sems.at[at, 0, c]),
                pltpu.make_async_copy(b.at[rows, wide], y.at[rows, :], sems.at[at, 1, c]),
            )
            for c, rows in enumerate(chunks)
        ]

    def start(f, g):
        for a, b, x, y, half, at in (
            (*f, xfa, raw, 0, 0),
            (*f, xfb, yfb, 1, 1),
            (*g, xga, yga, 0, 2),
            (*g, xgb, ygb, 1, 3),
        ):
            for pair in copies(a, b, x, y, half, at):
                for copy in pair:
                    copy.start()

    @pl.when(low)
    def _():
        start((k, v), (q, do))

    @pl.when(jnp.logical_not(low))
    def _():
        start((q, do), (k, v))

    at = lax.axis_index("ctx") * length + lax.broadcasted_iota(jnp.int32, (length, DV), 0)
    scale = 1.0 / jnp.sqrt(DK * (at.astype(F32) + 1.0))
    scale_low[...] = jnp.where(low, scale, 1.0)
    scale_high[...] = jnp.where(low, 1.0, scale)
    parts = []
    for rows, pair in zip(chunks, copies(k, v, xfa, raw, 0, 0)):
        for copy in pair:
            copy.wait()
        parts.append(chunk_states(xfa, raw, yfa, scale_high, rows))
    for p, new in enumerate(block_states(parts, jnp.logical_not(low), steps)):
        state[p] = new
    for x, y, at in ((xfb, yfb, 1), (xga, yga, 2), (xgb, ygb, 3)):
        for pair in copies(k, v, x, y, 0, at):
            for copy in pair:
                copy.wait()


def load(q, k, v, do):
    length = q.shape[0]
    x, y = x_shape(length), y_shape(length)
    scale = pltpu.VMEM((length, DV), F32)
    return pl.pallas_call(
        load_kernel,
        in_specs=[HBM] * 4,
        out_specs=[VMEM] * 12,
        out_shape=[x, y, x, y, x, y, x, y, scale, scale, STATE, steps_shape(length)],
        scratch_shapes=[y, pltpu.SemaphoreType.DMA((4, 2, length // CHUNK))],
        compiler_params=params(),
        name="load",
    )(q, k, v, do)


def f_kernel(x, y, scale, scaled, state, steps):
    parts = [chunk_states(x, y, scaled, scale, rows) for rows in chunks_of(x)]
    for p, new in enumerate(block_states(parts, jnp.logical_not(is_low()), steps)):
        state[p] = new


def f_states(x, y, scale):
    length = x.shape[0]
    return pl.pallas_call(
        f_kernel,
        in_specs=[VMEM] * 3,
        out_specs=[VMEM] * 3,
        out_shape=[y_shape(length), STATE, steps_shape(length)],
        compiler_params=params(),
        name="f_states",
    )(in_vmem(x), in_vmem(y), in_vmem(scale))


def g_kernel(xa, ya, xb, yb, scale, fb, scaled_a, scaled_b, steps_a, steps_b, mixed, inner_b):
    low = is_low()
    inner = is_inner()
    parts = [chunk_states(xa, ya, scaled_a, scale, rows) for rows in chunks_of(xa)]
    for p, new in enumerate(block_states(parts, low, steps_a)):
        mixed[p] = jnp.where(inner, new, fb[p])
    parts = [chunk_states(xb, yb, scaled_b, scale, rows) for rows in chunks_of(xb)]
    for p, new in enumerate(block_states(parts, low, steps_b)):
        inner_b[p] = jnp.where(inner, new, 0.0)


def g_states(xa, ya, xb, yb, scale, fb):
    length = xa.shape[0]
    y, steps = y_shape(length), steps_shape(length)
    return pl.pallas_call(
        g_kernel,
        in_specs=[VMEM] * 6,
        out_specs=[VMEM] * 6,
        out_shape=[y, y, steps, steps, STATE, STATE],
        compiler_params=params(),
        name="g_states",
    )(*map(in_vmem, (xa, ya, xb, yb, scale, fb)))


def add_kernel(parts, a, b, *refs):
    outs = refs[-parts:]
    count = a.shape[0] // parts
    for i, out in enumerate(outs):
        for p in range(count):
            out[p] = a[i * count + p] + b[i * count + p]


def add(a, b, parts, after=()):
    shape = pltpu.VMEM((HALF // parts, XW, DV), F32)
    return pl.pallas_call(
        functools.partial(add_kernel, parts),
        in_specs=[VMEM] * (2 + len(after)),
        out_specs=[VMEM] * parts,
        out_shape=[shape] * parts,
        compiler_params=params(),
        name="add",
    )(a, b, *map(in_vmem, after))


def head_rows(x):
    lane = lax.broadcasted_iota(jnp.int32, x.shape, 1)
    zero = jnp.zeros_like(x)
    return jnp.concatenate([jnp.where(lane < DK, x, zero), jnp.where(lane >= DK, x, zero)], axis=0)


def head_blocks(y):
    zero = jnp.zeros_like(y[:, :DV])
    top = jnp.concatenate([y[:, :DV], zero], axis=1)
    return jnp.concatenate([top, jnp.concatenate([zero, y[:, DV:]], axis=1)], axis=0)


def state_blocks(state):
    row = lax.broadcasted_iota(jnp.int32, state.shape, 0)
    zero = jnp.zeros_like(state)
    both = jnp.concatenate([jnp.where(row < DK, state, zero), jnp.where(row >= DK, state, zero)], axis=1)
    return both.astype(BF16)


def turned(scores):
    return jnp.concatenate([scores[:, :CHUNK].T, scores[:, CHUNK:].T], axis=1)


def out_copies(staged, at, when_low, when_high, pair, width, sem):
    source = staged.at[:, pl.ds(at * width, width)]
    columns = pl.ds(pair * width, width)
    return [pltpu.make_async_copy(source, target.at[:, columns], sem.at[at]) for target in (when_low, when_high)]


def send(copies, low):
    @pl.when(low)
    def _():
        copies[0].start()

    @pl.when(jnp.logical_not(low))
    def _():
        copies[1].start()


def local_kernel(first, with_near, xf, yf, xg, yg, *refs):
    low = is_low()
    if with_near:
        steps, near, scale = refs[:3]
        att, qg, kg, vg, o2, o4, o1_out, o3_out, sem1, sem3 = refs[-10:]
    else:
        o1_out, o3_out, o2, o4 = refs[-4:]
    row = lax.broadcasted_iota(jnp.int32, (CHUNK, 2 * CHUNK), 0)
    col = lax.rem(lax.broadcasted_iota(jnp.int32, (CHUNK, 2 * CHUNK), 1), CHUNK)
    keep = jnp.where(low, row - col, col - row) >= 0
    chunks = chunks_of(xf)
    started = []
    for p in range(HALF):
        if with_near:
            base = jnp.where(is_inner(), near[p], 0.0)
        parts, scores = [], []
        for c, rows in enumerate(chunks):
            x1, y1, x2, y2 = xf[rows, xs(p)], yf[rows, ys(p)], xg[rows, xs(p)], yg[rows, ys(p)]
            blocks = state_blocks(base + steps[p, c]) if with_near else None
            parts.append((head_rows(x1), head_blocks(y1), x2, y2, blocks))
        for x1s, y1s, x2, y2, _ in parts:
            m = jnp.where(keep, dot(x2, x1s, NT), 0.0).astype(BF16)
            n = jnp.where(keep, dot(y2, y1s, NT), 0.0).astype(BF16)
            scores.append((m, n))
        for rows, (x1s, y1s, x2, y2, blocks), (m, n) in zip(chunks, parts, scores):
            o1, o3 = dot(m, y1s), dot(n, x1s)
            if with_near:
                o1 = (o1 + dot(x2, blocks)) * twice(scale[rows, :])
                o3 = o3 + dot(y2, blocks, NT)
            o1_out[rows, ys(p)] = o1.astype(o1_out.dtype)
            o3_out[rows, xs(p)] = o3.astype(o3_out.dtype)
            o2[rows, ys(p)] = dot(turned(m), head_blocks(y2))
            o4[rows, xs(p)] = dot(turned(n), head_rows(x2))
        if with_near:
            wide = out_copies(o1_out, p, att, vg, first + p, YW, sem1)
            narrow = out_copies(o3_out, p, qg, kg, first + p, XW, sem3)
            send(wide, low)
            send(narrow, low)
            started += [wide[0], narrow[0]]
    for copy in started:
        copy.wait()


def out_shapes(length):
    wide = jax.ShapeDtypeStruct((length, H * DV), BF16)
    narrow = jax.ShapeDtypeStruct((length, H * DK), BF16)
    return [wide, narrow, narrow, wide]


def out_scratch(length, count):
    return [
        pltpu.VMEM((length, count * YW), BF16),
        pltpu.VMEM((length, count * XW), BF16),
        pltpu.SemaphoreType.DMA((count,)),
        pltpu.SemaphoreType.DMA((count,)),
    ]


def local_terms(xf, yf, xg, yg):
    length = xf.shape[0]
    x, y = x_shape(length, F32), y_shape(length, F32)
    return pl.pallas_call(
        functools.partial(local_kernel, 0, False),
        in_specs=[VMEM] * 4,
        out_specs=[VMEM] * 4,
        out_shape=[y, x, y, x],
        compiler_params=params(),
        name="local",
    )(*map(in_vmem, (xf, yf, xg, yg)))


def local_near_terms(first, xf, yf, xg, yg, steps, near, scale, after):
    length = xf.shape[0]
    return pl.pallas_call(
        functools.partial(local_kernel, first, True),
        in_specs=[VMEM] * (7 + len(after)),
        out_specs=[HBM] * 4 + [VMEM] * 2,
        out_shape=out_shapes(length) + [y_shape(length, F32), x_shape(length, F32)],
        scratch_shapes=out_scratch(length, HALF),
        compiler_params=params(),
        name="local_near",
    )(*map(in_vmem, (xf, yf, xg, yg, steps)), near, in_vmem(scale), *map(in_vmem, after))


def cross(chunks, x, y, blocks, wide, narrow, at, pair, scale, wide_out, narrow_out, copies, low):
    a = [dot(x[rows, xs(at)], b) for rows, b in zip(chunks, blocks)]
    b = [dot(y[rows, ys(at)], b, NT) for rows, b in zip(chunks, blocks)]
    for rows, new in zip(chunks, a):
        wide_out[rows, ys(pair)] = ((wide[rows, ys(at)] + new) * twice(scale[rows, :])).astype(BF16)
    send(copies[0], low)
    for rows, new in zip(chunks, b):
        narrow_out[rows, xs(pair)] = (narrow[rows, xs(at)] + new).astype(BF16)
    send(copies[1], low)
    return [copies[0][0], copies[1][0]]


def finish_kernel(xf, yf, xg, yg, f_steps, g_steps, near, far1, far2, o1, o2, o3, o4, scale_low, scale_high, *refs):
    att, qg, kg, vg, o1_out, o3_out, sem1, sem3, o2_out, o4_out, sem2, sem4 = refs[-12:]
    low = is_low()
    inner = is_inner()
    chunks = chunks_of(xf)
    started = []
    for p in range(HALF):
        base = jnp.where(inner, near[p], 0.0)
        blocks = [state_blocks(base + f_steps[p, c]) for c in range(len(chunks))]
        copies = out_copies(o1_out, p, att, vg, p, YW, sem1), out_copies(o3_out, p, qg, kg, p, XW, sem3)
        started += cross(chunks, xg, yg, blocks, o1, o3, p, p, scale_low, o1_out, o3_out, copies, low)
        base = far1[p] + jnp.where(inner, 0.0, far2[p])
        blocks = [state_blocks(base + g_steps[p, c]) for c in range(len(chunks))]
        copies = out_copies(o2_out, p, vg, att, p, YW, sem2), out_copies(o4_out, p, kg, qg, p, XW, sem4)
        started += cross(chunks, xf, yf, blocks, o2, o4, p, p, scale_high, o2_out, o4_out, copies, low)
    for copy in started:
        copy.wait()


def finish_terms(xf, yf, xg, yg, f_steps, g_steps, near, far1, far2, o1, o2, o3, o4, scale_low, scale_high, outs):
    length = xf.shape[0]
    ins = [
        *map(in_vmem, (xf, yf, xg, yg, f_steps, g_steps)),
        near,
        far1,
        far2,
        *map(in_vmem, (o1, o2, o3, o4, scale_low, scale_high)),
    ]
    return pl.pallas_call(
        finish_kernel,
        in_specs=[VMEM] * len(ins) + [HBM] * 4,
        out_specs=[HBM] * 4,
        out_shape=out_shapes(length),
        input_output_aliases={len(ins) + i: i for i in range(4)},
        scratch_shapes=out_scratch(length, HALF) * 2,
        compiler_params=params(),
        name="finish",
    )(*ins, *outs)


def far_kernel(first, offset, count, xf, yf, steps, far1, far2, o2, o4, scale, *refs):
    att, qg, kg, vg, o2_out, o4_out, sem2, sem4 = refs[-8:]
    low = is_low()
    chunks = chunks_of(xf)
    started = []
    for i in range(count):
        p = offset + i
        base = far1[p] + far2[i]
        blocks = [state_blocks(base + steps[p, c]) for c in range(len(chunks))]
        pair = first + p
        copies = out_copies(o2_out, i, vg, att, pair, YW, sem2), out_copies(o4_out, i, kg, qg, pair, XW, sem4)
        started += cross(chunks, xf, yf, blocks, o2, o4, p, i, scale, o2_out, o4_out, copies, low)
    for copy in started:
        copy.wait()


def far_terms(first, offset, count, xf, yf, steps, far1, far2, o2, o4, scale, outs):
    length = xf.shape[0]
    ins = [*map(in_vmem, (xf, yf, steps)), far1, far2, *map(in_vmem, (o2, o4, scale))]
    return pl.pallas_call(
        functools.partial(far_kernel, first, offset, count),
        in_specs=[VMEM] * 8 + [HBM] * 4,
        out_specs=[HBM] * 4,
        out_shape=out_shapes(length),
        input_output_aliases={8 + i: i for i in range(4)},
        scratch_shapes=out_scratch(length, count),
        compiler_params=params(),
        name="far",
    )(*ins, *outs)


def scan_sum(state, size, sign):
    def moved(array, step):
        return lax.ppermute(array, "ctx", [(i, i + sign * step) for i in range(size) if 0 <= i + sign * step < size])

    total, step = moved(state, 1), 1
    while step < size:
        total, step = total + moved(total, step), 2 * step
    return total


def local(queries, keys, values, out_grad):
    size = lax.axis_size("ctx")
    xfa, yfa, xfb, yfb, xga, yga, xgb, ygb, scale_low, scale_high, fa, fa_steps = load(
        *map(in_hbm, (queries, keys, values, out_grad))
    )
    swap_x = [(0, 1), (1, 0), (2, 3), (3, 2)]
    swap_y = [(0, 2), (2, 0), (1, 3), (3, 1)]
    if size == 4:
        got_xa = lax.ppermute(fa, "ctx", swap_x)
    yfb, fb, fb_steps = f_states(xfb, yfb, scale_high)
    if size == 4:
        got_y1 = lax.ppermute(fb, "ctx", swap_y)
    yga, ygb, ga_steps, gb_steps, mixed, inner_b = g_states(xga, yga, xgb, ygb, scale_low, fb)
    if size == 4:
        got_xb = lax.ppermute(mixed, "ctx", swap_x)
    o1a, o3a, o2a, o4a = local_terms(xfa, yfa, xga, yga)
    if size == 4:
        (sum_a,) = add(fa, got_xa, 1, [o4a])
        got_y2 = lax.ppermute(sum_a, "ctx", swap_y)
        sums = add(got_y1, inner_b, SPLIT, [sum_a])
        far_last = [lax.ppermute(s, "ctx", swap_x) for s in sums]
        near_a, near_b, token = got_xa, got_xb, list(sums)
        far_a, far_b = (got_y2, got_xb), got_y1
    else:
        near_a, near_b, token = scan_sum(fa, size, 1), scan_sum(fb, size, 1), []
        far_a, far_b = (scan_sum(mixed, size, -1), mixed), scan_sum(inner_b, size, -1)
        far_last = [jnp.zeros((HALF // SPLIT, XW, DV), F32)] * SPLIT
    *outs, o2b, o4b = local_near_terms(HALF, xfb, yfb, xgb, ygb, fb_steps, near_b, scale_low, token)
    outs = finish_terms(
        xfa, yfa, xga, yga, fa_steps, ga_steps, near_a, *far_a, o1a, o2a, o3a, o4a, scale_low, scale_high, outs
    )
    count = HALF // SPLIT
    for i in range(SPLIT):
        outs = far_terms(HALF, i * count, count, xfb, yfb, gb_steps, far_b, far_last[i], o2b, o4b, scale_high, outs)
    return tuple(outs)


def solution(mesh):
    spec = P(("batch", "ctx"), None)
    return jax.shard_map(local, mesh=mesh, in_specs=(spec,) * 4, out_specs=(spec,) * 4, check_vma=False)
```

time: 30.4 us -> 27.7 us (0.911)
  local copies, waits for them, and re-layouts: 1.22 us -> 0 us
  waiting for transfers between devices: 3.64 us -> 2.78 us
  Pallas kernels: 15.2 us -> 14.6 us
    ppermute x1, waiting for transfers between devices: 3.63 us -> 1.47 us  [local(): got_xa = lax.ppermute(fa, 'ctx', swap_x)]
    ppermute x1, waiting for transfers between devices: 0.01 us -> 1.3 us  [local(): got_xb = lax.ppermute(mixed, 'ctx', swap_x)]
    unnamed x2 -> x0, local copies, waits for them, and re-layouts: 1.22 us -> none
    pallas_call x7, Pallas kernels: 10.7 us -> 10.1 us  [the longest x1 3.46 us: local_near_terms(): pl.pallas_call(functools.partial(local_kernel, first, True), in_specs=[VM...]
  transfers between devices with their start and end apart: 6 -> 6, of which waited for: 1 -> 2; matrix products, arithmetic and copies ran while one was open for 0% -> 0% of each run, Pallas kernels for 36% -> 38%
where the time goes in v3:
time: 27.7 us; the launch traced here: 27.5 us
  Pallas kernels  14.6 us (53%)
  starting transfers between devices  9.44 us (34%)
  waiting for transfers between devices  2.78 us (10%)
  between operations  0.72 us (3%)
    pallas_call x1, Pallas kernels, local_near_terms(): pl.pallas_call(functools.partial(local_kernel, first, True), in_specs=[VM...  3.46 us
    pallas_call x1, Pallas kernels, load(): pl.pallas_call(load_kernel, in_specs=[HBM] * 4, out_specs=[VMEM] * 12, ou...  3.1 us
    ppermute x1, starting transfers between devices, local(): got_xa = lax.ppermute(fa, 'ctx', swap_x)  3 us
    pallas_call x2, Pallas kernels, far_terms(): pl.pallas_call(functools.partial(far_kernel, first, offset, count), in_sp...  2.28 us
    pallas_call x1, Pallas kernels, finish_terms(): pl.pallas_call(finish_kernel, in_specs=[VMEM] * len(ins) + [HBM] * 4, out...  2.21 us
    ppermute x1, starting transfers between devices, local(): got_y2 = lax.ppermute(sum_a, 'ctx', swap_y)  2.16 us
    pallas_call x1, Pallas kernels, local_terms(): pl.pallas_call(functools.partial(local_kernel, 0, False), in_specs=[VMEM]...  2.12 us
    ppermute x2, starting transfers between devices, local(): far_last = [lax.ppermute(s, 'ctx', swap_x) for s in sums]  2.09 us
  transfers between devices with their start and end apart: 6, of which 2 were waited for; matrix products, arithmetic and copies ran while one was open for 0% of the time, Pallas kernels for 38%

profile of v3, /device:TPU:0, one launch (start us, length us, event | category | flops | bytes accessed | tf_op | source)
XLA Modules:
  0.0 27.5 jit_solution(17027831739883536947)
XLA Ops:
  0.6 3.1 %load.1 = (bf16[512,512]{1,0:T(8,128)(2,1)S(1)}, bf16[512,1024]{1,0:T(8,128)(2,1)S(1)}, bf16[512,512]{1,0:T(8,128)(2,1)S(1)}, bf16[512,1024]{1,0:T(8,128)(2,1)S(...) custom-call(bf16[512,1024]{1,0:T(8,128)(2,1)} %q.1, ...), custom_call_target="tpu_custom_call" | custom-call | tf_op jit(solution)/shard_map/load/pallas_call | solution.py:173
  3.7 3.0 %collective-permute-start.1 = (f32[4,128,128]{2,1,0:T(8,128)S(1)}, f32[4,128,128]{2,1,0:T(8,128)S(1)}, u32[]{:S(2)}, u32[]{:S(2)}) collective-permute-start(f32[4,128,128]{2,1,0:T(8,128)S(1)} %get-tuple-element.57.a), channel_id=1, source_target_pairs={{0,1},{1,0},{2,3},{3,2},{4,5},{5,4},{6,7},{7,6},{8,9},{9,8},{10,11... | collective-permute-start | bytes 786440 | tf_op jit(solution)/shard_map/ppermute | solution.py:470
  6.7 0.5 %f_states.1 = (bf16[512,1024]{1,0:T(8,128)(2,1)S(1)}, f32[4,128,128]{2,1,0:T(8,128)S(1)}, f32[4,4,128,128]{3,2,1,0:T(8,128)S(1)}) custom-call(bf16[512,512]{1,0:T(8,128)(2,1)S(1)} %get-tuple-element.45.x.xf, bf16[512,1024]{1,0:T(8,128)(2,1)S(1)} %get-tuple-element.46.y, f32[512,128]{1,0:T(8,128)S(1)} %get-tuple-element.47.scale.scale_high), custom_call_target="tpu_custom_call" | custom-call | tf_op jit(solution)/shard_map/f_states/pallas_call | solution.py:192
  7.2 1.6 %collective-permute-start = (f32[4,128,128]{2,1,0:T(8,128)S(1)}, f32[4,128,128]{2,1,0:T(8,128)S(1)}, u32[]{:S(2)}, u32[]{:S(2)}) collective-permute-start(f32[4,128,128]{2,1,0:T(8,128)S(1)} %get-tuple-element.54.fb), channel_id=1, source_target_pairs={{0,2},{2,0},{1,3},{3,1},{4,6},{6,4},{5,7},{7,5},{8,10},{10,8},{9,1... | collective-permute-start | bytes 786440 | tf_op jit(solution)/shard_map/ppermute | solution.py:473
  8.8 0.9 %g_states.1 = (bf16[512,1024]{1,0:T(8,128)(2,1)S(1)}, bf16[512,1024]{1,0:T(8,128)(2,1)S(1)}, f32[4,4,128,128]{3,2,1,0:T(8,128)S(1)}, f32[4,4,128,128]{3,2,1,0:T(...) custom-call(bf16[512,512]{1,0:T(8,128)(2,1)S(1)} %get-tuple-element.49.xa.xg, ...), custom_call_target="tpu_custom_call" | custom-call | tf_op jit(solution)/shard_map/g_states/pallas_call | solution.py:216
  9.7 0.6 %collective-permute-start.3 = (f32[4,128,128]{2,1,0:T(8,128)S(1)}, f32[4,128,128]{2,1,0:T(8,128)S(1)}, u32[]{:S(2)}, u32[]{:S(2)}) collective-permute-start(f32[4,128,128]{2,1,0:T(8,128)S(1)} %get-tuple-element.65), channel_id=1, source_target_pairs={{0,1},{1,0},{2,3},{3,2},{4,5},{5,4},{6,7},{7,6},{8,9},{9,8},{10,11... | collective-permute-start | bytes 786440 | tf_op jit(solution)/shard_map/ppermute | solution.py:476
  10.3 2.1 %local.1 = (f32[512,1024]{1,0:T(8,128)S(1)}, f32[512,512]{1,0:T(8,128)S(1)}, f32[512,1024]{1,0:T(8,128)S(1)}, f32[512,512]{1,0:T(8,128)S(1)}) custom-call(bf16[512,512]{1,0:T(8,128)(2,1)S(1)} %get-tuple-element.58.xf, bf16[512,1024]{1,0:T(8,128)(2,1)S(1)} %get-tuple-element.59.yf, bf16[512,512]{1,0:T(8,128)(2,1)S(1)} %get-tuple-element.49.xa.xg, ...), custom_call_target="tpu_custom_call" | custom-call | tf_op jit(solution)/shard_map/local/pallas_call | solution.py:346
  12.4 1.5 %collective-permute-done.1.b.near = f32[4,128,128]{2,1,0:T(8,128)S(1)} collective-permute-done((f32[4,128,128]{2,1,0:T(8,128)S(1)}, f32[4,128,128]{2,1,0:T(8,128)S(1)}, u32[]{:S(2)}, u32[]{:S(2)}) %collective-permute-start.1) | collective-permute-done | bytes 262176 | tf_op jit(solution)/shard_map/ppermute | solution.py:470
  13.9 2.2 %collective-permute-start.5 = (f32[4,128,128]{2,1,0:T(8,128)S(1)}, f32[4,128,128]{2,1,0:T(8,128)S(1)}, u32[]{:S(2)}, u32[]{:S(2)}) collective-permute-start(f32[4,128,128]{2,1,0:T(8,128)S(1)} %add.2.refs_0_), channel_id=1, source_target_pairs={{0,2},{2,0},{1,3},{3,1},{4,6},{6,4},{5,7},{7,5},{8,10},{10,8},{9,1... | collective-permute-start | bytes 786440 | tf_op jit(solution)/shard_map/ppermute | solution.py:480
  16.1 0.0 collective-permute-done.a.far1
  16.1 1.6 %collective-permute-start.4 = (f32[2,128,128]{2,1,0:T(8,128)S(1)}, f32[2,128,128]{2,1,0:T(8,128)S(1)}, u32[]{:S(2)}, u32[]{:S(2)}) collective-permute-start(f32[2,128,128]{2,1,0:T(8,128)S(1)} %get-tuple-element.66.refs_3_), channel_id=1, source_target_pairs={{0,1},{1,0},{2,3},{3,2},{4,5},{5,4},{6,7},{7,6},{8,9},{9,8},{10,11... | collective-permute-start | bytes 393224 | tf_op jit(solution)/shard_map/ppermute | solution.py:482
  17.7 0.5 %collective-permute-start.2 = (f32[2,128,128]{2,1,0:T(8,128)S(1)}, f32[2,128,128]{2,1,0:T(8,128)S(1)}, u32[]{:S(2)}, u32[]{:S(2)}) collective-permute-start(f32[2,128,128]{2,1,0:T(8,128)S(1)} %get-tuple-element.62.refs_4_), channel_id=1, source_target_pairs={{0,1},{1,0},{2,3},{3,2},{4,5},{5,4},{6,7},{7,6},{8,9},{9,8},{10,11... | collective-permute-start | bytes 393224 | tf_op jit(solution)/shard_map/ppermute | solution.py:482
  18.2 1.3 %collective-permute-done.3.refs_1_.far2 = f32[4,128,128]{2,1,0:T(8,128)S(1)} collective-permute-done((f32[4,128,128]{2,1,0:T(8,128)S(1)}, f32[4,128,128]{2,1,0:T(8,128)S(1)}, u32[]{:S(2)}, u32[]{:S(2)}) %collective-permute-start.3) | collective-permute-done | bytes 262176 | tf_op jit(solution)/shard_map/ppermute | solution.py:476
  19.5 3.5 %local_near.1 = (bf16[512,2048]{1,0:T(8,128)(2,1)}, bf16[512,1024]{1,0:T(8,128)(2,1)}, bf16[512,1024]{1,0:T(8,128)(2,1)}, bf16[512,2048]{1,0:T(8,128)(2,1)}, f32...) custom-call(bf16[512,512]{1,0:T(8,128)(2,1)S(1)} %get-tuple-element.45.x.xf, bf16[512,1024]{1,0:T(8,128)(2,1)S(1)} %get-tuple-element.48.yf, ...), custom_call_target="tpu_custom_call" | custom-call | tf_op jit(solution)/shard_map/local_near/pallas_call | solution.py:358
  23.0 0.0 collective-permute-done.5.far1
  23.0 2.2 %finish.1 = (bf16[512,2048]{1,0:T(8,128)(2,1)}, bf16[512,1024]{1,0:T(8,128)(2,1)}, bf16[512,1024]{1,0:T(8,128)(2,1)}, bf16[512,2048]{1,0:T(8,128)(2,1)}) custom-call(bf16[512,512]{1,0:T(8,128)(2,1)S(1)} %get-tuple-element.58.xf, ...), custom_call_target="tpu_custom_call", output_to_operand_aliasing={{0}: (15, {}), {1}: (16, {}), {2}: (17, {}), {3}: (18, {})} | custom-call | tf_op jit(solution)/shard_map/finish/pallas_call | solution.py:409
  25.2 0.0 collective-permute-done.4.far2
  25.2 1.1 %far.2 = (bf16[512,2048]{1,0:T(8,128)(2,1)}, bf16[512,1024]{1,0:T(8,128)(2,1)}, bf16[512,1024]{1,0:T(8,128)(2,1)}, bf16[512,2048]{1,0:T(8,128)(2,1)}) custom-call(bf16[512,512]{1,0:T(8,128)(2,1)S(1)} %get-tuple-element.45.x.xf, ...), custom_call_target="tpu_custom_call", output_to_operand_aliasing={{0}: (8, {}), {1}: (9, {}), {2}: (10, {}), {3}: (11, {})} | custom-call | tf_op jit(solution)/shard_map/far/pallas_call | solution.py:440
  26.4 0.0 collective-permute-done.2.far2
  26.4 1.1 %far.3 = (bf16[512,2048]{1,0:T(8,128)(2,1)}, bf16[512,1024]{1,0:T(8,128)(2,1)}, bf16[512,1024]{1,0:T(8,128)(2,1)}, bf16[512,2048]{1,0:T(8,128)(2,1)}) custom-call(bf16[512,512]{1,0:T(8,128)(2,1)S(1)} %get-tuple-element.45.x.xf, ...), custom_call_target="tpu_custom_call", output_to_operand_aliasing={{0}: (8, {}), {1}: (9, {}), {2}: (10, {}), {3}: (11, {})} | custom-call | tf_op jit(solution)/shard_map/far/pallas_call | solution.py:440
  (2 shorter events, 0.1 us)
Async XLA Ops:
  3.7 10.1 %collective-permute-start.1 = (f32[4,128,128]{2,1,0:T(8,128)S(1)}, f32[4,128,128]{2,1,0:T(8,128)S(1)}, u32[]{:S(2)}, u32[]{:S(2)}) collective-permute-start(f32[4,128,128]{2,1,0:T(8,128)S(1)} %get-tuple-element.57.a), channel_id=1, source_target_pairs={{0,1},{1,0},{2,3},{3,2},{4,5},{5,4},{6,7},{7,6},{8,9},{9,8},{10,11... | collective-permute-start | bytes 786440 | tf_op jit(solution)/shard_map/ppermute | solution.py:470
  7.2 8.8 %collective-permute-start = (f32[4,128,128]{2,1,0:T(8,128)S(1)}, f32[4,128,128]{2,1,0:T(8,128)S(1)}, u32[]{:S(2)}, u32[]{:S(2)}) collective-permute-start(f32[4,128,128]{2,1,0:T(8,128)S(1)} %get-tuple-element.54.fb), channel_id=1, source_target_pairs={{0,2},{2,0},{1,3},{3,1},{4,6},{6,4},{5,7},{7,5},{8,10},{10,8},{9,1... | collective-permute-start | bytes 786440 | tf_op jit(solution)/shard_map/ppermute | solution.py:473
  9.7 9.8 %collective-permute-start.3 = (f32[4,128,128]{2,1,0:T(8,128)S(1)}, f32[4,128,128]{2,1,0:T(8,128)S(1)}, u32[]{:S(2)}, u32[]{:S(2)}) collective-permute-start(f32[4,128,128]{2,1,0:T(8,128)S(1)} %get-tuple-element.65), channel_id=1, source_target_pairs={{0,1},{1,0},{2,3},{3,2},{4,5},{5,4},{6,7},{7,6},{8,9},{9,8},{10,11... | collective-permute-start | bytes 786440 | tf_op jit(solution)/shard_map/ppermute | solution.py:476
  13.9 9.1 %collective-permute-start.5 = (f32[4,128,128]{2,1,0:T(8,128)S(1)}, f32[4,128,128]{2,1,0:T(8,128)S(1)}, u32[]{:S(2)}, u32[]{:S(2)}) collective-permute-start(f32[4,128,128]{2,1,0:T(8,128)S(1)} %add.2.refs_0_), channel_id=1, source_target_pairs={{0,2},{2,0},{1,3},{3,1},{4,6},{6,4},{5,7},{7,5},{8,10},{10,8},{9,1... | collective-permute-start | bytes 786440 | tf_op jit(solution)/shard_map/ppermute | solution.py:480
  16.1 9.1 %collective-permute-start.4 = (f32[2,128,128]{2,1,0:T(8,128)S(1)}, f32[2,128,128]{2,1,0:T(8,128)S(1)}, u32[]{:S(2)}, u32[]{:S(2)}) collective-permute-start(f32[2,128,128]{2,1,0:T(8,128)S(1)} %get-tuple-element.66.refs_3_), channel_id=1, source_target_pairs={{0,1},{1,0},{2,3},{3,2},{4,5},{5,4},{6,7},{7,6},{8,9},{9,8},{10,11... | collective-permute-start | bytes 393224 | tf_op jit(solution)/shard_map/ppermute | solution.py:482
  17.7 8.7 %collective-permute-start.2 = (f32[2,128,128]{2,1,0:T(8,128)S(1)}, f32[2,128,128]{2,1,0:T(8,128)S(1)}, u32[]{:S(2)}, u32[]{:S(2)}) collective-permute-start(f32[2,128,128]{2,1,0:T(8,128)S(1)} %get-tuple-element.62.refs_4_), channel_id=1, source_target_pairs={{0,1},{1,0},{2,3},{3,2},{4,5},{5,4},{6,7},{7,6},{8,9},{9,8},{10,11... | collective-permute-start | bytes 393224 | tf_op jit(solution)/shard_map/ppermute | solution.py:482

commit v4 on v3

v4 whole, which is shorter than its diff:
```python
import functools
import typing

import jax
import jax.numpy as jnp
from jax import lax
from jax.experimental import pallas as pl
from jax.experimental.pallas import tpu as pltpu
from jax.sharding import PartitionSpec as P


H = 16
DK = 64
DV = 128
PAIRS = H // 2
HALF = PAIRS // 2
XW = 2 * DK
YW = 2 * DV
CHUNK = 128
CUTS = ((0, 3), (3, 4))
VMEM_LIMIT = 12 * 1024 * 1024

NN = (((1,), (0,)), ((), ()))
NT = (((1,), (1,)), ((), ()))
TN = (((0,), (0,)), ((), ()))
F32 = jnp.float32
BF16 = jnp.bfloat16

HBM = pl.BlockSpec(memory_space=pltpu.HBM)
VMEM = pl.BlockSpec(memory_space=pltpu.VMEM)


def dot(a, b, dims=NN):
    return lax.dot_general(a, b, dims, preferred_element_type=F32)


def is_low():
    size = lax.axis_size("ctx")
    return lax.axis_index("ctx") < (size // 2 if size == 4 else size)


def is_inner():
    at = lax.axis_index("ctx")
    return (at == 1) | (at == 2) if lax.axis_size("ctx") == 4 else at >= 0


def in_vmem(array):
    return pltpu.with_memory_space_constraint(array, pltpu.VMEM)


def in_hbm(array):
    return pltpu.with_memory_space_constraint(array, pltpu.HBM)


def x_shape(length, dtype=BF16):
    return pltpu.VMEM((length, HALF * XW), dtype)


def y_shape(length, dtype=BF16):
    return pltpu.VMEM((length, HALF * YW), dtype)


STATE = pltpu.VMEM((HALF, XW, DV), F32)


def steps_shape(length):
    return pltpu.VMEM((HALF, length // CHUNK, XW, DV), F32)


def params():
    return pltpu.CompilerParams(vmem_limit_bytes=VMEM_LIMIT)


def diagonal(square):
    return jnp.concatenate([square[:DK, :DV], square[DK:, DV:]], axis=0)


def xs(p):
    return slice(p * XW, (p + 1) * XW)


def ys(p):
    return slice(p * YW, (p + 1) * YW)


def chunks_of(array):
    return [slice(c, c + CHUNK) for c in range(0, array.shape[0], CHUNK)]


def twice(scale):
    return jnp.concatenate([scale, scale], axis=1)


def chunk_states(x, y, scaled, scale, rows):
    s = twice(scale[rows, :])
    states = []
    for p in range(HALF):
        new = (y[rows, ys(p)].astype(F32) * s).astype(BF16)
        scaled[rows, ys(p)] = new
        states.append(diagonal(dot(x[rows, xs(p)], new, TN)))
    return states


def block_states(parts, backward, steps):
    count = len(parts)
    states = []
    for p in range(HALF):
        zero = jnp.zeros_like(parts[0][p])
        before, after = [zero], [zero]
        for c in range(count - 1):
            before.append(before[-1] + parts[c][p])
            after.append(after[-1] + parts[count - 1 - c][p])
        for c in range(count):
            steps[p, c] = jnp.where(backward, after[count - 1 - c], before[c])
        states.append(before[-1] + parts[-1][p])
    return states


def half_copies(a, b, x, y, half, sems):
    wide, narrow = pl.ds(half * HALF * YW, HALF * YW), pl.ds(half * HALF * XW, HALF * XW)
    return [
        (
            pltpu.make_async_copy(a.at[rows, narrow], x.at[rows, :], sems.at[0, c]),
            pltpu.make_async_copy(b.at[rows, wide], y.at[rows, :], sems.at[1, c]),
        )
        for c, rows in enumerate(chunks_of(a))
    ]


def start_all(chunks):
    for pair in chunks:
        for copy in pair:
            copy.start()


def arrived_states(copies, x, y, scaled, scale, state, steps):
    parts = []
    for rows, pair in zip(chunks_of(x), copies):
        for copy in pair:
            copy.wait()
        parts.append(chunk_states(x, y, scaled, scale, rows))
    for p, new in enumerate(block_states(parts, jnp.logical_not(is_low()), steps)):
        state[p] = new


def load_kernel(q, k, v, do, x, y, scale_low, scale_high, state, steps, raw, sems):
    low = is_low()
    length = q.shape[0]

    @pl.when(low)
    def _():
        start_all(half_copies(k, v, x, raw, 0, sems))

    @pl.when(jnp.logical_not(low))
    def _():
        start_all(half_copies(q, do, x, raw, 0, sems))

    at = lax.axis_index("ctx") * length + lax.broadcasted_iota(jnp.int32, (length, DV), 0)
    scale = 1.0 / jnp.sqrt(DK * (at.astype(F32) + 1.0))
    scale_low[...] = jnp.where(low, scale, 1.0)
    scale_high[...] = jnp.where(low, 1.0, scale)
    arrived_states(half_copies(k, v, x, raw, 0, sems), x, raw, y, scale_high, state, steps)


def load(q, k, v, do):
    length = q.shape[0]
    scale = pltpu.VMEM((length, DV), F32)
    return pl.pallas_call(
        load_kernel,
        in_specs=[HBM] * 4,
        out_specs=[VMEM] * 6,
        out_shape=[x_shape(length), y_shape(length), scale, scale, STATE, steps_shape(length)],
        scratch_shapes=[y_shape(length), pltpu.SemaphoreType.DMA((2, length // CHUNK))],
        compiler_params=params(),
        name="load",
    )(q, k, v, do)


def rest_kernel(q, k, v, do, scale, xfb, yfb, xga, yga, xgb, ygb, state, steps, raw, sems):
    def start(f, g):
        start_all(half_copies(*f, xfb, raw, 1, sems.at[0]))
        start_all(half_copies(*g, xga, yga, 0, sems.at[1]))
        start_all(half_copies(*g, xgb, ygb, 1, sems.at[2]))

    low = is_low()

    @pl.when(low)
    def _():
        start((k, v), (q, do))

    @pl.when(jnp.logical_not(low))
    def _():
        start((q, do), (k, v))

    arrived_states(half_copies(k, v, xfb, raw, 1, sems.at[0]), xfb, raw, yfb, scale, state, steps)
    for x, y, half in ((xga, yga, 0), (xgb, ygb, 1)):
        for pair in half_copies(k, v, x, y, half, sems.at[half + 1]):
            for copy in pair:
                copy.wait()


def rest(q, k, v, do, scale):
    length = q.shape[0]
    x, y = x_shape(length), y_shape(length)
    return pl.pallas_call(
        rest_kernel,
        in_specs=[HBM] * 4 + [VMEM],
        out_specs=[VMEM] * 8,
        out_shape=[x, y, x, y, x, y, STATE, steps_shape(length)],
        scratch_shapes=[y, pltpu.SemaphoreType.DMA((3, 2, length // CHUNK))],
        compiler_params=params(),
        name="rest",
    )(q, k, v, do, in_vmem(scale))


def g_kernel(xa, ya, xb, yb, scale, fb, scaled_a, scaled_b, steps_a, steps_b, mixed, inner_b):
    low = is_low()
    inner = is_inner()
    parts = [chunk_states(xa, ya, scaled_a, scale, rows) for rows in chunks_of(xa)]
    for p, new in enumerate(block_states(parts, low, steps_a)):
        mixed[p] = jnp.where(inner, new, fb[p])
    parts = [chunk_states(xb, yb, scaled_b, scale, rows) for rows in chunks_of(xb)]
    for p, new in enumerate(block_states(parts, low, steps_b)):
        inner_b[p] = jnp.where(inner, new, 0.0)


def g_states(xa, ya, xb, yb, scale, fb):
    length = xa.shape[0]
    y, steps = y_shape(length), steps_shape(length)
    return pl.pallas_call(
        g_kernel,
        in_specs=[VMEM] * 6,
        out_specs=[VMEM] * 6,
        out_shape=[y, y, steps, steps, STATE, STATE],
        compiler_params=params(),
        name="g_states",
    )(*map(in_vmem, (xa, ya, xb, yb, scale, fb)))


def add_kernel(cuts, a, b, *refs):
    for (start, stop), out in zip(cuts, refs[-len(cuts) :]):
        for p in range(start, stop):
            out[p - start] = a[p] + b[p]


def add(a, b, cuts, after=()):
    return pl.pallas_call(
        functools.partial(add_kernel, cuts),
        in_specs=[VMEM] * (2 + len(after)),
        out_specs=[VMEM] * len(cuts),
        out_shape=[pltpu.VMEM((stop - start, XW, DV), F32) for start, stop in cuts],
        compiler_params=params(),
        name="add",
    )(a, b, *map(in_vmem, after))


def head_rows(x):
    lane = lax.broadcasted_iota(jnp.int32, x.shape, 1)
    zero = jnp.zeros_like(x)
    return jnp.concatenate([jnp.where(lane < DK, x, zero), jnp.where(lane >= DK, x, zero)], axis=0)


def head_blocks(y):
    zero = jnp.zeros_like(y[:, :DV])
    top = jnp.concatenate([y[:, :DV], zero], axis=1)
    return jnp.concatenate([top, jnp.concatenate([zero, y[:, DV:]], axis=1)], axis=0)


def state_blocks(state):
    row = lax.broadcasted_iota(jnp.int32, state.shape, 0)
    zero = jnp.zeros_like(state)
    both = jnp.concatenate([jnp.where(row < DK, state, zero), jnp.where(row >= DK, state, zero)], axis=1)
    return both.astype(BF16)


def turned(scores):
    return jnp.concatenate([scores[:, :CHUNK].T, scores[:, CHUNK:].T], axis=1)


def out_copies(staged, at, when_low, when_high, pair, width, sem):
    source = staged.at[:, pl.ds(at * width, width)]
    columns = pl.ds(pair * width, width)
    return [pltpu.make_async_copy(source, target.at[:, columns], sem.at[at]) for target in (when_low, when_high)]


def send(copies, low):
    @pl.when(low)
    def _():
        copies[0].start()

    @pl.when(jnp.logical_not(low))
    def _():
        copies[1].start()


def local_kernel(start, stop, xf, yf, xg, yg, *refs):
    low = is_low()
    o1, o3, o2, o4 = refs[-4:]
    row = lax.broadcasted_iota(jnp.int32, (CHUNK, 2 * CHUNK), 0)
    col = lax.rem(lax.broadcasted_iota(jnp.int32, (CHUNK, 2 * CHUNK), 1), CHUNK)
    keep = jnp.where(low, row - col, col - row) >= 0
    chunks = chunks_of(xf)
    for p in range(start, stop):
        parts, scores = [], []
        for rows in chunks:
            x1, y1, x2, y2 = xf[rows, xs(p)], yf[rows, ys(p)], xg[rows, xs(p)], yg[rows, ys(p)]
            parts.append((head_rows(x1), head_blocks(y1), x2, y2))
        for x1s, y1s, x2, y2 in parts:
            m = jnp.where(keep, dot(x2, x1s, NT), 0.0).astype(BF16)
            n = jnp.where(keep, dot(y2, y1s, NT), 0.0).astype(BF16)
            scores.append((m, n))
        wide, narrow = ys(p - start), xs(p - start)
        for rows, (x1s, y1s, x2, y2), (m, n) in zip(chunks, parts, scores):
            o1[rows, wide] = dot(m, y1s)
            o3[rows, narrow] = dot(n, x1s)
            o2[rows, wide] = dot(turned(m), head_blocks(y2))
            o4[rows, narrow] = dot(turned(n), head_rows(x2))


def local_terms(start, stop, arrays, after=()):
    length = arrays[0].shape[0]
    wide = pltpu.VMEM((length, (stop - start) * YW), F32)
    narrow = pltpu.VMEM((length, (stop - start) * XW), F32)
    return pl.pallas_call(
        functools.partial(local_kernel, start, stop),
        in_specs=[VMEM] * (4 + len(after)),
        out_specs=[VMEM] * 4,
        out_shape=[wide, narrow, wide, narrow],
        compiler_params=params(),
        name="local",
    )(*map(in_vmem, (*arrays, *after)))


class Job(typing.NamedTuple):
    arrays: tuple
    at: int
    part: int
    second: int
    pair: int


def cross_kernel(places, near, scale_at, *refs):
    att, qg, kg, vg, wide_out, narrow_out, wide_sem, narrow_sem = refs[-8:]
    low = is_low()
    inner = is_inner()
    scale = refs[scale_at]
    started = []
    for i, (where, at, part, second, pair) in enumerate(places):
        x, y, steps, wide, narrow, *terms = [refs[w] for w in where]
        base = terms[0][at]
        if near:
            base = jnp.where(inner, base, 0.0)
        elif len(terms) > 1:
            base = base + (jnp.where(inner, 0.0, terms[1][at]) if second < 0 else terms[1][second])
        chunks = chunks_of(x)
        blocks = [state_blocks(base + steps[at, c]) for c in range(len(chunks))]
        a = [dot(x[rows, xs(at)], b) for rows, b in zip(chunks, blocks)]
        b = [dot(y[rows, ys(at)], b, NT) for rows, b in zip(chunks, blocks)]
        targets = (att, vg, qg, kg) if near else (vg, att, kg, qg)
        to_wide = out_copies(wide_out, i, targets[0], targets[1], pair, YW, wide_sem)
        to_narrow = out_copies(narrow_out, i, targets[2], targets[3], pair, XW, narrow_sem)
        for rows, new in zip(chunks, a):
            wide_out[rows, ys(i)] = ((wide[rows, ys(part)] + new) * twice(scale[rows, :])).astype(BF16)
        send(to_wide, low)
        for rows, new in zip(chunks, b):
            narrow_out[rows, xs(i)] = (narrow[rows, xs(part)] + new).astype(BF16)
        send(to_narrow, low)
        started += [to_wide[0], to_narrow[0]]
    for copy in started:
        copy.wait()


def cross_terms(jobs, near, scale, outs, received):
    arrays = []

    def place(array):
        for i, other in enumerate(arrays):
            if other is array:
                return i
        arrays.append(array)
        return len(arrays) - 1

    scale_at = place(scale)
    places = [(tuple(map(place, job.arrays)), *job[1:]) for job in jobs]
    length = scale.shape[0]
    ins = [a if any(a is r for r in received) else in_vmem(a) for a in arrays]
    count = len(jobs)
    return pl.pallas_call(
        functools.partial(cross_kernel, places, near, scale_at),
        in_specs=[VMEM] * len(ins) + [HBM] * len(outs),
        out_specs=[HBM] * 4,
        out_shape=[
            jax.ShapeDtypeStruct((length, H * DV), BF16),
            jax.ShapeDtypeStruct((length, H * DK), BF16),
            jax.ShapeDtypeStruct((length, H * DK), BF16),
            jax.ShapeDtypeStruct((length, H * DV), BF16),
        ],
        input_output_aliases={len(ins) + i: i for i in range(len(outs))},
        scratch_shapes=[
            pltpu.VMEM((length, count * YW), BF16),
            pltpu.VMEM((length, count * XW), BF16),
            pltpu.SemaphoreType.DMA((count,)),
            pltpu.SemaphoreType.DMA((count,)),
        ],
        compiler_params=params(),
        name="near" if near else "far",
    )(*ins, *outs)


def scan_sum(state, size, sign):
    def moved(array, step):
        return lax.ppermute(array, "ctx", [(i, i + sign * step) for i in range(size) if 0 <= i + sign * step < size])

    total, step = moved(state, 1), 1
    while step < size:
        total, step = total + moved(total, step), 2 * step
    return total


def local(queries, keys, values, out_grad):
    size = lax.axis_size("ctx")
    args = list(map(in_hbm, (queries, keys, values, out_grad)))
    swap_x = [(0, 1), (1, 0), (2, 3), (3, 2)]
    swap_y = [(0, 2), (2, 0), (1, 3), (3, 1)]
    xfa, yfa, scale_low, scale_high, fa, fa_steps = load(*args)
    if size == 4:
        got_xa = lax.ppermute(fa, "ctx", swap_x)
    xfb, yfb, xga, yga, xgb, ygb, fb, fb_steps = rest(*args, scale_high)
    if size == 4:
        got_y1 = lax.ppermute(fb, "ctx", swap_y)
    yga, ygb, ga_steps, gb_steps, mixed, inner_b = g_states(xga, yga, xgb, ygb, scale_low, fb)
    if size == 4:
        got_xb = lax.ppermute(mixed, "ctx", swap_x)
    half_a, half_b = (xfa, yfa, xga, yga), (xfb, yfb, xgb, ygb)
    part_a = local_terms(0, HALF, half_a)
    if size == 4:
        (sum_a,) = add(fa, got_xa, [(0, HALF)], [part_a[0]])
        got_y2 = lax.ppermute(sum_a, "ctx", swap_y)
        after = [sum_a]
    else:
        after = []
    parts_b = [local_terms(*CUTS[0], half_b, after)]
    if size == 4:
        sums = add(got_y1, inner_b, CUTS, [parts_b[0][0]])
        far_last = [lax.ppermute(s, "ctx", swap_x) for s in sums]
        near_a, near_b = got_xa, got_xb
        far_a, far_b = (got_y2, got_xb), got_y1
        after = list(sums)
    else:
        near_a, near_b = scan_sum(fa, size, 1), scan_sum(fb, size, 1)
        far_a, far_b = (scan_sum(mixed, size, -1),), scan_sum(inner_b, size, -1)
    parts_b += [local_terms(*cut, half_b, after) for cut in CUTS[1:]]
    received = (near_a, near_b, *far_a, far_b)
    places = [(cut, p) for cut in range(len(CUTS)) for p in range(*CUTS[cut])]
    jobs = [Job((xga, yga, fa_steps, part_a[0], part_a[1], near_a), p, p, 0, p) for p in range(HALF)]
    for cut, p in places:
        arrays = (xgb, ygb, fb_steps, parts_b[cut][0], parts_b[cut][1], near_b)
        jobs.append(Job(arrays, p, p - CUTS[cut][0], 0, HALF + p))
    outs = cross_terms(jobs, True, scale_low, [], received)
    jobs = [Job((xfa, yfa, ga_steps, part_a[2], part_a[3], *far_a), p, p, -1, p) for p in range(HALF)]
    outs = cross_terms(jobs, False, scale_high, outs, received)
    for cut, (start, stop) in enumerate(CUTS):
        last = (far_last[cut],) if size == 4 else ()
        arrays = (xfb, yfb, gb_steps, parts_b[cut][2], parts_b[cut][3], far_b, *last)
        jobs = [Job(arrays, p, p - start, p - start, HALF + p) for p in range(start, stop)]
        outs = cross_terms(jobs, False, scale_high, outs, (*received, *last))
    return tuple(outs)


def solution(mesh):
    spec = P(("batch", "ctx"), None)
    return jax.shard_map(local, mesh=mesh, in_specs=(spec,) * 4, out_specs=(spec,) * 4, check_vma=False)
```

time: 27.7 us -> 25.9 us (0.935)
  waiting for transfers between devices: 2.78 us -> 0.9 us
  Pallas kernels: 14.6 us -> 15.8 us
  starting transfers between devices: 9.44 us -> 8.25 us
    ppermute x1, waiting for transfers between devices: 1.47 us -> 0.01 us  [local(): got_xa = lax.ppermute(fa, 'ctx', swap_x)]
    ppermute x1, waiting for transfers between devices: 1.3 us -> 0.01 us  [local(): got_xb = lax.ppermute(mixed, 'ctx', swap_x)]
    pallas_call x9 -> x11, Pallas kernels: 13.7 us -> 15 us  [the longest x4 5.84 us: cross_terms(): pl.pallas_call(functools.partial(cross_kernel, places, near, scale_at), i...]
    ppermute x1, starting transfers between devices: 2.16 us -> 0.97 us  [local(): got_y2 = lax.ppermute(sum_a, 'ctx', swap_y)]
    ppermute x1, waiting for transfers between devices: 0.01 us -> 0.89 us  [local(): got_y1 = lax.ppermute(fb, 'ctx', swap_y)]
  transfers between devices with their start and end apart: 6 -> 6, of which waited for: 2 -> 1; matrix products, arithmetic and copies ran while one was open for 0% -> 0% of each run, Pallas kernels for 38% -> 49%
where the time goes in v4:
time: 25.9 us; the launch traced here: 25.7 us
  Pallas kernels  15.8 us (61%)
  starting transfers between devices  8.25 us (32%)
  waiting for transfers between devices  0.9 us (3%)
  between operations  0.75 us (3%)
    pallas_call x4, Pallas kernels, cross_terms(): pl.pallas_call(functools.partial(cross_kernel, places, near, scale_at), i...  5.84 us
    pallas_call x3, Pallas kernels, local_terms(): pl.pallas_call(functools.partial(local_kernel, start, stop), in_specs=[VM...  4.39 us
    ppermute x1, starting transfers between devices, local(): got_xa = lax.ppermute(fa, 'ctx', swap_x)  3 us
    pallas_call x1, Pallas kernels, rest(): pl.pallas_call(rest_kernel, in_specs=[HBM] * 4 + [VMEM], out_specs=[VMEM]...  2.55 us
    pallas_call x1, Pallas kernels, load(): pl.pallas_call(load_kernel, in_specs=[HBM] * 4, out_specs=[VMEM] * 6, out...  2.12 us
    ppermute x2, starting transfers between devices, local(): far_last = [lax.ppermute(s, 'ctx', swap_x) for s in sums]  2.09 us
    ppermute x1, starting transfers between devices, local(): got_y1 = lax.ppermute(fb, 'ctx', swap_y)  1.6 us
    ppermute x1, starting transfers between devices, local(): got_y2 = lax.ppermute(sum_a, 'ctx', swap_y)  0.97 us
  transfers between devices with their start and end apart: 6, of which 1 were waited for; matrix products, arithmetic and copies ran while one was open for 0% of the time, Pallas kernels for 49%

profile of v4, /device:TPU:0, one launch (start us, length us, event | category | flops | bytes accessed | tf_op | source)
XLA Modules:
  0.0 25.7 jit_solution(15807918677402115592)
XLA Ops:
  0.6 2.1 %load.1 = (bf16[512,512]{1,0:T(8,128)(2,1)S(1)}, bf16[512,1024]{1,0:T(8,128)(2,1)S(1)}, f32[512,128]{1,0:T(8,128)S(1)}, f32[512,128]{1,0:T(8,128)S(1)}, f32[4,12...) custom-call(bf16[512,1024]{1,0:T(8,128)(2,1)} %q.3, bf16[512,1024]{1,0:T(8,128)(2,1)} %k.3, bf16[512,2048]{1,0:T(8,128)(2,1)} %v.3, ...), custom_call_target="tpu_custom_call" | custom-call | tf_op jit(solution)/shard_map/load/pallas_call | solution.py:168
  2.8 3.0 %collective-permute-start.1 = (f32[4,128,128]{2,1,0:T(8,128)S(1)}, f32[4,128,128]{2,1,0:T(8,128)S(1)}, u32[]{:S(2)}, u32[]{:S(2)}) collective-permute-start(f32[4,128,128]{2,1,0:T(8,128)S(1)} %get-tuple-element.62.a), channel_id=1, source_target_pairs={{0,1},{1,0},{2,3},{3,2},{4,5},{5,4},{6,7},{7,6},{8,9},{9,8},{10,11... | collective-permute-start | bytes 786440 | tf_op jit(solution)/shard_map/ppermute | solution.py:427
  5.8 2.6 %rest.1 = (bf16[512,512]{1,0:T(8,128)(2,1)S(1)}, bf16[512,1024]{1,0:T(8,128)(2,1)S(1)}, bf16[512,512]{1,0:T(8,128)(2,1)S(1)}, bf16[512,1024]{1,0:T(8,128)(2,1)S(...) custom-call(bf16[512,1024]{1,0:T(8,128)(2,1)} %q.3, ...), custom_call_target="tpu_custom_call" | custom-call | tf_op jit(solution)/shard_map/rest/pallas_call | solution.py:205
  8.3 1.6 %collective-permute-start = (f32[4,128,128]{2,1,0:T(8,128)S(1)}, f32[4,128,128]{2,1,0:T(8,128)S(1)}, u32[]{:S(2)}, u32[]{:S(2)}) collective-permute-start(f32[4,128,128]{2,1,0:T(8,128)S(1)} %get-tuple-element.58.fb), channel_id=1, source_target_pairs={{0,2},{2,0},{1,3},{3,1},{4,6},{6,4},{5,7},{7,5},{8,10},{10,8},{9,1... | collective-permute-start | bytes 786440 | tf_op jit(solution)/shard_map/ppermute | solution.py:430
  9.9 0.9 %g_states.1 = (bf16[512,1024]{1,0:T(8,128)(2,1)S(1)}, bf16[512,1024]{1,0:T(8,128)(2,1)S(1)}, f32[4,4,128,128]{3,2,1,0:T(8,128)S(1)}, f32[4,4,128,128]{3,2,1,0:T(...) custom-call(bf16[512,512]{1,0:T(8,128)(2,1)S(1)} %get-tuple-element.53.xa.xg.refs_1_, ...), custom_call_target="tpu_custom_call" | custom-call | tf_op jit(solution)/shard_map/g_states/pallas_call | solution.py:230
  10.8 0.6 %collective-permute-start.5 = (f32[4,128,128]{2,1,0:T(8,128)S(1)}, f32[4,128,128]{2,1,0:T(8,128)S(1)}, u32[]{:S(2)}, u32[]{:S(2)}) collective-permute-start(f32[4,128,128]{2,1,0:T(8,128)S(1)} %get-tuple-element.77), channel_id=1, source_target_pairs={{0,1},{1,0},{2,3},{3,2},{4,5},{5,4},{6,7},{7,6},{8,9},{9,8},{10,11... | collective-permute-start | bytes 786440 | tf_op jit(solution)/shard_map/ppermute | solution.py:433
  11.4 2.1 %local.3 = (f32[512,1024]{1,0:T(8,128)S(1)}, f32[512,512]{1,0:T(8,128)S(1)}, f32[512,1024]{1,0:T(8,128)S(1)}, f32[512,512]{1,0:T(8,128)S(1)}) custom-call(bf16[512,512]{1,0:T(8,128)(2,1)S(1)} %get-tuple-element.63.xf.refs_1_, bf16[512,1024]{1,0:T(8,128)(2,1)S(1)} %get-tuple-element.64.yf.refs_2_, bf16[512,512]{1,0:T(8,128)(2,1)S(1)} %get-tuple-element.53.xa.xg.refs_1_, ...), custom_call_target="tpu_custom_call" | custom-call | tf_op jit(solution)/shard_map/local/pallas_call | solution.py:324
  13.5 0.0 collective-permute-done.1.b.refs_6_
  13.5 1.0 %collective-permute-start.4 = (f32[4,128,128]{2,1,0:T(8,128)S(1)}, f32[4,128,128]{2,1,0:T(8,128)S(1)}, u32[]{:S(2)}, u32[]{:S(2)}) collective-permute-start(f32[4,128,128]{2,1,0:T(8,128)S(1)} %add.2.refs_0_), channel_id=1, source_target_pairs={{0,2},{2,0},{1,3},{3,1},{4,6},{6,4},{5,7},{7,5},{8,10},{10,8},{9,1... | collective-permute-start | bytes 786440 | tf_op jit(solution)/shard_map/ppermute | solution.py:438
  14.5 1.6 %local.4 = (f32[512,768]{1,0:T(8,128)S(1)}, f32[512,384]{1,0:T(8,128)S(1)}, f32[512,768]{1,0:T(8,128)S(1)}, f32[512,384]{1,0:T(8,128)S(1)}) custom-call(bf16[512,512]{1,0:T(8,128)(2,1)S(1)} %get-tuple-element.51.xf.refs_1_, bf16[512,1024]{1,0:T(8,128)(2,1)S(1)} %get-tuple-element.52.yf.refs_2_, bf16[512,512]{1,0:T(8,128)(2,1)S(1)} %get-tuple-element.55.xb.xg.refs_7_, ...), custom_call_target="tpu_custom_call" | custom-call | tf_op jit(solution)/shard_map/local/pallas_call | solution.py:324
  16.1 0.9 %collective-permute-done.a.refs_6_ = f32[4,128,128]{2,1,0:T(8,128)S(1)} collective-permute-done((f32[4,128,128]{2,1,0:T(8,128)S(1)}, f32[4,128,128]{2,1,0:T(8,128)S(1)}, u32[]{:S(2)}, u32[]{:S(2)}) %collective-permute-start) | collective-permute-done | bytes 262176 | tf_op jit(solution)/shard_map/ppermute | solution.py:430
  17.1 1.3 %collective-permute-start.3 = (f32[3,128,128]{2,1,0:T(8,128)S(1)}, f32[3,128,128]{2,1,0:T(8,128)S(1)}, u32[]{:S(2)}, u32[]{:S(2)}) collective-permute-start(f32[3,128,128]{2,1,0:T(8,128)S(1)} %get-tuple-element.68.refs_0_), channel_id=1, source_target_pairs={{0,1},{1,0},{2,3},{3,2},{4,5},{5,4},{6,7},{7,6},{8,9},{9,8},{10,11... | collective-permute-start | bytes 589832 | tf_op jit(solution)/shard_map/ppermute | solution.py:445
  18.3 0.8 %collective-permute-start.2 = (f32[1,128,128]{2,1,0:T(8,128)S(1)}, f32[1,128,128]{2,1,0:T(8,128)S(1)}, u32[]{:S(2)}, u32[]{:S(2)}) collective-permute-start(f32[1,128,128]{2,1,0:T(8,128)S(1)} %get-tuple-element.69.refs_1_), channel_id=1, source_target_pairs={{0,1},{1,0},{2,3},{3,2},{4,5},{5,4},{6,7},{7,6},{8,9},{9,8},{10,11... | collective-permute-start | bytes 196616 | tf_op jit(solution)/shard_map/ppermute | solution.py:445
  19.2 0.6 %local.5 = (f32[512,256]{1,0:T(8,128)S(1)}, f32[512,128]{1,0:T(8,128)S(1)}, f32[512,256]{1,0:T(8,128)S(1)}, f32[512,128]{1,0:T(8,128)S(1)}) custom-call(bf16[512,512]{1,0:T(8,128)(2,1)S(1)} %get-tuple-element.51.xf.refs_1_, bf16[512,1024]{1,0:T(8,128)(2,1)S(1)} %get-tuple-element.52.yf.refs_2_, bf16[512,512]{1,0:T(8,128)(2,1)S(1)} %get-tuple-element.55.xb.xg.refs_7_, ...), custom_call_target="tpu_custom_call" | custom-call | tf_op jit(solution)/shard_map/local/pallas_call | solution.py:324
  19.8 0.0 collective-permute-done.5.refs_12_.refs_7_
  19.8 2.1 %near.1 = (bf16[512,2048]{1,0:T(8,128)(2,1)}, bf16[512,1024]{1,0:T(8,128)(2,1)}, bf16[512,1024]{1,0:T(8,128)(2,1)}, bf16[512,2048]{1,0:T(8,128)(2,1)}) custom-call(f32[512,128]{1,0:T(8,128)S(1)} %get-tuple-element.57.scale.refs_0_, bf16[512,512]{1,0:T(8,128)(2,1)S(1)} %get-tuple-element.53.xa.xg.refs_1_, bf16[512,1024]{1,0:T(8,128)(2,1)S(1)} %get-tuple-element.65.yg.refs_2_, ...), custom_call_target="tpu_custom_call" | custom-call | tf_op jit(solution)/shard_map/near/pallas_call | solution.py:388
  21.9 0.0 collective-permute-done.4.refs_6_
  21.9 1.5 %far.3 = (bf16[512,2048]{1,0:T(8,128)(2,1)}, bf16[512,1024]{1,0:T(8,128)(2,1)}, bf16[512,1024]{1,0:T(8,128)(2,1)}, bf16[512,2048]{1,0:T(8,128)(2,1)}) custom-call(f32[512,128]{1,0:T(8,128)S(1)} %get-tuple-element.50.scale.refs_0_, ...), custom_call_target="tpu_custom_call", output_to_operand_aliasing={{0}: (8, {}), {1}: (9, {}), {2}: (10, {}), {3}: (11, {})} | custom-call | tf_op jit(solution)/shard_map/far/pallas_call | solution.py:388
  23.4 0.0 collective-permute-done.3.refs_7_
  23.4 1.3 %far.4 = (bf16[512,2048]{1,0:T(8,128)(2,1)}, bf16[512,1024]{1,0:T(8,128)(2,1)}, bf16[512,1024]{1,0:T(8,128)(2,1)}, bf16[512,2048]{1,0:T(8,128)(2,1)}) custom-call(f32[512,128]{1,0:T(8,128)S(1)} %get-tuple-element.50.scale.refs_0_, ...), custom_call_target="tpu_custom_call", output_to_operand_aliasing={{0}: (8, {}), {1}: (9, {}), {2}: (10, {}), {3}: (11, {})} | custom-call | tf_op jit(solution)/shard_map/far/pallas_call | solution.py:388
  24.7 0.0 collective-permute-done.2.refs_7_
  24.7 1.0 %far.5 = (bf16[512,2048]{1,0:T(8,128)(2,1)}, bf16[512,1024]{1,0:T(8,128)(2,1)}, bf16[512,1024]{1,0:T(8,128)(2,1)}, bf16[512,2048]{1,0:T(8,128)(2,1)}) custom-call(f32[512,128]{1,0:T(8,128)S(1)} %get-tuple-element.50.scale.refs_0_, ...), custom_call_target="tpu_custom_call", output_to_operand_aliasing={{0}: (8, {}), {1}: (9, {}), {2}: (10, {}), {3}: (11, {})} | custom-call | tf_op jit(solution)/shard_map/far/pallas_call | solution.py:388
  (2 shorter events, 0.1 us)
Async XLA Ops:
  2.8 10.7 %collective-permute-start.1 = (f32[4,128,128]{2,1,0:T(8,128)S(1)}, f32[4,128,128]{2,1,0:T(8,128)S(1)}, u32[]{:S(2)}, u32[]{:S(2)}) collective-permute-start(f32[4,128,128]{2,1,0:T(8,128)S(1)} %get-tuple-element.62.a), channel_id=1, source_target_pairs={{0,1},{1,0},{2,3},{3,2},{4,5},{5,4},{6,7},{7,6},{8,9},{9,8},{10,11... | collective-permute-start | bytes 786440 | tf_op jit(solution)/shard_map/ppermute | solution.py:427
  8.3 8.7 %collective-permute-start = (f32[4,128,128]{2,1,0:T(8,128)S(1)}, f32[4,128,128]{2,1,0:T(8,128)S(1)}, u32[]{:S(2)}, u32[]{:S(2)}) collective-permute-start(f32[4,128,128]{2,1,0:T(8,128)S(1)} %get-tuple-element.58.fb), channel_id=1, source_target_pairs={{0,2},{2,0},{1,3},{3,1},{4,6},{6,4},{5,7},{7,5},{8,10},{10,8},{9,1... | collective-permute-start | bytes 786440 | tf_op jit(solution)/shard_map/ppermute | solution.py:430
  10.8 9.0 %collective-permute-start.5 = (f32[4,128,128]{2,1,0:T(8,128)S(1)}, f32[4,128,128]{2,1,0:T(8,128)S(1)}, u32[]{:S(2)}, u32[]{:S(2)}) collective-permute-start(f32[4,128,128]{2,1,0:T(8,128)S(1)} %get-tuple-element.77), channel_id=1, source_target_pairs={{0,1},{1,0},{2,3},{3,2},{4,5},{5,4},{6,7},{7,6},{8,9},{9,8},{10,11... | collective-permute-start | bytes 786440 | tf_op jit(solution)/shard_map/ppermute | solution.py:433
  13.5 8.4 %collective-permute-start.4 = (f32[4,128,128]{2,1,0:T(8,128)S(1)}, f32[4,128,128]{2,1,0:T(8,128)S(1)}, u32[]{:S(2)}, u32[]{:S(2)}) collective-permute-start(f32[4,128,128]{2,1,0:T(8,128)S(1)} %add.2.refs_0_), channel_id=1, source_target_pairs={{0,2},{2,0},{1,3},{3,1},{4,6},{6,4},{5,7},{7,5},{8,10},{10,8},{9,1... | collective-permute-start | bytes 786440 | tf_op jit(solution)/shard_map/ppermute | solution.py:438
  17.1 6.3 %collective-permute-start.3 = (f32[3,128,128]{2,1,0:T(8,128)S(1)}, f32[3,128,128]{2,1,0:T(8,128)S(1)}, u32[]{:S(2)}, u32[]{:S(2)}) collective-permute-start(f32[3,128,128]{2,1,0:T(8,128)S(1)} %get-tuple-element.68.refs_0_), channel_id=1, source_target_pairs={{0,1},{1,0},{2,3},{3,2},{4,5},{5,4},{6,7},{7,6},{8,9},{9,8},{10,11... | collective-permute-start | bytes 589832 | tf_op jit(solution)/shard_map/ppermute | solution.py:445
  18.3 6.4 %collective-permute-start.2 = (f32[1,128,128]{2,1,0:T(8,128)S(1)}, f32[1,128,128]{2,1,0:T(8,128)S(1)}, u32[]{:S(2)}, u32[]{:S(2)}) collective-permute-start(f32[1,128,128]{2,1,0:T(8,128)S(1)} %get-tuple-element.69.refs_1_), channel_id=1, source_target_pairs={{0,1},{1,0},{2,3},{3,2},{4,5},{5,4},{6,7},{7,6},{8,9},{9,8},{10,11... | collective-permute-start | bytes 196616 | tf_op jit(solution)/shard_map/ppermute | solution.py:445

commit v5 on v4

--- a/solution.py
+++ b/solution.py
@@ -17,7 +17,7 @@
 XW = 2 * DK
 YW = 2 * DV
 CHUNK = 128
-CUTS = ((0, 3), (3, 4))
+CUTS = ((0, 4),)
 VMEM_LIMIT = 12 * 1024 * 1024
 
 NN = (((1,), (0,)), ((), ()))
@@ -91,13 +91,16 @@
     return jnp.concatenate([scale, scale], axis=1)
 
 
-def chunk_states(x, y, scaled, scale, rows):
+def chunk_states(x, y, scaled, scale, rows, half=0, kept=None):
     s = twice(scale[rows, :])
     states = []
     for p in range(HALF):
-        new = (y[rows, ys(p)].astype(F32) * s).astype(BF16)
+        old = x[rows, xs(half * HALF + p)]
+        if kept is not None:
+            kept[rows, xs(p)] = old
+        new = (y[rows, ys(half * HALF + p)].astype(F32) * s).astype(BF16)
         scaled[rows, ys(p)] = new
-        states.append(diagonal(dot(x[rows, xs(p)], new, TN)))
+        states.append(diagonal(dot(old, new, TN)))
     return states
 
 
@@ -176,65 +179,65 @@
     )(q, k, v, do)
 
 
-def rest_kernel(q, k, v, do, scale, xfb, yfb, xga, yga, xgb, ygb, state, steps, raw, sems):
-    def start(f, g):
-        start_all(half_copies(*f, xfb, raw, 1, sems.at[0]))
-        start_all(half_copies(*g, xga, yga, 0, sems.at[1]))
-        start_all(half_copies(*g, xgb, ygb, 1, sems.at[2]))
-
+def either(low, work, kv, qd):
+    @pl.when(low)
+    def _():
+        work(*kv)
+
+    @pl.when(jnp.logical_not(low))
+    def _():
+        work(*qd)
+
+
+def f_kernel(q, k, v, do, scale, x, y, state, steps):
     low = is_low()
 
-    @pl.when(low)
-    def _():
-        start((k, v), (q, do))
-
-    @pl.when(jnp.logical_not(low))
-    def _():
-        start((q, do), (k, v))
-
-    arrived_states(half_copies(k, v, xfb, raw, 1, sems.at[0]), xfb, raw, yfb, scale, state, steps)
-    for x, y, half in ((xga, yga, 0), (xgb, ygb, 1)):
-        for pair in half_copies(k, v, x, y, half, sems.at[half + 1]):
-            for copy in pair:
-                copy.wait()
-
-
-def rest(q, k, v, do, scale):
+    def work(a, b):
+        parts = [chunk_states(a, b, y, scale, rows, 1, x) for rows in chunks_of(x)]
+        for p, new in enumerate(block_states(parts, jnp.logical_not(low), steps)):
+            state[p] = new
+
+    either(low, work, (k, v), (q, do))
+
+
+def f_states(q, k, v, do, scale):
     length = q.shape[0]
-    x, y = x_shape(length), y_shape(length)
-    return pl.pallas_call(
-        rest_kernel,
-        in_specs=[HBM] * 4 + [VMEM],
-        out_specs=[VMEM] * 8,
-        out_shape=[x, y, x, y, x, y, STATE, steps_shape(length)],
-        scratch_shapes=[y, pltpu.SemaphoreType.DMA((3, 2, length // CHUNK))],
-        compiler_params=params(),
-        name="rest",
-    )(q, k, v, do, in_vmem(scale))
-
-
-def g_kernel(xa, ya, xb, yb, scale, fb, scaled_a, scaled_b, steps_a, steps_b, mixed, inner_b):
+    return pl.pallas_call(
+        f_kernel,
+        in_specs=[VMEM] * 5,
+        out_specs=[VMEM] * 4,
+        out_shape=[x_shape(length), y_shape(length), STATE, steps_shape(length)],
+        compiler_params=params(),
+        name="f_states",
+    )(*map(in_vmem, (q, k, v, do, scale)))
+
+
+def g_kernel(q, k, v, do, scale, fb, xa, ya, xb, yb, steps_a, steps_b, mixed, inner_b):
     low = is_low()
     inner = is_inner()
-    parts = [chunk_states(xa, ya, scaled_a, scale, rows) for rows in chunks_of(xa)]
-    for p, new in enumerate(block_states(parts, low, steps_a)):
-        mixed[p] = jnp.where(inner, new, fb[p])
-    parts = [chunk_states(xb, yb, scaled_b, scale, rows) for rows in chunks_of(xb)]
-    for p, new in enumerate(block_states(parts, low, steps_b)):
-        inner_b[p] = jnp.where(inner, new, 0.0)
-
-
-def g_states(xa, ya, xb, yb, scale, fb):
-    length = xa.shape[0]
-    y, steps = y_shape(length), steps_shape(length)
+
+    def work(a, b):
+        parts = [chunk_states(a, b, ya, scale, rows, 0, xa) for rows in chunks_of(xa)]
+        for p, new in enumerate(block_states(parts, low, steps_a)):
+            mixed[p] = jnp.where(inner, new, fb[p])
+        parts = [chunk_states(a, b, yb, scale, rows, 1, xb) for rows in chunks_of(xb)]
+        for p, new in enumerate(block_states(parts, low, steps_b)):
+            inner_b[p] = jnp.where(inner, new, 0.0)
+
+    either(low, work, (q, do), (k, v))
+
+
+def g_states(q, k, v, do, scale, fb):
+    length = q.shape[0]
+    x, y, steps = x_shape(length), y_shape(length), steps_shape(length)
     return pl.pallas_call(
         g_kernel,
         in_specs=[VMEM] * 6,
-        out_specs=[VMEM] * 6,
-        out_shape=[y, y, steps, steps, STATE, STATE],
+        out_specs=[VMEM] * 8,
+        out_shape=[x, y, x, y, steps, steps, STATE, STATE],
         compiler_params=params(),
         name="g_states",
-    )(*map(in_vmem, (xa, ya, xb, yb, scale, fb)))
+    )(*map(in_vmem, (q, k, v, do, scale, fb)))
 
 
 def add_kernel(cuts, a, b, *refs):
@@ -293,14 +296,13 @@
         copies[1].start()
 
 
-def local_kernel(start, stop, xf, yf, xg, yg, *refs):
+def local_kernel(xf, yf, xg, yg, o1, o3, o2, o4):
     low = is_low()
-    o1, o3, o2, o4 = refs[-4:]
     row = lax.broadcasted_iota(jnp.int32, (CHUNK, 2 * CHUNK), 0)
     col = lax.rem(lax.broadcasted_iota(jnp.int32, (CHUNK, 2 * CHUNK), 1), CHUNK)
     keep = jnp.where(low, row - col, col - row) >= 0
     chunks = chunks_of(xf)
-    for p in range(start, stop):
+    for p in range(HALF):
         parts, scores = [], []
         for rows in chunks:
             x1, y1, x2, y2 = xf[rows, xs(p)], yf[rows, ys(p)], xg[rows, xs(p)], yg[rows, ys(p)]
@@ -309,32 +311,29 @@
             m = jnp.where(keep, dot(x2, x1s, NT), 0.0).astype(BF16)
             n = jnp.where(keep, dot(y2, y1s, NT), 0.0).astype(BF16)
             scores.append((m, n))
-        wide, narrow = ys(p - start), xs(p - start)
         for rows, (x1s, y1s, x2, y2), (m, n) in zip(chunks, parts, scores):
-            o1[rows, wide] = dot(m, y1s)
-            o3[rows, narrow] = dot(n, x1s)
-            o2[rows, wide] = dot(turned(m), head_blocks(y2))
-            o4[rows, narrow] = dot(turned(n), head_rows(x2))
-
-
-def local_terms(start, stop, arrays, after=()):
+            o1[rows, ys(p)] = dot(m, y1s)
+            o3[rows, xs(p)] = dot(n, x1s)
+            o2[rows, ys(p)] = dot(turned(m), head_blocks(y2))
+            o4[rows, xs(p)] = dot(turned(n), head_rows(x2))
+
+
+def local_terms(arrays):
     length = arrays[0].shape[0]
-    wide = pltpu.VMEM((length, (stop - start) * YW), F32)
-    narrow = pltpu.VMEM((length, (stop - start) * XW), F32)
-    return pl.pallas_call(
-        functools.partial(local_kernel, start, stop),
-        in_specs=[VMEM] * (4 + len(after)),
+    x, y = x_shape(length, F32), y_shape(length, F32)
+    return pl.pallas_call(
+        local_kernel,
+        in_specs=[VMEM] * 4,
         out_specs=[VMEM] * 4,
-        out_shape=[wide, narrow, wide, narrow],
+        out_shape=[y, x, y, x],
         compiler_params=params(),
         name="local",
-    )(*map(in_vmem, (*arrays, *after)))
+    )(*map(in_vmem, arrays))
 
 
 class Job(typing.NamedTuple):
     arrays: tuple
     at: int
-    part: int
     second: int
     pair: int
 
@@ -345,7 +344,7 @@
     inner = is_inner()
     scale = refs[scale_at]
     started = []
-    for i, (where, at, part, second, pair) in enumerate(places):
+    for i, (where, at, second, pair) in enumerate(places):
         x, y, steps, wide, narrow, *terms = [refs[w] for w in where]
         base = terms[0][at]
         if near:
@@ -360,17 +359,17 @@
         to_wide = out_copies(wide_out, i, targets[0], targets[1], pair, YW, wide_sem)
         to_narrow = out_copies(narrow_out, i, targets[2], targets[3], pair, XW, narrow_sem)
         for rows, new in zip(chunks, a):
-            wide_out[rows, ys(i)] = ((wide[rows, ys(part)] + new) * twice(scale[rows, :])).astype(BF16)
+            wide_out[rows, ys(i)] = ((wide[rows, ys(at)] + new) * twice(scale[rows, :])).astype(BF16)
         send(to_wide, low)
         for rows, new in zip(chunks, b):
-            narrow_out[rows, xs(i)] = (narrow[rows, xs(part)] + new).astype(BF16)
+            narrow_out[rows, xs(i)] = (narrow[rows, xs(at)] + new).astype(BF16)
         send(to_narrow, low)
         started += [to_wide[0], to_narrow[0]]
     for copy in started:
         copy.wait()
 
 
-def cross_terms(jobs, near, scale, outs, received):
+def cross_terms(jobs, near, scale, outs, received, after=()):
     arrays = []
 
     def place(array):
@@ -387,7 +386,7 @@
     count = len(jobs)
     return pl.pallas_call(
         functools.partial(cross_kernel, places, near, scale_at),
-        in_specs=[VMEM] * len(ins) + [HBM] * len(outs),
+        in_specs=[VMEM] * len(ins) + [HBM] * len(outs) + [VMEM] * len(after),
         out_specs=[HBM] * 4,
         out_shape=[
             jax.ShapeDtypeStruct((length, H * DV), BF16),
@@ -404,7 +403,7 @@
         ],
         compiler_params=params(),
         name="near" if near else "far",
-    )(*ins, *outs)
+    )(*ins, *outs, *map(in_vmem, after))
 
 
 def scan_sum(state, size, sign):
@@ -425,44 +424,37 @@
     xfa, yfa, scale_low, scale_high, fa, fa_steps = load(*args)
     if size == 4:
         got_xa = lax.ppermute(fa, "ctx", swap_x)
-    xfb, yfb, xga, yga, xgb, ygb, fb, fb_steps = rest(*args, scale_high)
+    whole = (queries, keys, values, out_grad)
+    xfb, yfb, fb, fb_steps = f_states(*whole, scale_high)
     if size == 4:
         got_y1 = lax.ppermute(fb, "ctx", swap_y)
-    yga, ygb, ga_steps, gb_steps, mixed, inner_b = g_states(xga, yga, xgb, ygb, scale_low, fb)
+    xga, yga, xgb, ygb, ga_steps, gb_steps, mixed, inner_b = g_states(*whole, scale_low, fb)
     if size == 4:
         got_xb = lax.ppermute(mixed, "ctx", swap_x)
     half_a, half_b = (xfa, yfa, xga, yga), (xfb, yfb, xgb, ygb)
-    part_a = local_terms(0, HALF, half_a)
+    part_a, part_b = local_terms(half_a), local_terms(half_b)
     if size == 4:
-        (sum_a,) = add(fa, got_xa, [(0, HALF)], [part_a[0]])
+        (sum_a,) = add(fa, got_xa, [(0, HALF)], [part_a[0], part_b[0]])
         got_y2 = lax.ppermute(sum_a, "ctx", swap_y)
-        after = [sum_a]
-    else:
-        after = []
-    parts_b = [local_terms(*CUTS[0], half_b, after)]
-    if size == 4:
-        sums = add(got_y1, inner_b, CUTS, [parts_b[0][0]])
+        sums = add(got_y1, inner_b, CUTS, [sum_a])
         far_last = [lax.ppermute(s, "ctx", swap_x) for s in sums]
         near_a, near_b = got_xa, got_xb
         far_a, far_b = (got_y2, got_xb), got_y1
-        after = list(sums)
+        after = sums
     else:
         near_a, near_b = scan_sum(fa, size, 1), scan_sum(fb, size, 1)
         far_a, far_b = (scan_sum(mixed, size, -1),), scan_sum(inner_b, size, -1)
-    parts_b += [local_terms(*cut, half_b, after) for cut in CUTS[1:]]
+        after = []
     received = (near_a, near_b, *far_a, far_b)
-    places = [(cut, p) for cut in range(len(CUTS)) for p in range(*CUTS[cut])]
-    jobs = [Job((xga, yga, fa_steps, part_a[0], part_a[1], near_a), p, p, 0, p) for p in range(HALF)]
-    for cut, p in places:
-        arrays = (xgb, ygb, fb_steps, parts_b[cut][0], parts_b[cut][1], near_b)
-        jobs.append(Job(arrays, p, p - CUTS[cut][0], 0, HALF + p))
-    outs = cross_terms(jobs, True, scale_low, [], received)
-    jobs = [Job((xfa, yfa, ga_steps, part_a[2], part_a[3], *far_a), p, p, -1, p) for p in range(HALF)]
+    jobs = [Job((xga, yga, fa_steps, part_a[0], part_a[1], near_a), p, 0, p) for p in range(HALF)]
+    jobs += [Job((xgb, ygb, fb_steps, part_b[0], part_b[1], near_b), p, 0, HALF + p) for p in range(HALF)]
+    outs = cross_terms(jobs, True, scale_low, [], received, after)
+    jobs = [Job((xfa, yfa, ga_steps, part_a[2], part_a[3], *far_a), p, -1, p) for p in range(HALF)]
     outs = cross_terms(jobs, False, scale_high, outs, received)
     for cut, (start, stop) in enumerate(CUTS):
         last = (far_last[cut],) if size == 4 else ()
-        arrays = (xfb, yfb, gb_steps, parts_b[cut][2], parts_b[cut][3], far_b, *last)
-        jobs = [Job(arrays, p, p - start, p - start, HALF + p) for p in range(start, stop)]
+        arrays = (xfb, yfb, gb_steps, part_b[2], part_b[3], far_b, *last)
+        jobs = [Job(arrays, p, p - start, HALF + p) for p in range(start, stop)]
         outs = cross_terms(jobs, False, scale_high, outs, (*received, *last))
     return tuple(outs)
 

time: 25.9 us -> 25.1 us (0.969)
  Pallas kernels: 15.8 us -> 13.2 us
  waiting for transfers between devices: 0.9 us -> 3.06 us
  starting transfers between devices: 8.25 us -> 7.95 us
    pallas_call x5 -> x4, Pallas kernels: 7.79 us -> 5.85 us  [the longest x2 4.24 us: local_terms(): pl.pallas_call(local_kernel, in_specs=[VMEM] * 4, out_specs=[VMEM] * 4, o...]
    ppermute x1, waiting for transfers between devices: 0.01 us -> 1.83 us  [local(): got_xb = lax.ppermute(mixed, 'ctx', swap_x)]
    ppermute x1, waiting for transfers between devices: 0.01 us -> 1.19 us  [local(): got_y2 = lax.ppermute(sum_a, 'ctx', swap_y)]
    ppermute x1, waiting for transfers between devices: 0.89 us -> 0.01 us  [local(): got_y1 = lax.ppermute(fb, 'ctx', swap_y)]
    pallas_call x4 -> x3, Pallas kernels: 5.84 us -> 5 us  [cross_terms(): pl.pallas_call(functools.partial(cross_kernel, places, near, scale_at), i...]
    ppermute x2 -> x1, starting transfers between devices: 2.09 us -> 1.55 us  [local(): far_last = [lax.ppermute(s, 'ctx', swap_x) for s in sums]]
    ppermute x1, starting transfers between devices: 0.59 us -> 0.96 us  [local(): got_xb = lax.ppermute(mixed, 'ctx', swap_x)]
  transfers between devices with their start and end apart: 6 -> 5, of which waited for: 1 -> 2; matrix products, arithmetic and copies ran while one was open for 0% -> 0% of each run, Pallas kernels for 49% -> 38%
where the time goes in v5:
time: 25.1 us; the launch traced here: 24.9 us
  Pallas kernels  13.2 us (53%)
  starting transfers between devices  7.95 us (32%)
  waiting for transfers between devices  3.06 us (12%)
  between operations  0.74 us (3%)
    pallas_call x3, Pallas kernels, cross_terms(): pl.pallas_call(functools.partial(cross_kernel, places, near, scale_at), i...  5 us
    pallas_call x2, Pallas kernels, local_terms(): pl.pallas_call(local_kernel, in_specs=[VMEM] * 4, out_specs=[VMEM] * 4, o...  4.24 us
    ppermute x1, starting transfers between devices, local(): got_xa = lax.ppermute(fa, 'ctx', swap_x)  3 us
    pallas_call x1, Pallas kernels, load(): pl.pallas_call(load_kernel, in_specs=[HBM] * 4, out_specs=[VMEM] * 6, out...  2.27 us
    ppermute x1, waiting for transfers between devices, local(): got_xb = lax.ppermute(mixed, 'ctx', swap_x)  1.83 us
    ppermute x1, starting transfers between devices, local(): got_y1 = lax.ppermute(fb, 'ctx', swap_y)  1.6 us
    ppermute x1, starting transfers between devices, local(): far_last = [lax.ppermute(s, 'ctx', swap_x) for s in sums]  1.55 us
    ppermute x1, waiting for transfers between devices, local(): got_y2 = lax.ppermute(sum_a, 'ctx', swap_y)  1.19 us
  transfers between devices with their start and end apart: 5, of which 2 were waited for; matrix products, arithmetic and copies ran while one was open for 0% of the time, Pallas kernels for 38%

profile of v5, /device:TPU:0, one launch (start us, length us, event | category | flops | bytes accessed | tf_op | source)
XLA Modules:
  0.0 24.9 jit_solution(15812747253606123564)
XLA Ops:
  0.6 0.0 copy-start.1
  0.6 0.0 copy-start
  0.7 0.0 copy-start.3
  0.7 0.0 copy-start.2
  0.7 2.3 %load.1 = (bf16[512,512]{1,0:T(8,128)(2,1)S(1)}, bf16[512,1024]{1,0:T(8,128)(2,1)S(1)}, f32[512,128]{1,0:T(8,128)S(1)}, f32[512,128]{1,0:T(8,128)S(1)}, f32[4,12...) custom-call(bf16[512,1024]{1,0:T(8,128)(2,1)} %q.5, bf16[512,1024]{1,0:T(8,128)(2,1)} %k.5, bf16[512,2048]{1,0:T(8,128)(2,1)} %v.5, ...), custom_call_target="tpu_custom_call" | custom-call | tf_op jit(solution)/shard_map/load/pallas_call | solution.py:171
  2.9 3.0 %collective-permute-start.1 = (f32[4,128,128]{2,1,0:T(8,128)S(1)}, f32[4,128,128]{2,1,0:T(8,128)S(1)}, u32[]{:S(2)}, u32[]{:S(2)}) collective-permute-start(f32[4,128,128]{2,1,0:T(8,128)S(1)} %get-tuple-element.49.a), channel_id=1, source_target_pairs={{0,1},{1,0},{2,3},{3,2},{4,5},{5,4},{6,7},{7,6},{8,9},{9,8},{10,11... | collective-permute-start | bytes 786440 | tf_op jit(solution)/shard_map/ppermute | solution.py:426
  5.9 0.0 copy-done.1
  6.0 0.0 copy-done
  6.0 0.0 copy-done.3
  6.0 0.0 copy-done.2
  6.0 0.6 %f_states.1 = (bf16[512,512]{1,0:T(8,128)(2,1)S(1)}, bf16[512,1024]{1,0:T(8,128)(2,1)S(1)}, f32[4,128,128]{2,1,0:T(8,128)S(1)}, f32[4,4,128,128]{3,2,1,0:T(8,128)S(1)}) custom-call(bf16[512,1024]{1,0:T(8,128)(2,1)S(1)} %copy-done.2, bf16[512,1024]{1,0:T(8,128)(2,1)S(1)} %copy-done.3, bf16[512,2048]{1,0:T(8,128)(2,1)S(1)} %copy-done, ...), custom_call_target="tpu_custom_call" | custom-call | tf_op jit(solution)/shard_map/f_states/pallas_call | solution.py:205
  6.5 1.6 %collective-permute-start = (f32[4,128,128]{2,1,0:T(8,128)S(1)}, f32[4,128,128]{2,1,0:T(8,128)S(1)}, u32[]{:S(2)}, u32[]{:S(2)}) collective-permute-start(f32[4,128,128]{2,1,0:T(8,128)S(1)} %get-tuple-element.42.fb), channel_id=1, source_target_pairs={{0,2},{2,0},{1,3},{3,1},{4,6},{6,4},{5,7},{7,5},{8,10},{10,8},{9,1... | collective-permute-start | bytes 786440 | tf_op jit(solution)/shard_map/ppermute | solution.py:430
  8.1 1.0 %g_states.1 = (bf16[512,512]{1,0:T(8,128)(2,1)S(1)}, bf16[512,1024]{1,0:T(8,128)(2,1)S(1)}, bf16[512,512]{1,0:T(8,128)(2,1)S(1)}, bf16[512,1024]{1,0:T(8,128)(2,...) custom-call(bf16[512,1024]{1,0:T(8,128)(2,1)S(1)} %copy-done.2, ...), custom_call_target="tpu_custom_call" | custom-call | tf_op jit(solution)/shard_map/g_states/pallas_call | solution.py:233
  9.2 1.0 %collective-permute-start.4 = (f32[4,128,128]{2,1,0:T(8,128)S(1)}, f32[4,128,128]{2,1,0:T(8,128)S(1)}, u32[]{:S(2)}, u32[]{:S(2)}) collective-permute-start(f32[4,128,128]{2,1,0:T(8,128)S(1)} %get-tuple-element.59), channel_id=1, source_target_pairs={{0,1},{1,0},{2,3},{3,2},{4,5},{5,4},{6,7},{7,6},{8,9},{9,8},{10,11... | collective-permute-start | bytes 786440 | tf_op jit(solution)/shard_map/ppermute | solution.py:433
  10.1 2.1 %local.2 = (f32[512,1024]{1,0:T(8,128)S(1)}, f32[512,512]{1,0:T(8,128)S(1)}, f32[512,1024]{1,0:T(8,128)S(1)}, f32[512,512]{1,0:T(8,128)S(1)}) custom-call(bf16[512,512]{1,0:T(8,128)(2,1)S(1)} %get-tuple-element.39.xf.refs_1_, bf16[512,1024]{1,0:T(8,128)(2,1)S(1)} %get-tuple-element.40.yf.refs_2_, bf16[512,512]{1,0:T(8,128)(2,1)S(1)} %get-tuple-element.44.xg.refs_7_, ...), custom_call_target="tpu_custom_call" | custom-call | tf_op jit(solution)/shard_map/local/pallas_call | solution.py:324
  12.3 2.1 %local.3 = (f32[512,1024]{1,0:T(8,128)S(1)}, f32[512,512]{1,0:T(8,128)S(1)}, f32[512,1024]{1,0:T(8,128)S(1)}, f32[512,512]{1,0:T(8,128)S(1)}) custom-call(bf16[512,512]{1,0:T(8,128)(2,1)S(1)} %get-tuple-element.50.xf.refs_1_, bf16[512,1024]{1,0:T(8,128)(2,1)S(1)} %get-tuple-element.51.yf.refs_2_, bf16[512,512]{1,0:T(8,128)(2,1)S(1)} %get-tuple-element.52.xg.refs_1_, ...), custom_call_target="tpu_custom_call" | custom-call | tf_op jit(solution)/shard_map/local/pallas_call | solution.py:324
  14.4 0.0 collective-permute-done.1.b.refs_6_
  14.4 0.8 %collective-permute-start.3 = (f32[4,128,128]{2,1,0:T(8,128)S(1)}, f32[4,128,128]{2,1,0:T(8,128)S(1)}, u32[]{:S(2)}, u32[]{:S(2)}) collective-permute-start(f32[4,128,128]{2,1,0:T(8,128)S(1)} %add.2.refs_0_), channel_id=1, source_target_pairs={{0,2},{2,0},{1,3},{3,1},{4,6},{6,4},{5,7},{7,5},{8,10},{10,8},{9,1... | collective-permute-start | bytes 786440 | tf_op jit(solution)/shard_map/ppermute | solution.py:438
  15.3 0.0 collective-permute-done.a.refs_6_
  15.3 1.6 %collective-permute-start.2 = (f32[4,128,128]{2,1,0:T(8,128)S(1)}, f32[4,128,128]{2,1,0:T(8,128)S(1)}, u32[]{:S(2)}, u32[]{:S(2)}) collective-permute-start(f32[4,128,128]{2,1,0:T(8,128)S(1)} %add.3.refs_13_), channel_id=1, source_target_pairs={{0,1},{1,0},{2,3},{3,2},{4,5},{5,4},{6,7},{7,6},{8,9},{9,8},{10,11... | collective-permute-start | bytes 786440 | tf_op jit(solution)/shard_map/ppermute | solution.py:440
  16.9 1.8 %collective-permute-done.4.refs_12_.refs_7_ = f32[4,128,128]{2,1,0:T(8,128)S(1)} collective-permute-done((f32[4,128,128]{2,1,0:T(8,128)S(1)}, f32[4,128,128]{2,1,0:T(8,128)S(1)}, u32[]{:S(2)}, u32[]{:S(2)}) %collective-permute-start.4) | collective-permute-done | bytes 262176 | tf_op jit(solution)/shard_map/ppermute | solution.py:433
  18.7 2.1 %near.1 = (bf16[512,2048]{1,0:T(8,128)(2,1)}, bf16[512,1024]{1,0:T(8,128)(2,1)}, bf16[512,1024]{1,0:T(8,128)(2,1)}, bf16[512,2048]{1,0:T(8,128)(2,1)}) custom-call(f32[512,128]{1,0:T(8,128)S(1)} %get-tuple-element.41.scale.refs_0_, bf16[512,512]{1,0:T(8,128)(2,1)S(1)} %get-tuple-element.52.xg.refs_1_, bf16[512,1024]{1,0:T(8,128)(2,1)S(1)} %get-tuple-element.53.yg.refs_2_, ...), custom_call_target="tpu_custom_call" | custom-call | tf_op jit(solution)/shard_map/near/pallas_call | solution.py:387
  20.8 1.2 %collective-permute-done.3.refs_6_ = f32[4,128,128]{2,1,0:T(8,128)S(1)} collective-permute-done((f32[4,128,128]{2,1,0:T(8,128)S(1)}, f32[4,128,128]{2,1,0:T(8,128)S(1)}, u32[]{:S(2)}, u32[]{:S(2)}) %collective-permute-start.3) | collective-permute-done | bytes 262176 | tf_op jit(solution)/shard_map/ppermute | solution.py:438
  22.0 1.5 %far.2 = (bf16[512,2048]{1,0:T(8,128)(2,1)}, bf16[512,1024]{1,0:T(8,128)(2,1)}, bf16[512,1024]{1,0:T(8,128)(2,1)}, bf16[512,2048]{1,0:T(8,128)(2,1)}) custom-call(f32[512,128]{1,0:T(8,128)S(1)} %get-tuple-element.38.scale.refs_0_, ...), custom_call_target="tpu_custom_call", output_to_operand_aliasing={{0}: (8, {}), {1}: (9, {}), {2}: (10, {}), {3}: (11, {})} | custom-call | tf_op jit(solution)/shard_map/far/pallas_call | solution.py:387
  23.5 0.0 collective-permute-done.2.refs_7_
  23.5 1.5 %far.3 = (bf16[512,2048]{1,0:T(8,128)(2,1)}, bf16[512,1024]{1,0:T(8,128)(2,1)}, bf16[512,1024]{1,0:T(8,128)(2,1)}, bf16[512,2048]{1,0:T(8,128)(2,1)}) custom-call(f32[512,128]{1,0:T(8,128)S(1)} %get-tuple-element.38.scale.refs_0_, ...), custom_call_target="tpu_custom_call", output_to_operand_aliasing={{0}: (8, {}), {1}: (9, {}), {2}: (10, {}), {3}: (11, {})} | custom-call | tf_op jit(solution)/shard_map/far/pallas_call | solution.py:387
  (2 shorter events, 0.1 us)
Async XLA Ops:
  0.6 5.3 %copy-start.1 = (bf16[512,2048]{1,0:T(8,128)(2,1)S(1)}, bf16[512,2048]{1,0:T(8,128)(2,1)}, u32[]{:S(2)}) copy-start(bf16[512,2048]{1,0:T(8,128)(2,1)} %do.5) | copy-start | bytes 6291460
  0.6 5.3 %copy-start = (bf16[512,2048]{1,0:T(8,128)(2,1)S(1)}, bf16[512,2048]{1,0:T(8,128)(2,1)}, u32[]{:S(2)}) copy-start(bf16[512,2048]{1,0:T(8,128)(2,1)} %v.5) | copy-start | bytes 6291460
  0.7 5.3 %copy-start.3 = (bf16[512,1024]{1,0:T(8,128)(2,1)S(1)}, bf16[512,1024]{1,0:T(8,128)(2,1)}, u32[]{:S(2)}) copy-start(bf16[512,1024]{1,0:T(8,128)(2,1)} %k.5) | copy-start | bytes 3145732
  0.7 5.3 %copy-start.2 = (bf16[512,1024]{1,0:T(8,128)(2,1)S(1)}, bf16[512,1024]{1,0:T(8,128)(2,1)}, u32[]{:S(2)}) copy-start(bf16[512,1024]{1,0:T(8,128)(2,1)} %q.5) | copy-start | bytes 3145732
  2.9 11.5 %collective-permute-start.1 = (f32[4,128,128]{2,1,0:T(8,128)S(1)}, f32[4,128,128]{2,1,0:T(8,128)S(1)}, u32[]{:S(2)}, u32[]{:S(2)}) collective-permute-start(f32[4,128,128]{2,1,0:T(8,128)S(1)} %get-tuple-element.49.a), channel_id=1, source_target_pairs={{0,1},{1,0},{2,3},{3,2},{4,5},{5,4},{6,7},{7,6},{8,9},{9,8},{10,11... | collective-permute-start | bytes 786440 | tf_op jit(solution)/shard_map/ppermute | solution.py:426
  6.5 8.8 %collective-permute-start = (f32[4,128,128]{2,1,0:T(8,128)S(1)}, f32[4,128,128]{2,1,0:T(8,128)S(1)}, u32[]{:S(2)}, u32[]{:S(2)}) collective-permute-start(f32[4,128,128]{2,1,0:T(8,128)S(1)} %get-tuple-element.42.fb), channel_id=1, source_target_pairs={{0,2},{2,0},{1,3},{3,1},{4,6},{6,4},{5,7},{7,5},{8,10},{10,8},{9,1... | collective-permute-start | bytes 786440 | tf_op jit(solution)/shard_map/ppermute | solution.py:430
  9.2 9.5 %collective-permute-start.4 = (f32[4,128,128]{2,1,0:T(8,128)S(1)}, f32[4,128,128]{2,1,0:T(8,128)S(1)}, u32[]{:S(2)}, u32[]{:S(2)}) collective-permute-start(f32[4,128,128]{2,1,0:T(8,128)S(1)} %get-tuple-element.59), channel_id=1, source_target_pairs={{0,1},{1,0},{2,3},{3,2},{4,5},{5,4},{6,7},{7,6},{8,9},{9,8},{10,11... | collective-permute-start | bytes 786440 | tf_op jit(solution)/shard_map/ppermute | solution.py:433
  14.4 7.6 %collective-permute-start.3 = (f32[4,128,128]{2,1,0:T(8,128)S(1)}, f32[4,128,128]{2,1,0:T(8,128)S(1)}, u32[]{:S(2)}, u32[]{:S(2)}) collective-permute-start(f32[4,128,128]{2,1,0:T(8,128)S(1)} %add.2.refs_0_), channel_id=1, source_target_pairs={{0,2},{2,0},{1,3},{3,1},{4,6},{6,4},{5,7},{7,5},{8,10},{10,8},{9,1... | collective-permute-start | bytes 786440 | tf_op jit(solution)/shard_map/ppermute | solution.py:438
  15.3 8.2 %collective-permute-start.2 = (f32[4,128,128]{2,1,0:T(8,128)S(1)}, f32[4,128,128]{2,1,0:T(8,128)S(1)}, u32[]{:S(2)}, u32[]{:S(2)}) collective-permute-start(f32[4,128,128]{2,1,0:T(8,128)S(1)} %add.3.refs_13_), channel_id=1, source_target_pairs={{0,1},{1,0},{2,3},{3,2},{4,5},{5,4},{6,7},{7,6},{8,9},{9,8},{10,11... | collective-permute-start | bytes 786440 | tf_op jit(solution)/shard_map/ppermute | solution.py:440

commit v6 on v5

v6 whole, which is shorter than its diff:
```python
import functools
import typing

import jax
import jax.numpy as jnp
from jax import lax
from jax.experimental import pallas as pl
from jax.experimental.pallas import tpu as pltpu
from jax.sharding import PartitionSpec as P


H = 16
DK = 64
DV = 128
PAIRS = H // 2
HALF = PAIRS // 2
XW = 2 * DK
YW = 2 * DV
CHUNK = 128
PIECE = 256
FIRST = HALF
EARLY = 0
LATE = 5
VMEM_LIMIT = 12 * 1024 * 1024

NN = (((1,), (0,)), ((), ()))
NT = (((1,), (1,)), ((), ()))
TN = (((0,), (0,)), ((), ()))
F32 = jnp.float32
BF16 = jnp.bfloat16

HBM = pl.BlockSpec(memory_space=pltpu.HBM)
VMEM = pl.BlockSpec(memory_space=pltpu.VMEM)


def dot(a, b, dims=NN):
    return lax.dot_general(a, b, dims, preferred_element_type=F32)


def is_low():
    size = lax.axis_size("ctx")
    return lax.axis_index("ctx") < (size // 2 if size == 4 else size)


def is_inner():
    at = lax.axis_index("ctx")
    return (at == 1) | (at == 2) if lax.axis_size("ctx") == 4 else at >= 0


def in_vmem(array):
    return pltpu.with_memory_space_constraint(array, pltpu.VMEM)


def in_hbm(array):
    return pltpu.with_memory_space_constraint(array, pltpu.HBM)


def x_shape(length, pairs, dtype=BF16):
    return pltpu.VMEM((length, pairs * XW), dtype)


def y_shape(length, pairs, dtype=BF16):
    return pltpu.VMEM((length, pairs * YW), dtype)


def states_shape(pairs):
    return pltpu.VMEM((pairs, XW, DV), F32)


def steps_shape(length, pairs):
    return pltpu.VMEM((pairs, length // CHUNK, XW, DV), F32)


def params():
    return pltpu.CompilerParams(vmem_limit_bytes=VMEM_LIMIT)


def diagonal(square):
    return jnp.concatenate([square[:DK, :DV], square[DK:, DV:]], axis=0)


def xs(p):
    return slice(p * XW, (p + 1) * XW)


def ys(p):
    return slice(p * YW, (p + 1) * YW)


def chunks_of(array, size=CHUNK):
    return [slice(c, c + size) for c in range(0, array.shape[0], size)]


def twice(scale):
    return jnp.concatenate([scale, scale], axis=1)


class Pair(typing.NamedTuple):
    x: typing.Any
    y: typing.Any
    steps: typing.Any
    at: int


def pairs_of(x, y, steps):
    return [Pair(x, y, steps, i) for i in range(steps.shape[0])]


class Places:
    def __init__(self):
        self.arrays = []

    def __call__(self, array):
        for i, other in enumerate(self.arrays):
            if other is array:
                return i
        self.arrays.append(array)
        return len(self.arrays) - 1


def chunk_states(x, y, first, count, scaled, scale, rows, kept=None):
    states = []
    for p in range(count):
        old, new = x[rows, xs(first + p)], y[rows, ys(first + p)]
        if kept is not None:
            kept[rows, xs(p)] = old
        if scale is not None:
            new = (new.astype(F32) * twice(scale[rows, :])).astype(BF16)
            scaled[rows, ys(p)] = new
        states.append(diagonal(dot(old, new, TN)))
    return states


def block_states(parts, backward, steps):
    count = len(parts)
    states = []
    for p in range(len(parts[0])):
        zero = jnp.zeros_like(parts[0][p])
        before, after = [zero], [zero]
        for c in range(count - 1):
            before.append(before[-1] + parts[c][p])
            after.append(after[-1] + parts[count - 1 - c][p])
        for c in range(count):
            steps[p, c] = jnp.where(backward, after[count - 1 - c], before[c])
        states.append(before[-1] + parts[-1][p])
    return states


def either(low, work, kv, qd):
    @pl.when(low)
    def _():
        work(*kv)

    @pl.when(jnp.logical_not(low))
    def _():
        work(*qd)


def load_kernel(q, k, v, do, x, y, scale_low, scale_high, state, raw, sems):
    low = is_low()
    length = q.shape[0]
    pieces = chunks_of(q, PIECE)

    def copies(a, b):
        return [
            (
                pltpu.make_async_copy(a.at[rows, pl.ds(0, FIRST * XW)], x.at[rows, :], sems.at[0, c]),
                pltpu.make_async_copy(b.at[rows, pl.ds(0, FIRST * YW)], raw.at[rows, :], sems.at[1, c]),
            )
            for c, rows in enumerate(pieces)
        ]

    def start(a, b):
        for pair in copies(a, b):
            for copy in pair:
                copy.start()

    either(low, start, (k, v), (q, do))
    at = lax.axis_index("ctx") * length + lax.broadcasted_iota(jnp.int32, (length, DV), 0)
    scale = 1.0 / jnp.sqrt(DK * (at.astype(F32) + 1.0))
    scale_low[...] = jnp.where(low, scale, 1.0)
    scale_high[...] = jnp.where(low, 1.0, scale)
    total = None
    for rows, pair in zip(pieces, copies(k, v)):
        for copy in pair:
            copy.wait()
        parts = chunk_states(x, raw, 0, FIRST, y, scale_high, rows)
        total = parts if total is None else [a + b for a, b in zip(total, parts)]
    for p, new in enumerate(total):
        state[p] = new


def load(q, k, v, do):
    length = q.shape[0]
    x, y = x_shape(length, FIRST), y_shape(length, FIRST)
    scale = pltpu.VMEM((length, DV), F32)
    return pl.pallas_call(
        load_kernel,
        in_specs=[HBM] * 4,
        out_specs=[VMEM] * 5,
        out_shape=[x, y, scale, scale, states_shape(FIRST)],
        scratch_shapes=[y, pltpu.SemaphoreType.DMA((2, length // PIECE))],
        compiler_params=params(),
        name="load",
    )(*map(in_hbm, (q, k, v, do)))


def f_kernel(q, k, v, do, scale, x, y, steps, state):
    low = is_low()

    def work(a, b):
        parts = [chunk_states(a, b, FIRST, PAIRS - FIRST, y, scale, rows, x) for rows in chunks_of(x)]
        states = block_states(parts, jnp.logical_not(low), steps)
        for p, new in enumerate(states):
            state[p] = new

    either(low, work, (k, v), (q, do))


def f_states(q, k, v, do, scale):
    length, count = q.shape[0], PAIRS - FIRST
    return pl.pallas_call(
        f_kernel,
        in_specs=[VMEM] * 5,
        out_specs=[VMEM] * 4,
        out_shape=[
            x_shape(length, count),
            y_shape(length, count),
            steps_shape(length, count),
            states_shape(count),
        ],
        compiler_params=params(),
        name="f_states",
    )(*map(in_vmem, (q, k, v, do, scale)))


def g_kernel(q, k, v, do, scale, x, y, steps, state):
    low = is_low()

    def work(a, b):
        for first in (0, HALF):
            half_x, half_y = x.at[:, pl.ds(first * XW, HALF * XW)], y.at[:, pl.ds(first * YW, HALF * YW)]
            parts = [chunk_states(a, b, first, HALF, half_y, scale, rows, half_x) for rows in chunks_of(x)]
            for p, new in enumerate(block_states(parts, low, steps.at[pl.ds(first, HALF)])):
                state[first + p] = new

    either(low, work, (q, do), (k, v))


def g_states(q, k, v, do, scale):
    length = q.shape[0]
    return pl.pallas_call(
        g_kernel,
        in_specs=[VMEM] * 5,
        out_specs=[VMEM] * 4,
        out_shape=[x_shape(length, PAIRS), y_shape(length, PAIRS), steps_shape(length, PAIRS), states_shape(PAIRS)],
        compiler_params=params(),
        name="g_states",
    )(*map(in_vmem, (q, k, v, do, scale)))


def steps_kernel(x, y, *refs):
    parts = [chunk_states(x, y, 0, FIRST, None, None, rows) for rows in chunks_of(x)]
    block_states(parts, jnp.logical_not(is_low()), refs[-1])


def first_steps(x, y, after):
    return pl.pallas_call(
        steps_kernel,
        in_specs=[VMEM] * (2 + len(after)),
        out_specs=VMEM,
        out_shape=steps_shape(x.shape[0], FIRST),
        compiler_params=params(),
        name="first_steps",
    )(*map(in_vmem, (x, y, *after)))


def payload_kernel(work, taken, *refs):
    out = refs[-1]
    for p in range(out.shape[0]):
        out[p] = work(p, *refs[:taken])


def payload(name, work, count, ins, after=()):
    return pl.pallas_call(
        functools.partial(payload_kernel, work, len(ins)),
        in_specs=[VMEM] * (len(ins) + len(after)),
        out_specs=VMEM,
        out_shape=states_shape(count),
        compiler_params=params(),
        name=name,
    )(*ins, *map(in_vmem, after))


def head_rows(x):
    lane = lax.broadcasted_iota(jnp.int32, x.shape, 1)
    zero = jnp.zeros_like(x)
    return jnp.concatenate([jnp.where(lane < DK, x, zero), jnp.where(lane >= DK, x, zero)], axis=0)


def head_blocks(y):
    zero = jnp.zeros_like(y[:, :DV])
    top = jnp.concatenate([y[:, :DV], zero], axis=1)
    return jnp.concatenate([top, jnp.concatenate([zero, y[:, DV:]], axis=1)], axis=0)


def state_blocks(state):
    row = lax.broadcasted_iota(jnp.int32, state.shape, 0)
    zero = jnp.zeros_like(state)
    both = jnp.concatenate([jnp.where(row < DK, state, zero), jnp.where(row >= DK, state, zero)], axis=1)
    return both.astype(BF16)


def turned(scores):
    return jnp.concatenate([scores[:, :CHUNK].T, scores[:, CHUNK:].T], axis=1)


def out_copies(staged, at, when_low, when_high, pair, width, sem):
    source = staged.at[:, pl.ds(at * width, width)]
    columns = pl.ds(pair * width, width)
    return [pltpu.make_async_copy(source, target.at[:, columns], sem.at[at]) for target in (when_low, when_high)]


def send(copies, low):
    @pl.when(low)
    def _():
        copies[0].start()

    @pl.when(jnp.logical_not(low))
    def _():
        copies[1].start()


def local_kernel(places, *refs):
    low = is_low()
    o1, o3, o2, o4 = refs[-4:]
    row = lax.broadcasted_iota(jnp.int32, (CHUNK, 2 * CHUNK), 0)
    col = lax.rem(lax.broadcasted_iota(jnp.int32, (CHUNK, 2 * CHUNK), 1), CHUNK)
    keep = jnp.where(low, row - col, col - row) >= 0
    chunks = chunks_of(o1)
    for p, (f, g) in enumerate(places):
        (xf, yf), (xg, yg) = (refs[f.x], refs[f.y]), (refs[g.x], refs[g.y])
        parts, scores = [], []
        for rows in chunks:
            x1, y1, x2, y2 = xf[rows, xs(f.at)], yf[rows, ys(f.at)], xg[rows, xs(g.at)], yg[rows, ys(g.at)]
            parts.append((head_rows(x1), head_blocks(y1), x2, y2))
        for x1s, y1s, x2, y2 in parts:
            m = jnp.where(keep, dot(x2, x1s, NT), 0.0).astype(BF16)
            n = jnp.where(keep, dot(y2, y1s, NT), 0.0).astype(BF16)
            scores.append((m, n))
        for rows, (x1s, y1s, x2, y2), (m, n) in zip(chunks, parts, scores):
            o1[rows, ys(p)] = dot(m, y1s)
            o3[rows, xs(p)] = dot(n, x1s)
            o2[rows, ys(p)] = dot(turned(m), head_blocks(y2))
            o4[rows, xs(p)] = dot(turned(n), head_rows(x2))


def local_terms(f, g, after=()):
    place = Places()
    places = [[Pair(place(s.x), place(s.y), None, s.at) for s in both] for both in zip(f, g)]
    length, count = f[0].x.shape[0], len(f)
    x, y = x_shape(length, count, F32), y_shape(length, count, F32)
    return pl.pallas_call(
        functools.partial(local_kernel, places),
        in_specs=[VMEM] * (len(place.arrays) + len(after)),
        out_specs=[VMEM] * 4,
        out_shape=[y, x, y, x],
        compiler_params=params(),
        name="local",
    )(*map(in_vmem, (*place.arrays, *after)))


ALWAYS, INNER, OUTER = range(3)


class Job(typing.NamedTuple):
    side: Pair
    other: Pair
    wide: typing.Any
    narrow: typing.Any
    at: int
    terms: tuple
    pair: int


def cross_kernel(jobs, near, scale_at, *refs):
    att, qg, kg, vg, wide_out, narrow_out, wide_sem, narrow_sem = refs[-8:]
    low = is_low()
    inner = is_inner()
    scale = refs[scale_at]
    started = []
    for i, job in enumerate(jobs):
        x, y, steps, wide, narrow = [refs[w] for w in (job.side.x, job.side.y, job.other.steps, job.wide, job.narrow)]
        at = job.side.at
        base = None
        for array, where, when in job.terms:
            term = refs[array][where]
            if when != ALWAYS:
                term = jnp.where(inner, term, 0.0) if when == INNER else jnp.where(inner, 0.0, term)
            base = term if base is None else base + term
        chunks = chunks_of(x)
        blocks = [state_blocks(base + steps[job.other.at, c]) for c in range(len(chunks))]
        a = [dot(x[rows, xs(at)], b) for rows, b in zip(chunks, blocks)]
        b = [dot(y[rows, ys(at)], b, NT) for rows, b in zip(chunks, blocks)]
        targets = (att, vg, qg, kg) if near else (vg, att, kg, qg)
        to_wide = out_copies(wide_out, i, targets[0], targets[1], job.pair, YW, wide_sem)
        to_narrow = out_copies(narrow_out, i, targets[2], targets[3], job.pair, XW, narrow_sem)
        for rows, new in zip(chunks, a):
            wide_out[rows, ys(i)] = ((wide[rows, ys(job.at)] + new) * twice(scale[rows, :])).astype(BF16)
        send(to_wide, low)
        for rows, new in zip(chunks, b):
            narrow_out[rows, xs(i)] = (narrow[rows, xs(job.at)] + new).astype(BF16)
        send(to_narrow, low)
        started += [to_wide[0], to_narrow[0]]
    for copy in started:
        copy.wait()


def cross_terms(jobs, near, scale, outs):
    place, received = Places(), Places()
    scale_at = place(scale)
    placed = []
    for job in jobs:
        side = Pair(place(job.side.x), place(job.side.y), None, job.side.at)
        other = Pair(None, None, place(job.other.steps), job.other.at)
        terms = []
        for array, where, when in job.terms:
            received(array)
            terms.append((place(array), where, when))
        placed.append(Job(side, other, place(job.wide), place(job.narrow), job.at, tuple(terms), job.pair))
    length, count = scale.shape[0], len(jobs)
    ins = [a if any(a is r for r in received.arrays) else in_vmem(a) for a in place.arrays]
    wide = jax.ShapeDtypeStruct((length, H * DV), BF16)
    narrow = jax.ShapeDtypeStruct((length, H * DK), BF16)
    return pl.pallas_call(
        functools.partial(cross_kernel, placed, near, scale_at),
        in_specs=[VMEM] * len(ins) + [HBM] * len(outs),
        out_specs=[HBM] * 4,
        out_shape=[wide, narrow, narrow, wide],
        input_output_aliases={len(ins) + i: i for i in range(len(outs))},
        scratch_shapes=[
            pltpu.VMEM((length, count * YW), BF16),
            pltpu.VMEM((length, count * XW), BF16),
            pltpu.SemaphoreType.DMA((count,)),
            pltpu.SemaphoreType.DMA((count,)),
        ],
        compiler_params=params(),
        name="near" if near else "far",
    )(*ins, *outs)


def scan_sum(state, size, sign):
    def moved(array, step):
        return lax.ppermute(array, "ctx", [(i, i + sign * step) for i in range(size) if 0 <= i + sign * step < size])

    total, step = moved(state, 1), 1
    while step < size:
        total, step = total + moved(total, step), 2 * step
    return total


def local(queries, keys, values, out_grad):
    size = lax.axis_size("ctx")
    args = (queries, keys, values, out_grad)
    x1, y1, scale_low, scale_high, fa = load(*args)
    swap_x = functools.partial(lax.ppermute, axis_name="ctx", perm=[(0, 1), (1, 0), (2, 3), (3, 2)])
    swap_y = functools.partial(lax.ppermute, axis_name="ctx", perm=[(0, 2), (2, 0), (1, 3), (3, 1)])
    if size == 4:
        got_xa = swap_x(fa)
    x2, y2, f_steps, fb = f_states(*args, scale_high)
    if size == 4:
        got_y1 = swap_y(fb)
    x, y, g_steps, gs = g_states(*args, scale_low)
    g = pairs_of(x, y, g_steps)
    f = pairs_of(x1, y1, f_steps) + pairs_of(x2, y2, f_steps)
    parts, token = [], []
    if EARLY:
        parts.append(local_terms(f[:EARLY], g[:EARLY]))
        token = parts[0][:1]
    if size == 4:
        mixed = payload("mixed", lambda p, a, b: jnp.where(is_inner(), a[p], b[p]), HALF, (gs, fb), token)
        got_xb = swap_x(mixed)
        parts.append(local_terms(f[EARLY:LATE], g[EARLY:LATE], [mixed]))
        sum_a = payload("swapped", lambda p, a, b: a[p] + b[p], HALF, (fa, got_xa), parts[-1][:1])
        got_y2 = swap_y(sum_a)
        last = payload(
            "summed", lambda p, a, b: a[p] + jnp.where(is_inner(), b[HALF + p], 0.0), HALF, (got_y1, gs), [sum_a]
        )
        got_last = swap_x(last)
        parts.append(local_terms(f[LATE:], g[LATE:], [last]))
        token = [last]
        near = [(array, p, INNER) for array in (got_xa, got_xb) for p in range(HALF)]
        far = [((got_y2, p, ALWAYS), (got_xb, p, OUTER)) for p in range(HALF)]
        far += [((got_y1, p, ALWAYS), (got_last, p, ALWAYS)) for p in range(HALF)]
    else:
        parts += [local_terms(f[EARLY:LATE], g[EARLY:LATE]), local_terms(f[LATE:], g[LATE:])]
        token = []
        near = [(array, p, ALWAYS) for array in [scan_sum(s, size, 1) for s in (fa, fb)] for p in range(HALF)]
        after_me = scan_sum(gs, size, -1)
        far = [((after_me, p, ALWAYS),) for p in range(PAIRS)]
    x1_steps = first_steps(x1, y1, token)
    f[:HALF] = pairs_of(x1, y1, x1_steps)
    local_of = [(part, p) for part in parts for p in range(part[0].shape[1] // YW)]

    def jobs(pairs, side, other, results, terms):
        return [Job(side[p], other[p], local_of[p][0][results], local_of[p][0][results + 1], local_of[p][1], terms(p), p) for p in pairs]

    outs = cross_terms(jobs(range(PAIRS), g, f, 0, lambda p: (near[p],)), True, scale_low, [])
    for pairs in (range(HALF), range(HALF, PAIRS)):
        outs = cross_terms(jobs(pairs, f, g, 2, lambda p: far[p]), False, scale_high, outs)
    return tuple(outs)


def solution(mesh):
    spec = P(("batch", "ctx"), None)
    return jax.shard_map(local, mesh=mesh, in_specs=(spec,) * 4, out_specs=(spec,) * 4, check_vma=False)
```

time: 25.1 us -> 24.7 us (0.984)
  waiting for transfers between devices: 3.06 us -> 0.92 us
  starting transfers between devices: 7.95 us -> 9.54 us
    ppermute x5, waiting for transfers between devices: 3.06 us -> 0.92 us  [the longest x1 0.91 us: local(): got_last = swap_x(last)]
    ppermute x5, starting transfers between devices: 7.95 us -> 9.54 us  [the longest x1 3 us: local(): got_xa = swap_x(fa)]
    pallas_call x9 -> x11, Pallas kernels: 12.6 us -> 12.7 us  [the longest x3 5.01 us: cross_terms(): pl.pallas_call(functools.partial(cross_kernel, placed, near, scale_at), i...]
  transfers between devices with their start and end apart: 5 -> 5, of which waited for: 2 -> 1; matrix products, arithmetic and copies ran while one was open for 0% -> 0% of each run, Pallas kernels for 38% -> 41%
where the time goes in v6:
time: 24.7 us; the launch traced here: 24.5 us
  Pallas kernels  13.3 us (54%)
  starting transfers between devices  9.54 us (39%)
  waiting for transfers between devices  0.92 us (4%)
  between operations  0.77 us (3%)
    pallas_call x3, Pallas kernels, cross_terms(): pl.pallas_call(functools.partial(cross_kernel, placed, near, scale_at), i...  5.01 us
    pallas_call x2, Pallas kernels, local_terms(): pl.pallas_call(functools.partial(local_kernel, places), in_specs=[VMEM] *...  4.25 us
    ppermute x1, starting transfers between devices, local(): got_xa = swap_x(fa)  3 us
    ppermute x1, starting transfers between devices, local(): got_y2 = swap_y(sum_a)  1.95 us
    pallas_call x1, Pallas kernels, load(): pl.pallas_call(load_kernel, in_specs=[HBM] * 4, out_specs=[VMEM] * 5, out...  1.84 us
    ppermute x1, starting transfers between devices, local(): got_y1 = swap_y(fb)  1.59 us
    ppermute x1, starting transfers between devices, local(): got_last = swap_x(last)  1.56 us
    ppermute x1, starting transfers between devices, local(): got_xb = swap_x(mixed)  1.44 us
  transfers between devices with their start and end apart: 5, of which 1 were waited for; matrix products, arithmetic and copies ran while one was open for 0% of the time, Pallas kernels for 41%

profile of v6, /device:TPU:0, one launch (start us, length us, event | category | flops | bytes accessed | tf_op | source)
XLA Modules:
  0.0 24.5 jit_solution(2490893092076629265)
XLA Ops:
  0.6 0.0 copy-start.2
  0.6 0.0 copy-start.3
  0.7 0.0 copy-start
  0.7 0.0 copy-start.1
  0.7 1.8 %load.1 = (bf16[512,512]{1,0:T(8,128)(2,1)S(1)}, bf16[512,1024]{1,0:T(8,128)(2,1)S(1)}, f32[512,128]{1,0:T(8,128)S(1)}, f32[512,128]{1,0:T(8,128)S(1)}, f32[4,128,128]{2,1,0:T(8,128)S(1)}) custom-call(bf16[512,1024]{1,0:T(8,128)(2,1)} %q.5, bf16[512,1024]{1,0:T(8,128)(2,1)} %k.5, bf16[512,2048]{1,0:T(8,128)(2,1)} %v.5, bf16[512,2048]{1,0:T(8,128)(2,1)} %do.5), custom_call_target="tpu_custom_call" | custom-call | tf_op jit(solution)/shard_map/load/pallas_call | solution.py:197
  2.5 3.0 %collective-permute-start.1 = (f32[4,128,128]{2,1,0:T(8,128)S(1)}, f32[4,128,128]{2,1,0:T(8,128)S(1)}, u32[]{:S(2)}, u32[]{:S(2)}) collective-permute-start(f32[4,128,128]{2,1,0:T(8,128)S(1)} %get-tuple-element.40.refs_0_), channel_id=1, source_target_pairs={{0,1},{1,0},{2,3},{3,2},{4,5},{5,4},{6,7},{7,6},{8,9},{9,8},{10,11... | collective-permute-start | bytes 786440 | tf_op jit(solution)/shard_map/ppermute | solution.py:469
  5.5 0.0 copy-done.2
  5.5 0.0 copy-done.3
  5.5 0.0 copy-done
  5.5 0.0 copy-done.1
  5.5 0.6 %f_states.1 = (bf16[512,512]{1,0:T(8,128)(2,1)S(1)}, bf16[512,1024]{1,0:T(8,128)(2,1)S(1)}, f32[4,4,128,128]{3,2,1,0:T(8,128)S(1)}, f32[4,128,128]{2,1,0:T(8,128)S(1)}) custom-call(bf16[512,1024]{1,0:T(8,128)(2,1)S(1)} %copy-done.2, bf16[512,1024]{1,0:T(8,128)(2,1)S(1)} %copy-done.3, bf16[512,2048]{1,0:T(8,128)(2,1)S(1)} %copy-done, ...), custom_call_target="tpu_custom_call" | custom-call | tf_op jit(solution)/shard_map/f_states/pallas_call | solution.py:222
  6.1 1.6 %collective-permute-start = (f32[4,128,128]{2,1,0:T(8,128)S(1)}, f32[4,128,128]{2,1,0:T(8,128)S(1)}, u32[]{:S(2)}, u32[]{:S(2)}) collective-permute-start(f32[4,128,128]{2,1,0:T(8,128)S(1)} %get-tuple-element.38.refs_1_), channel_id=1, source_target_pairs={{0,2},{2,0},{1,3},{3,1},{4,6},{6,4},{5,7},{7,5},{8,10},{10,8},{9,1... | collective-permute-start | bytes 786440 | tf_op jit(solution)/shard_map/ppermute | solution.py:472
  7.7 1.0 %g_states.1 = (bf16[512,1024]{1,0:T(8,128)(2,1)S(1)}, bf16[512,2048]{1,0:T(8,128)(2,1)S(1)}, f32[8,4,128,128]{3,2,1,0:T(8,128)S(1)}, f32[8,128,128]{2,1,0:T(8,128)S(1)}) custom-call(bf16[512,1024]{1,0:T(8,128)(2,1)S(1)} %copy-done.2, bf16[512,1024]{1,0:T(8,128)(2,1)S(1)} %copy-done.3, bf16[512,2048]{1,0:T(8,128)(2,1)S(1)} %copy-done, ...), custom_call_target="tpu_custom_call" | custom-call | tf_op jit(solution)/shard_map/g_states/pallas_call | solution.py:252
  8.8 1.4 %collective-permute-start.4 = (f32[4,128,128]{2,1,0:T(8,128)S(1)}, f32[4,128,128]{2,1,0:T(8,128)S(1)}, u32[]{:S(2)}, u32[]{:S(2)}) collective-permute-start(f32[4,128,128]{2,1,0:T(8,128)S(1)} %mixed.1.refs_6_), channel_id=1, source_target_pairs={{0,1},{1,0},{2,3},{3,2},{4,5},{5,4},{6,7},{7,6},{8,9},{9,8},{10,11... | collective-permute-start | bytes 786440 | tf_op jit(solution)/shard_map/ppermute | solution.py:482
  10.2 2.6 %local.2 = (f32[512,1280]{1,0:T(8,128)S(1)}, f32[512,640]{1,0:T(8,128)S(1)}, f32[512,1280]{1,0:T(8,128)S(1)}, f32[512,640]{1,0:T(8,128)S(1)}) custom-call(bf16[512,512]{1,0:T(8,128)(2,1)S(1)} %get-tuple-element.41.refs_0_.x.refs_1_, bf16[512,1024]{1,0:T(8,128)(2,1)S(1)} %get-tuple-element.42.refs_1_.y.refs_2_, ...), custom_call_target="tpu_custom_call" | custom-call | tf_op jit(solution)/shard_map/local/pallas_call | solution.py:363
  12.8 0.0 collective-permute-done.1.refs_1_.refs_4_
  12.9 2.0 %collective-permute-start.3 = (f32[4,128,128]{2,1,0:T(8,128)S(1)}, f32[4,128,128]{2,1,0:T(8,128)S(1)}, u32[]{:S(2)}, u32[]{:S(2)}) collective-permute-start(f32[4,128,128]{2,1,0:T(8,128)S(1)} %swapped.1.refs_2_), channel_id=1, source_target_pairs={{0,2},{2,0},{1,3},{3,1},{4,6},{6,4},{5,7},{7,5},{8,10},{10,8},{9,1... | collective-permute-start | bytes 786440 | tf_op jit(solution)/shard_map/ppermute | solution.py:485
  14.8 0.0 collective-permute-done.refs_0_.refs_4_
  14.9 1.6 %collective-permute-start.2 = (f32[4,128,128]{2,1,0:T(8,128)S(1)}, f32[4,128,128]{2,1,0:T(8,128)S(1)}, u32[]{:S(2)}, u32[]{:S(2)}) collective-permute-start(f32[4,128,128]{2,1,0:T(8,128)S(1)} %summed.1.refs_4_.refs_0_), channel_id=1, source_target_pairs={{0,1},{1,0},{2,3},{3,2},{4,5},{5,4},{6,7},{7,6},{8,9},{9,8},{10,11... | collective-permute-start | bytes 786440 | tf_op jit(solution)/shard_map/ppermute | solution.py:489
  16.5 1.6 %local.3 = (f32[512,768]{1,0:T(8,128)S(1)}, f32[512,384]{1,0:T(8,128)S(1)}, f32[512,768]{1,0:T(8,128)S(1)}, f32[512,384]{1,0:T(8,128)S(1)}) custom-call(bf16[512,512]{1,0:T(8,128)(2,1)S(1)} %get-tuple-element.34.refs_4_.refs_0_.refs_1_, bf16[512,1024]{1,0:T(8,128)(2,1)S(1)} %get-tuple-element.35.refs_5_.refs_1_.refs_2_, ...), custom_call_target="tpu_custom_call" | custom-call | tf_op jit(solution)/shard_map/local/pallas_call | solution.py:363
  18.1 0.5 %first_steps.1.refs_3_ = f32[4,4,128,128]{3,2,1,0:T(8,128)S(1)} custom-call(bf16[512,512]{1,0:T(8,128)(2,1)S(1)} %get-tuple-element.41.refs_0_.x.refs_1_, bf16[512,1024]{1,0:T(8,128)(2,1)S(1)} %get-tuple-element.42.refs_1_.y.refs_2_, f32[4,128,128]{2,1,0:T(8,128)S(1)} %summed.1.refs_4_.refs_0_), custom_call_target="tpu_custom_call" | custom-call | tf_op jit(solution)/shard_map/first_steps/pallas_call | solution.py:268
  18.6 0.0 collective-permute-done.4.refs_8_.refs_5_
  18.6 2.1 %near.1 = (bf16[512,2048]{1,0:T(8,128)(2,1)}, bf16[512,1024]{1,0:T(8,128)(2,1)}, bf16[512,1024]{1,0:T(8,128)(2,1)}, bf16[512,2048]{1,0:T(8,128)(2,1)}) custom-call(f32[512,128]{1,0:T(8,128)S(1)} %get-tuple-element.36.scale.refs_0_, bf16[512,1024]{1,0:T(8,128)(2,1)S(1)} %get-tuple-element.43.refs_2_.refs_1_, ...), custom_call_target="tpu_custom_call" | custom-call | tf_op jit(solution)/shard_map/near/pallas_call | solution.py:435
  20.7 0.0 collective-permute-done.3.refs_4_
  20.7 1.5 %far.2 = (bf16[512,2048]{1,0:T(8,128)(2,1)}, bf16[512,1024]{1,0:T(8,128)(2,1)}, bf16[512,1024]{1,0:T(8,128)(2,1)}, bf16[512,2048]{1,0:T(8,128)(2,1)}) custom-call(f32[512,128]{1,0:T(8,128)S(1)} %get-tuple-element.33.scale.refs_0_, ...), custom_call_target="tpu_custom_call", output_to_operand_aliasing={{0}: (8, {}), {1}: (9, {}), {2}: (10, {}), {3}: (11, {})} | custom-call | tf_op jit(solution)/shard_map/far/pallas_call | solution.py:435
  22.2 0.9 %collective-permute-done.2.refs_5_ = f32[4,128,128]{2,1,0:T(8,128)S(1)} collective-permute-done((f32[4,128,128]{2,1,0:T(8,128)S(1)}, f32[4,128,128]{2,1,0:T(8,128)S(1)}, u32[]{:S(2)}, u32[]{:S(2)}) %collective-permute-start.2) | collective-permute-done | bytes 262176 | tf_op jit(solution)/shard_map/ppermute | solution.py:489
  23.1 1.4 %far.3 = (bf16[512,2048]{1,0:T(8,128)(2,1)}, bf16[512,1024]{1,0:T(8,128)(2,1)}, bf16[512,1024]{1,0:T(8,128)(2,1)}, bf16[512,2048]{1,0:T(8,128)(2,1)}) custom-call(f32[512,128]{1,0:T(8,128)S(1)} %get-tuple-element.33.scale.refs_0_, ...), custom_call_target="tpu_custom_call", output_to_operand_aliasing={{0}: (10, {}), {1}: (11, {}), {2}: (12, {}), {3}: (13, {})} | custom-call | tf_op jit(solution)/shard_map/far/pallas_call | solution.py:435
  (3 shorter events, 0.1 us)
Async XLA Ops:
  0.6 4.9 %copy-start.2 = (bf16[512,1024]{1,0:T(8,128)(2,1)S(1)}, bf16[512,1024]{1,0:T(8,128)(2,1)}, u32[]{:S(2)}) copy-start(bf16[512,1024]{1,0:T(8,128)(2,1)} %q.5) | copy-start | bytes 3145732
  0.6 4.9 %copy-start.3 = (bf16[512,1024]{1,0:T(8,128)(2,1)S(1)}, bf16[512,1024]{1,0:T(8,128)(2,1)}, u32[]{:S(2)}) copy-start(bf16[512,1024]{1,0:T(8,128)(2,1)} %k.5) | copy-start | bytes 3145732
  0.7 4.9 %copy-start = (bf16[512,2048]{1,0:T(8,128)(2,1)S(1)}, bf16[512,2048]{1,0:T(8,128)(2,1)}, u32[]{:S(2)}) copy-start(bf16[512,2048]{1,0:T(8,128)(2,1)} %v.5) | copy-start | bytes 6291460
  0.7 4.9 %copy-start.1 = (bf16[512,2048]{1,0:T(8,128)(2,1)S(1)}, bf16[512,2048]{1,0:T(8,128)(2,1)}, u32[]{:S(2)}) copy-start(bf16[512,2048]{1,0:T(8,128)(2,1)} %do.5) | copy-start | bytes 6291460
  2.5 10.3 %collective-permute-start.1 = (f32[4,128,128]{2,1,0:T(8,128)S(1)}, f32[4,128,128]{2,1,0:T(8,128)S(1)}, u32[]{:S(2)}, u32[]{:S(2)}) collective-permute-start(f32[4,128,128]{2,1,0:T(8,128)S(1)} %get-tuple-element.40.refs_0_), channel_id=1, source_target_pairs={{0,1},{1,0},{2,3},{3,2},{4,5},{5,4},{6,7},{7,6},{8,9},{9,8},{10,11... | collective-permute-start | bytes 786440 | tf_op jit(solution)/shard_map/ppermute | solution.py:469
  6.1 8.8 %collective-permute-start = (f32[4,128,128]{2,1,0:T(8,128)S(1)}, f32[4,128,128]{2,1,0:T(8,128)S(1)}, u32[]{:S(2)}, u32[]{:S(2)}) collective-permute-start(f32[4,128,128]{2,1,0:T(8,128)S(1)} %get-tuple-element.38.refs_1_), channel_id=1, source_target_pairs={{0,2},{2,0},{1,3},{3,1},{4,6},{6,4},{5,7},{7,5},{8,10},{10,8},{9,1... | collective-permute-start | bytes 786440 | tf_op jit(solution)/shard_map/ppermute | solution.py:472
  8.8 9.8 %collective-permute-start.4 = (f32[4,128,128]{2,1,0:T(8,128)S(1)}, f32[4,128,128]{2,1,0:T(8,128)S(1)}, u32[]{:S(2)}, u32[]{:S(2)}) collective-permute-start(f32[4,128,128]{2,1,0:T(8,128)S(1)} %mixed.1.refs_6_), channel_id=1, source_target_pairs={{0,1},{1,0},{2,3},{3,2},{4,5},{5,4},{6,7},{7,6},{8,9},{9,8},{10,11... | collective-permute-start | bytes 786440 | tf_op jit(solution)/shard_map/ppermute | solution.py:482
  12.9 7.8 %collective-permute-start.3 = (f32[4,128,128]{2,1,0:T(8,128)S(1)}, f32[4,128,128]{2,1,0:T(8,128)S(1)}, u32[]{:S(2)}, u32[]{:S(2)}) collective-permute-start(f32[4,128,128]{2,1,0:T(8,128)S(1)} %swapped.1.refs_2_), channel_id=1, source_target_pairs={{0,2},{2,0},{1,3},{3,1},{4,6},{6,4},{5,7},{7,5},{8,10},{10,8},{9,1... | collective-permute-start | bytes 786440 | tf_op jit(solution)/shard_map/ppermute | solution.py:485
  14.9 8.2 %collective-permute-start.2 = (f32[4,128,128]{2,1,0:T(8,128)S(1)}, f32[4,128,128]{2,1,0:T(8,128)S(1)}, u32[]{:S(2)}, u32[]{:S(2)}) collective-permute-start(f32[4,128,128]{2,1,0:T(8,128)S(1)} %summed.1.refs_4_.refs_0_), channel_id=1, source_target_pairs={{0,1},{1,0},{2,3},{3,2},{4,5},{5,4},{6,7},{7,6},{8,9},{9,8},{10,11... | collective-permute-start | bytes 786440 | tf_op jit(solution)/shard_map/ppermute | solution.py:489

commit v7 on v6

--- a/solution.py
+++ b/solution.py
@@ -20,7 +20,9 @@
 PIECE = 256
 FIRST = HALF
 EARLY = 0
-LATE = 5
+LATE = 6
+CUT = 2
+ORDER = range(HALF + CUT), range(HALF + CUT, PAIRS)
 VMEM_LIMIT = 12 * 1024 * 1024
 
 NN = (((1,), (0,)), ((), ()))
@@ -416,7 +418,7 @@
         copy.wait()
 
 
-def cross_terms(jobs, near, scale, outs):
+def cross_terms(jobs, near, scale, outs, after=()):
     place, received = Places(), Places()
     scale_at = place(scale)
     placed = []
@@ -434,7 +436,7 @@
     narrow = jax.ShapeDtypeStruct((length, H * DK), BF16)
     return pl.pallas_call(
         functools.partial(cross_kernel, placed, near, scale_at),
-        in_specs=[VMEM] * len(ins) + [HBM] * len(outs),
+        in_specs=[VMEM] * len(ins) + [HBM] * len(outs) + [VMEM] * len(after),
         out_specs=[HBM] * 4,
         out_shape=[wide, narrow, narrow, wide],
         input_output_aliases={len(ins) + i: i for i in range(len(outs))},
@@ -446,7 +448,7 @@
         ],
         compiler_params=params(),
         name="near" if near else "far",
-    )(*ins, *outs)
+    )(*ins, *outs, *map(in_vmem, after))
 
 
 def scan_sum(state, size, sign):
@@ -483,30 +485,37 @@
         parts.append(local_terms(f[EARLY:LATE], g[EARLY:LATE], [mixed]))
         sum_a = payload("swapped", lambda p, a, b: a[p] + b[p], HALF, (fa, got_xa), parts[-1][:1])
         got_y2 = swap_y(sum_a)
-        last = payload(
-            "summed", lambda p, a, b: a[p] + jnp.where(is_inner(), b[HALF + p], 0.0), HALF, (got_y1, gs), [sum_a]
-        )
-        got_last = swap_x(last)
-        parts.append(local_terms(f[LATE:], g[LATE:], [last]))
-        token = [last]
+
+        def summed(start, stop, after):
+            def work(p, got, own):
+                return got[start + p] + jnp.where(is_inner(), own[HALF + start + p], 0.0)
+
+            return payload("summed", work, stop - start, (got_y1, gs), after)
+
+        last = [summed(0, CUT, [sum_a])]
+        got_last = [swap_x(last[0])]
+        parts.append(local_terms(f[LATE:], g[LATE:], last))
+        x1_steps = first_steps(x1, y1, last)
+        last.append(summed(CUT, HALF, [parts[-1][0], x1_steps]))
+        got_last.append(swap_x(last[1]))
         near = [(array, p, INNER) for array in (got_xa, got_xb) for p in range(HALF)]
         far = [((got_y2, p, ALWAYS), (got_xb, p, OUTER)) for p in range(HALF)]
-        far += [((got_y1, p, ALWAYS), (got_last, p, ALWAYS)) for p in range(HALF)]
+        far += [((got_y1, p, ALWAYS), (got_last[p >= CUT], p % CUT, ALWAYS)) for p in range(HALF)]
+        after = last[1:]
     else:
         parts += [local_terms(f[EARLY:LATE], g[EARLY:LATE]), local_terms(f[LATE:], g[LATE:])]
-        token = []
+        x1_steps, after = first_steps(x1, y1, []), []
         near = [(array, p, ALWAYS) for array in [scan_sum(s, size, 1) for s in (fa, fb)] for p in range(HALF)]
         after_me = scan_sum(gs, size, -1)
         far = [((after_me, p, ALWAYS),) for p in range(PAIRS)]
-    x1_steps = first_steps(x1, y1, token)
     f[:HALF] = pairs_of(x1, y1, x1_steps)
     local_of = [(part, p) for part in parts for p in range(part[0].shape[1] // YW)]
 
     def jobs(pairs, side, other, results, terms):
         return [Job(side[p], other[p], local_of[p][0][results], local_of[p][0][results + 1], local_of[p][1], terms(p), p) for p in pairs]
 
-    outs = cross_terms(jobs(range(PAIRS), g, f, 0, lambda p: (near[p],)), True, scale_low, [])
-    for pairs in (range(HALF), range(HALF, PAIRS)):
+    outs = cross_terms(jobs(range(PAIRS), g, f, 0, lambda p: (near[p],)), True, scale_low, [], after)
+    for pairs in ORDER:
         outs = cross_terms(jobs(pairs, f, g, 2, lambda p: far[p]), False, scale_high, outs)
     return tuple(outs)
 

time: 24.7 us -> 24.5 us (level)
  waiting for transfers between devices: 0.92 us -> 0.6 us
    ppermute x1 -> x2, starting transfers between devices: 1.56 us -> 2.15 us  [the longest x1 1.56 us: local(): got_last = [swap_x(last[0])]]
    ppermute x1, starting transfers between devices: 1.95 us -> 1.53 us  [local(): got_y2 = swap_y(sum_a)]
    ppermute x1 -> x2, waiting for transfers between devices: 0.91 us -> 0.59 us  [the longest x1 0.59 us: local(): got_last = [swap_x(last[0])]]
  transfers between devices with their start and end apart: 5 -> 6, of which waited for: 1 -> 1; matrix products, arithmetic and copies ran while one was open for 0% -> 0% of each run, Pallas kernels for 41% -> 42%
where the time goes in v7:
time: 24.5 us; the launch traced here: 24.3 us
  Pallas kernels  13.3 us (54%)
  starting transfers between devices  9.63 us (39%)
  between operations  0.77 us (3%)
  waiting for transfers between devices  0.6 us (2%)
    pallas_call x3, Pallas kernels, cross_terms(): pl.pallas_call(functools.partial(cross_kernel, placed, near, scale_at), i...  5 us
    pallas_call x2, Pallas kernels, local_terms(): pl.pallas_call(functools.partial(local_kernel, places), in_specs=[VMEM] *...  4.27 us
    ppermute x1, starting transfers between devices, local(): got_xa = swap_x(fa)  3 us
    pallas_call x1, Pallas kernels, load(): pl.pallas_call(load_kernel, in_specs=[HBM] * 4, out_specs=[VMEM] * 5, out...  1.84 us
    ppermute x1, starting transfers between devices, local(): got_y1 = swap_y(fb)  1.59 us
    ppermute x1, starting transfers between devices, local(): got_last = [swap_x(last[0])]  1.56 us
    ppermute x1, starting transfers between devices, local(): got_y2 = swap_y(sum_a)  1.53 us
    ppermute x1, starting transfers between devices, local(): got_xb = swap_x(mixed)  1.35 us
  transfers between devices with their start and end apart: 6, of which 1 were waited for; matrix products, arithmetic and copies ran while one was open for 0% of the time, Pallas kernels for 42%

profile of v7, /device:TPU:0, one launch (start us, length us, event | category | flops | bytes accessed | tf_op | source)
XLA Modules:
  0.0 24.3 jit_solution(15841364435635860906)
XLA Ops:
  0.6 0.0 copy-start.1
  0.6 0.0 copy-start
  0.7 0.0 copy-start.3
  0.7 0.0 copy-start.2
  0.7 1.8 %load.1 = (bf16[512,512]{1,0:T(8,128)(2,1)S(1)}, bf16[512,1024]{1,0:T(8,128)(2,1)S(1)}, f32[512,128]{1,0:T(8,128)S(1)}, f32[512,128]{1,0:T(8,128)S(1)}, f32[4,128,128]{2,1,0:T(8,128)S(1)}) custom-call(bf16[512,1024]{1,0:T(8,128)(2,1)} %q.5, bf16[512,1024]{1,0:T(8,128)(2,1)} %k.5, bf16[512,2048]{1,0:T(8,128)(2,1)} %v.5, bf16[512,2048]{1,0:T(8,128)(2,1)} %do.5), custom_call_target="tpu_custom_call" | custom-call | tf_op jit(solution)/shard_map/load/pallas_call | solution.py:199
  2.5 3.0 %collective-permute-start.1 = (f32[4,128,128]{2,1,0:T(8,128)S(1)}, f32[4,128,128]{2,1,0:T(8,128)S(1)}, u32[]{:S(2)}, u32[]{:S(2)}) collective-permute-start(f32[4,128,128]{2,1,0:T(8,128)S(1)} %get-tuple-element.42.refs_0_), channel_id=1, source_target_pairs={{0,1},{1,0},{2,3},{3,2},{4,5},{5,4},{6,7},{7,6},{8,9},{9,8},{10,11... | collective-permute-start | bytes 786440 | tf_op jit(solution)/shard_map/ppermute | solution.py:471
  5.5 0.0 copy-done.1
  5.5 0.0 copy-done
  5.5 0.0 copy-done.3
  5.5 0.0 copy-done.2
  5.5 0.6 %f_states.1 = (bf16[512,512]{1,0:T(8,128)(2,1)S(1)}, bf16[512,1024]{1,0:T(8,128)(2,1)S(1)}, f32[4,4,128,128]{3,2,1,0:T(8,128)S(1)}, f32[4,128,128]{2,1,0:T(8,128)S(1)}) custom-call(bf16[512,1024]{1,0:T(8,128)(2,1)S(1)} %copy-done.2, bf16[512,1024]{1,0:T(8,128)(2,1)S(1)} %copy-done.3, bf16[512,2048]{1,0:T(8,128)(2,1)S(1)} %copy-done, ...), custom_call_target="tpu_custom_call" | custom-call | tf_op jit(solution)/shard_map/f_states/pallas_call | solution.py:224
  6.1 1.6 %collective-permute-start = (f32[4,128,128]{2,1,0:T(8,128)S(1)}, f32[4,128,128]{2,1,0:T(8,128)S(1)}, u32[]{:S(2)}, u32[]{:S(2)}) collective-permute-start(f32[4,128,128]{2,1,0:T(8,128)S(1)} %get-tuple-element.38.refs_1_), channel_id=1, source_target_pairs={{0,2},{2,0},{1,3},{3,1},{4,6},{6,4},{5,7},{7,5},{8,10},{10,8},{9,1... | collective-permute-start | bytes 786440 | tf_op jit(solution)/shard_map/ppermute | solution.py:474
  7.7 1.0 %g_states.1 = (bf16[512,1024]{1,0:T(8,128)(2,1)S(1)}, bf16[512,2048]{1,0:T(8,128)(2,1)S(1)}, f32[8,4,128,128]{3,2,1,0:T(8,128)S(1)}, f32[8,128,128]{2,1,0:T(8,128)S(1)}) custom-call(bf16[512,1024]{1,0:T(8,128)(2,1)S(1)} %copy-done.2, bf16[512,1024]{1,0:T(8,128)(2,1)S(1)} %copy-done.3, bf16[512,2048]{1,0:T(8,128)(2,1)S(1)} %copy-done, ...), custom_call_target="tpu_custom_call" | custom-call | tf_op jit(solution)/shard_map/g_states/pallas_call | solution.py:254
  8.8 1.4 %collective-permute-start.4 = (f32[4,128,128]{2,1,0:T(8,128)S(1)}, f32[4,128,128]{2,1,0:T(8,128)S(1)}, u32[]{:S(2)}, u32[]{:S(2)}) collective-permute-start(f32[4,128,128]{2,1,0:T(8,128)S(1)} %mixed.1.refs_6_), channel_id=1, source_target_pairs={{0,1},{1,0},{2,3},{3,2},{4,5},{5,4},{6,7},{7,6},{8,9},{9,8},{10,11... | collective-permute-start | bytes 786440 | tf_op jit(solution)/shard_map/ppermute | solution.py:484
  10.1 3.1 %local.2 = (f32[512,1536]{1,0:T(8,128)S(1)}, f32[512,768]{1,0:T(8,128)S(1)}, f32[512,1536]{1,0:T(8,128)S(1)}, f32[512,768]{1,0:T(8,128)S(1)}) custom-call(bf16[512,512]{1,0:T(8,128)(2,1)S(1)} %get-tuple-element.43.refs_0_.x.refs_1_, bf16[512,1024]{1,0:T(8,128)(2,1)S(1)} %get-tuple-element.44.refs_1_.y.refs_2_, ...), custom_call_target="tpu_custom_call" | custom-call | tf_op jit(solution)/shard_map/local/pallas_call | solution.py:365
  13.3 0.0 collective-permute-done.1.refs_1_.refs_4_
  13.3 1.5 %collective-permute-start.3 = (f32[4,128,128]{2,1,0:T(8,128)S(1)}, f32[4,128,128]{2,1,0:T(8,128)S(1)}, u32[]{:S(2)}, u32[]{:S(2)}) collective-permute-start(f32[4,128,128]{2,1,0:T(8,128)S(1)} %swapped.1.refs_2_), channel_id=1, source_target_pairs={{0,2},{2,0},{1,3},{3,1},{4,6},{6,4},{5,7},{7,5},{8,10},{10,8},{9,1... | collective-permute-start | bytes 786440 | tf_op jit(solution)/shard_map/ppermute | solution.py:487
  14.8 0.0 collective-permute-done.refs_0_.refs_10_.refs_4_
  14.9 1.6 %collective-permute-start.5 = (f32[2,128,128]{2,1,0:T(8,128)S(1)}, f32[2,128,128]{2,1,0:T(8,128)S(1)}, u32[]{:S(2)}, u32[]{:S(2)}) collective-permute-start(f32[2,128,128]{2,1,0:T(8,128)S(1)} %summed.2.refs_4_.refs_0_), channel_id=1, source_target_pairs={{0,1},{1,0},{2,3},{3,2},{4,5},{5,4},{6,7},{7,6},{8,9},{9,8},{10,11... | collective-permute-start | bytes 393224 | tf_op jit(solution)/shard_map/ppermute | solution.py:496
  16.4 0.5 %first_steps.1.refs_3_ = f32[4,4,128,128]{3,2,1,0:T(8,128)S(1)} custom-call(bf16[512,512]{1,0:T(8,128)(2,1)S(1)} %get-tuple-element.43.refs_0_.x.refs_1_, bf16[512,1024]{1,0:T(8,128)(2,1)S(1)} %get-tuple-element.44.refs_1_.y.refs_2_, f32[2,128,128]{2,1,0:T(8,128)S(1)} %summed.2.refs_4_.refs_0_), custom_call_target="tpu_custom_call" | custom-call | tf_op jit(solution)/shard_map/first_steps/pallas_call | solution.py:270
  16.9 1.1 %local.3 = (f32[512,512]{1,0:T(8,128)S(1)}, f32[512,256]{1,0:T(8,128)S(1)}, f32[512,512]{1,0:T(8,128)S(1)}, f32[512,256]{1,0:T(8,128)S(1)}) custom-call(bf16[512,512]{1,0:T(8,128)(2,1)S(1)} %get-tuple-element.34.refs_4_.refs_0_.refs_8_.refs_1_, bf16[512,1024]{1,0:T(8,128)(2,1)S(1)} %get-tuple-element.35.refs_5_.refs_1_.refs_9_.refs_2_, ...), custom_call_target="tpu_custom_call" | custom-call | tf_op jit(solution)/shard_map/local/pallas_call | solution.py:365
  18.1 0.6 %collective-permute-start.2 = (f32[2,128,128]{2,1,0:T(8,128)S(1)}, f32[2,128,128]{2,1,0:T(8,128)S(1)}, u32[]{:S(2)}, u32[]{:S(2)}) collective-permute-start(f32[2,128,128]{2,1,0:T(8,128)S(1)} %summed.3.refs_11_), channel_id=1, source_target_pairs={{0,1},{1,0},{2,3},{3,2},{4,5},{5,4},{6,7},{7,6},{8,9},{9,8},{10,11... | collective-permute-start | bytes 393224 | tf_op jit(solution)/shard_map/ppermute | solution.py:500
  18.7 0.0 collective-permute-done.4.refs_8_.refs_5_
  18.7 2.1 %near.1 = (bf16[512,2048]{1,0:T(8,128)(2,1)}, bf16[512,1024]{1,0:T(8,128)(2,1)}, bf16[512,1024]{1,0:T(8,128)(2,1)}, bf16[512,2048]{1,0:T(8,128)(2,1)}) custom-call(f32[512,128]{1,0:T(8,128)S(1)} %get-tuple-element.36.scale.refs_0_, bf16[512,1024]{1,0:T(8,128)(2,1)S(1)} %get-tuple-element.40.refs_2_.refs_1_, ...), custom_call_target="tpu_custom_call" | custom-call | tf_op jit(solution)/shard_map/near/pallas_call | solution.py:437
  20.8 0.6 %collective-permute-done.5.refs_11_ = f32[2,128,128]{2,1,0:T(8,128)S(1)} collective-permute-done((f32[2,128,128]{2,1,0:T(8,128)S(1)}, f32[2,128,128]{2,1,0:T(8,128)S(1)}, u32[]{:S(2)}, u32[]{:S(2)}) %collective-permute-start.5) | collective-permute-done | bytes 131104 | tf_op jit(solution)/shard_map/ppermute | solution.py:496
  21.4 0.0 collective-permute-done.3.refs_4_
  21.4 1.8 %far.2 = (bf16[512,2048]{1,0:T(8,128)(2,1)}, bf16[512,1024]{1,0:T(8,128)(2,1)}, bf16[512,1024]{1,0:T(8,128)(2,1)}, bf16[512,2048]{1,0:T(8,128)(2,1)}) custom-call(f32[512,128]{1,0:T(8,128)S(1)} %get-tuple-element.33.scale.refs_0_, ...), custom_call_target="tpu_custom_call", output_to_operand_aliasing={{0}: (12, {}), {1}: (13, {}), {2}: (14, {}), {3}: (15, {})} | custom-call | tf_op jit(solution)/shard_map/far/pallas_call | solution.py:437
  23.2 0.0 collective-permute-done.2.refs_5_
  23.2 1.1 %far.3 = (bf16[512,2048]{1,0:T(8,128)(2,1)}, bf16[512,1024]{1,0:T(8,128)(2,1)}, bf16[512,1024]{1,0:T(8,128)(2,1)}, bf16[512,2048]{1,0:T(8,128)(2,1)}) custom-call(f32[512,128]{1,0:T(8,128)S(1)} %get-tuple-element.33.scale.refs_0_, ...), custom_call_target="tpu_custom_call", output_to_operand_aliasing={{0}: (8, {}), {1}: (9, {}), {2}: (10, {}), {3}: (11, {})} | custom-call | tf_op jit(solution)/shard_map/far/pallas_call | solution.py:437
  (4 shorter events, 0.1 us)
Async XLA Ops:
  0.6 4.9 %copy-start.1 = (bf16[512,2048]{1,0:T(8,128)(2,1)S(1)}, bf16[512,2048]{1,0:T(8,128)(2,1)}, u32[]{:S(2)}) copy-start(bf16[512,2048]{1,0:T(8,128)(2,1)} %do.5) | copy-start | bytes 6291460
  0.6 4.9 %copy-start = (bf16[512,2048]{1,0:T(8,128)(2,1)S(1)}, bf16[512,2048]{1,0:T(8,128)(2,1)}, u32[]{:S(2)}) copy-start(bf16[512,2048]{1,0:T(8,128)(2,1)} %v.5) | copy-start | bytes 6291460
  0.7 4.9 %copy-start.3 = (bf16[512,1024]{1,0:T(8,128)(2,1)S(1)}, bf16[512,1024]{1,0:T(8,128)(2,1)}, u32[]{:S(2)}) copy-start(bf16[512,1024]{1,0:T(8,128)(2,1)} %k.5) | copy-start | bytes 3145732
  0.7 4.9 %copy-start.2 = (bf16[512,1024]{1,0:T(8,128)(2,1)S(1)}, bf16[512,1024]{1,0:T(8,128)(2,1)}, u32[]{:S(2)}) copy-start(bf16[512,1024]{1,0:T(8,128)(2,1)} %q.5) | copy-start | bytes 3145732
  2.5 10.8 %collective-permute-start.1 = (f32[4,128,128]{2,1,0:T(8,128)S(1)}, f32[4,128,128]{2,1,0:T(8,128)S(1)}, u32[]{:S(2)}, u32[]{:S(2)}) collective-permute-start(f32[4,128,128]{2,1,0:T(8,128)S(1)} %get-tuple-element.42.refs_0_), channel_id=1, source_target_pairs={{0,1},{1,0},{2,3},{3,2},{4,5},{5,4},{6,7},{7,6},{8,9},{9,8},{10,11... | collective-permute-start | bytes 786440 | tf_op jit(solution)/shard_map/ppermute | solution.py:471
  6.1 8.8 %collective-permute-start = (f32[4,128,128]{2,1,0:T(8,128)S(1)}, f32[4,128,128]{2,1,0:T(8,128)S(1)}, u32[]{:S(2)}, u32[]{:S(2)}) collective-permute-start(f32[4,128,128]{2,1,0:T(8,128)S(1)} %get-tuple-element.38.refs_1_), channel_id=1, source_target_pairs={{0,2},{2,0},{1,3},{3,1},{4,6},{6,4},{5,7},{7,5},{8,10},{10,8},{9,1... | collective-permute-start | bytes 786440 | tf_op jit(solution)/shard_map/ppermute | solution.py:474
  8.8 9.9 %collective-permute-start.4 = (f32[4,128,128]{2,1,0:T(8,128)S(1)}, f32[4,128,128]{2,1,0:T(8,128)S(1)}, u32[]{:S(2)}, u32[]{:S(2)}) collective-permute-start(f32[4,128,128]{2,1,0:T(8,128)S(1)} %mixed.1.refs_6_), channel_id=1, source_target_pairs={{0,1},{1,0},{2,3},{3,2},{4,5},{5,4},{6,7},{7,6},{8,9},{9,8},{10,11... | collective-permute-start | bytes 786440 | tf_op jit(solution)/shard_map/ppermute | solution.py:484
  13.3 8.1 %collective-permute-start.3 = (f32[4,128,128]{2,1,0:T(8,128)S(1)}, f32[4,128,128]{2,1,0:T(8,128)S(1)}, u32[]{:S(2)}, u32[]{:S(2)}) collective-permute-start(f32[4,128,128]{2,1,0:T(8,128)S(1)} %swapped.1.refs_2_), channel_id=1, source_target_pairs={{0,2},{2,0},{1,3},{3,1},{4,6},{6,4},{5,7},{7,5},{8,10},{10,8},{9,1... | collective-permute-start | bytes 786440 | tf_op jit(solution)/shard_map/ppermute | solution.py:487
  14.9 6.5 %collective-permute-start.5 = (f32[2,128,128]{2,1,0:T(8,128)S(1)}, f32[2,128,128]{2,1,0:T(8,128)S(1)}, u32[]{:S(2)}, u32[]{:S(2)}) collective-permute-start(f32[2,128,128]{2,1,0:T(8,128)S(1)} %summed.2.refs_4_.refs_0_), channel_id=1, source_target_pairs={{0,1},{1,0},{2,3},{3,2},{4,5},{5,4},{6,7},{7,6},{8,9},{9,8},{10,11... | collective-permute-start | bytes 393224 | tf_op jit(solution)/shard_map/ppermute | solution.py:496
  18.1 5.1 %collective-permute-start.2 = (f32[2,128,128]{2,1,0:T(8,128)S(1)}, f32[2,128,128]{2,1,0:T(8,128)S(1)}, u32[]{:S(2)}, u32[]{:S(2)}) collective-permute-start(f32[2,128,128]{2,1,0:T(8,128)S(1)} %summed.3.refs_11_), channel_id=1, source_target_pairs={{0,1},{1,0},{2,3},{3,2},{4,5},{5,4},{6,7},{7,6},{8,9},{9,8},{10,11... | collective-permute-start | bytes 393224 | tf_op jit(solution)/shard_map/ppermute | solution.py:500

commit v8 on v7

--- a/solution.py
+++ b/solution.py
@@ -17,7 +17,7 @@
 XW = 2 * DK
 YW = 2 * DV
 CHUNK = 128
-PIECE = 256
+PARTS = 2
 FIRST = HALF
 EARLY = 0
 LATE = 6
@@ -161,15 +161,16 @@
 def load_kernel(q, k, v, do, x, y, scale_low, scale_high, state, raw, sems):
     low = is_low()
     length = q.shape[0]
-    pieces = chunks_of(q, PIECE)
+    count = FIRST // PARTS
 
     def copies(a, b):
         return [
             (
-                pltpu.make_async_copy(a.at[rows, pl.ds(0, FIRST * XW)], x.at[rows, :], sems.at[0, c]),
-                pltpu.make_async_copy(b.at[rows, pl.ds(0, FIRST * YW)], raw.at[rows, :], sems.at[1, c]),
+                pltpu.make_async_copy(a.at[:, narrow], x.at[:, narrow], sems.at[0, c]),
+                pltpu.make_async_copy(b.at[:, wide], raw.at[:, wide], sems.at[1, c]),
             )
-            for c, rows in enumerate(pieces)
+            for c in range(PARTS)
+            for narrow, wide in [(pl.ds(c * count * XW, count * XW), pl.ds(c * count * YW, count * YW))]
         ]
 
     def start(a, b):
@@ -182,14 +183,12 @@
     scale = 1.0 / jnp.sqrt(DK * (at.astype(F32) + 1.0))
     scale_low[...] = jnp.where(low, scale, 1.0)
     scale_high[...] = jnp.where(low, 1.0, scale)
-    total = None
-    for rows, pair in zip(pieces, copies(k, v)):
+    for c, pair in enumerate(copies(k, v)):
         for copy in pair:
             copy.wait()
-        parts = chunk_states(x, raw, 0, FIRST, y, scale_high, rows)
-        total = parts if total is None else [a + b for a, b in zip(total, parts)]
-    for p, new in enumerate(total):
-        state[p] = new
+        target = y.at[:, pl.ds(c * count * YW, count * YW)]
+        for p, new in enumerate(chunk_states(x, raw, c * count, count, target, scale_high, slice(0, length))):
+            state[c * count + p] = new
 
 
 def load(q, k, v, do):
@@ -201,7 +200,7 @@
         in_specs=[HBM] * 4,
         out_specs=[VMEM] * 5,
         out_shape=[x, y, scale, scale, states_shape(FIRST)],
-        scratch_shapes=[y, pltpu.SemaphoreType.DMA((2, length // PIECE))],
+        scratch_shapes=[y, pltpu.SemaphoreType.DMA((2, PARTS))],
         compiler_params=params(),
         name="load",
     )(*map(in_hbm, (q, k, v, do)))

time: 24.5 us -> 24.5 us (level)
  no operation moved by 1% of the time
where the time goes in v8:
time: 24.5 us; the launch traced here: 24.4 us
  Pallas kernels  13.3 us (54%)
  starting transfers between devices  9.64 us (39%)
  between operations  0.77 us (3%)
  waiting for transfers between devices  0.6 us (2%)
    pallas_call x3, Pallas kernels, cross_terms(): pl.pallas_call(functools.partial(cross_kernel, placed, near, scale_at), i...  5 us
    pallas_call x2, Pallas kernels, local_terms(): pl.pallas_call(functools.partial(local_kernel, places), in_specs=[VMEM] *...  4.27 us
    ppermute x1, starting transfers between devices, local(): got_xa = swap_x(fa)  3 us
    pallas_call x1, Pallas kernels, load(): pl.pallas_call(load_kernel, in_specs=[HBM] * 4, out_specs=[VMEM] * 5, out...  1.91 us
    ppermute x1, starting transfers between devices, local(): got_y1 = swap_y(fb)  1.6 us
    ppermute x1, starting transfers between devices, local(): got_y2 = swap_y(sum_a)  1.58 us
    ppermute x1, starting transfers between devices, local(): got_last = [swap_x(last[0])]  1.56 us
    ppermute x1, starting transfers between devices, local(): got_xb = swap_x(mixed)  1.3 us
  transfers between devices with their start and end apart: 6, of which 1 were waited for; matrix products, arithmetic and copies ran while one was open for 0% of the time, Pallas kernels for 42%

profile of v8, /device:TPU:0, one launch (start us, length us, event | category | flops | bytes accessed | tf_op | source)
XLA Modules:
  0.0 24.4 jit_solution(3893850102549163083)
XLA Ops:
  0.6 0.0 copy-start.1
  0.6 0.0 copy-start
  0.7 0.0 copy-start.3
  0.7 0.0 copy-start.2
  0.7 1.9 %load.1 = (bf16[512,512]{1,0:T(8,128)(2,1)S(1)}, bf16[512,1024]{1,0:T(8,128)(2,1)S(1)}, f32[512,128]{1,0:T(8,128)S(1)}, f32[512,128]{1,0:T(8,128)S(1)}, f32[4,128,128]{2,1,0:T(8,128)S(1)}) custom-call(bf16[512,1024]{1,0:T(8,128)(2,1)} %q.5, bf16[512,1024]{1,0:T(8,128)(2,1)} %k.5, bf16[512,2048]{1,0:T(8,128)(2,1)} %v.5, bf16[512,2048]{1,0:T(8,128)(2,1)} %do.5), custom_call_target="tpu_custom_call" | custom-call | tf_op jit(solution)/shard_map/load/pallas_call | solution.py:198
  2.6 3.0 %collective-permute-start.1 = (f32[4,128,128]{2,1,0:T(8,128)S(1)}, f32[4,128,128]{2,1,0:T(8,128)S(1)}, u32[]{:S(2)}, u32[]{:S(2)}) collective-permute-start(f32[4,128,128]{2,1,0:T(8,128)S(1)} %get-tuple-element.42.refs_0_), channel_id=1, source_target_pairs={{0,1},{1,0},{2,3},{3,2},{4,5},{5,4},{6,7},{7,6},{8,9},{9,8},{10,11... | collective-permute-start | bytes 786440 | tf_op jit(solution)/shard_map/ppermute | solution.py:470
  5.6 0.0 copy-done.1
  5.6 0.0 copy-done
  5.6 0.0 copy-done.3
  5.6 0.0 copy-done.2
  5.6 0.6 %f_states.1 = (bf16[512,512]{1,0:T(8,128)(2,1)S(1)}, bf16[512,1024]{1,0:T(8,128)(2,1)S(1)}, f32[4,4,128,128]{3,2,1,0:T(8,128)S(1)}, f32[4,128,128]{2,1,0:T(8,128)S(1)}) custom-call(bf16[512,1024]{1,0:T(8,128)(2,1)S(1)} %copy-done.2, bf16[512,1024]{1,0:T(8,128)(2,1)S(1)} %copy-done.3, bf16[512,2048]{1,0:T(8,128)(2,1)S(1)} %copy-done, ...), custom_call_target="tpu_custom_call" | custom-call | tf_op jit(solution)/shard_map/f_states/pallas_call | solution.py:223
  6.2 1.6 %collective-permute-start = (f32[4,128,128]{2,1,0:T(8,128)S(1)}, f32[4,128,128]{2,1,0:T(8,128)S(1)}, u32[]{:S(2)}, u32[]{:S(2)}) collective-permute-start(f32[4,128,128]{2,1,0:T(8,128)S(1)} %get-tuple-element.38.refs_1_), channel_id=1, source_target_pairs={{0,2},{2,0},{1,3},{3,1},{4,6},{6,4},{5,7},{7,5},{8,10},{10,8},{9,1... | collective-permute-start | bytes 786440 | tf_op jit(solution)/shard_map/ppermute | solution.py:473
  7.8 1.0 %g_states.1 = (bf16[512,1024]{1,0:T(8,128)(2,1)S(1)}, bf16[512,2048]{1,0:T(8,128)(2,1)S(1)}, f32[8,4,128,128]{3,2,1,0:T(8,128)S(1)}, f32[8,128,128]{2,1,0:T(8,128)S(1)}) custom-call(bf16[512,1024]{1,0:T(8,128)(2,1)S(1)} %copy-done.2, bf16[512,1024]{1,0:T(8,128)(2,1)S(1)} %copy-done.3, bf16[512,2048]{1,0:T(8,128)(2,1)S(1)} %copy-done, ...), custom_call_target="tpu_custom_call" | custom-call | tf_op jit(solution)/shard_map/g_states/pallas_call | solution.py:253
  8.9 1.3 %collective-permute-start.4 = (f32[4,128,128]{2,1,0:T(8,128)S(1)}, f32[4,128,128]{2,1,0:T(8,128)S(1)}, u32[]{:S(2)}, u32[]{:S(2)}) collective-permute-start(f32[4,128,128]{2,1,0:T(8,128)S(1)} %mixed.1.refs_6_), channel_id=1, source_target_pairs={{0,1},{1,0},{2,3},{3,2},{4,5},{5,4},{6,7},{7,6},{8,9},{9,8},{10,11... | collective-permute-start | bytes 786440 | tf_op jit(solution)/shard_map/ppermute | solution.py:483
  10.2 3.1 %local.2 = (f32[512,1536]{1,0:T(8,128)S(1)}, f32[512,768]{1,0:T(8,128)S(1)}, f32[512,1536]{1,0:T(8,128)S(1)}, f32[512,768]{1,0:T(8,128)S(1)}) custom-call(bf16[512,512]{1,0:T(8,128)(2,1)S(1)} %get-tuple-element.43.refs_0_.x.refs_1_, bf16[512,1024]{1,0:T(8,128)(2,1)S(1)} %get-tuple-element.44.refs_1_.y.refs_2_, ...), custom_call_target="tpu_custom_call" | custom-call | tf_op jit(solution)/shard_map/local/pallas_call | solution.py:364
  13.3 0.0 collective-permute-done.1.refs_1_.refs_4_
  13.3 1.6 %collective-permute-start.3 = (f32[4,128,128]{2,1,0:T(8,128)S(1)}, f32[4,128,128]{2,1,0:T(8,128)S(1)}, u32[]{:S(2)}, u32[]{:S(2)}) collective-permute-start(f32[4,128,128]{2,1,0:T(8,128)S(1)} %swapped.1.refs_2_), channel_id=1, source_target_pairs={{0,2},{2,0},{1,3},{3,1},{4,6},{6,4},{5,7},{7,5},{8,10},{10,8},{9,1... | collective-permute-start | bytes 786440 | tf_op jit(solution)/shard_map/ppermute | solution.py:486
  14.9 0.0 collective-permute-done.refs_0_.refs_10_.refs_4_
  14.9 1.6 %collective-permute-start.5 = (f32[2,128,128]{2,1,0:T(8,128)S(1)}, f32[2,128,128]{2,1,0:T(8,128)S(1)}, u32[]{:S(2)}, u32[]{:S(2)}) collective-permute-start(f32[2,128,128]{2,1,0:T(8,128)S(1)} %summed.2.refs_4_.refs_0_), channel_id=1, source_target_pairs={{0,1},{1,0},{2,3},{3,2},{4,5},{5,4},{6,7},{7,6},{8,9},{9,8},{10,11... | collective-permute-start | bytes 393224 | tf_op jit(solution)/shard_map/ppermute | solution.py:495
  16.5 0.5 %first_steps.1.refs_3_ = f32[4,4,128,128]{3,2,1,0:T(8,128)S(1)} custom-call(bf16[512,512]{1,0:T(8,128)(2,1)S(1)} %get-tuple-element.43.refs_0_.x.refs_1_, bf16[512,1024]{1,0:T(8,128)(2,1)S(1)} %get-tuple-element.44.refs_1_.y.refs_2_, f32[2,128,128]{2,1,0:T(8,128)S(1)} %summed.2.refs_4_.refs_0_), custom_call_target="tpu_custom_call" | custom-call | tf_op jit(solution)/shard_map/first_steps/pallas_call | solution.py:269
  17.0 1.1 %local.3 = (f32[512,512]{1,0:T(8,128)S(1)}, f32[512,256]{1,0:T(8,128)S(1)}, f32[512,512]{1,0:T(8,128)S(1)}, f32[512,256]{1,0:T(8,128)S(1)}) custom-call(bf16[512,512]{1,0:T(8,128)(2,1)S(1)} %get-tuple-element.34.refs_4_.refs_0_.refs_8_.refs_1_, bf16[512,1024]{1,0:T(8,128)(2,1)S(1)} %get-tuple-element.35.refs_5_.refs_1_.refs_9_.refs_2_, ...), custom_call_target="tpu_custom_call" | custom-call | tf_op jit(solution)/shard_map/local/pallas_call | solution.py:364
  18.2 0.6 %collective-permute-start.2 = (f32[2,128,128]{2,1,0:T(8,128)S(1)}, f32[2,128,128]{2,1,0:T(8,128)S(1)}, u32[]{:S(2)}, u32[]{:S(2)}) collective-permute-start(f32[2,128,128]{2,1,0:T(8,128)S(1)} %summed.3.refs_11_), channel_id=1, source_target_pairs={{0,1},{1,0},{2,3},{3,2},{4,5},{5,4},{6,7},{7,6},{8,9},{9,8},{10,11... | collective-permute-start | bytes 393224 | tf_op jit(solution)/shard_map/ppermute | solution.py:499
  18.8 0.0 collective-permute-done.4.refs_8_.refs_5_
  18.8 2.1 %near.1 = (bf16[512,2048]{1,0:T(8,128)(2,1)}, bf16[512,1024]{1,0:T(8,128)(2,1)}, bf16[512,1024]{1,0:T(8,128)(2,1)}, bf16[512,2048]{1,0:T(8,128)(2,1)}) custom-call(f32[512,128]{1,0:T(8,128)S(1)} %get-tuple-element.36.scale.refs_0_, bf16[512,1024]{1,0:T(8,128)(2,1)S(1)} %get-tuple-element.40.refs_2_.refs_1_, ...), custom_call_target="tpu_custom_call" | custom-call | tf_op jit(solution)/shard_map/near/pallas_call | solution.py:436
  20.9 0.6 %collective-permute-done.5.refs_11_ = f32[2,128,128]{2,1,0:T(8,128)S(1)} collective-permute-done((f32[2,128,128]{2,1,0:T(8,128)S(1)}, f32[2,128,128]{2,1,0:T(8,128)S(1)}, u32[]{:S(2)}, u32[]{:S(2)}) %collective-permute-start.5) | collective-permute-done | bytes 131104 | tf_op jit(solution)/shard_map/ppermute | solution.py:495
  21.4 0.0 collective-permute-done.3.refs_4_
  21.4 1.8 %far.2 = (bf16[512,2048]{1,0:T(8,128)(2,1)}, bf16[512,1024]{1,0:T(8,128)(2,1)}, bf16[512,1024]{1,0:T(8,128)(2,1)}, bf16[512,2048]{1,0:T(8,128)(2,1)}) custom-call(f32[512,128]{1,0:T(8,128)S(1)} %get-tuple-element.33.scale.refs_0_, ...), custom_call_target="tpu_custom_call", output_to_operand_aliasing={{0}: (12, {}), {1}: (13, {}), {2}: (14, {}), {3}: (15, {})} | custom-call | tf_op jit(solution)/shard_map/far/pallas_call | solution.py:436
  23.2 0.0 collective-permute-done.2.refs_5_
  23.2 1.1 %far.3 = (bf16[512,2048]{1,0:T(8,128)(2,1)}, bf16[512,1024]{1,0:T(8,128)(2,1)}, bf16[512,1024]{1,0:T(8,128)(2,1)}, bf16[512,2048]{1,0:T(8,128)(2,1)}) custom-call(f32[512,128]{1,0:T(8,128)S(1)} %get-tuple-element.33.scale.refs_0_, ...), custom_call_target="tpu_custom_call", output_to_operand_aliasing={{0}: (8, {}), {1}: (9, {}), {2}: (10, {}), {3}: (11, {})} | custom-call | tf_op jit(solution)/shard_map/far/pallas_call | solution.py:436
  (4 shorter events, 0.1 us)
Async XLA Ops:
  0.6 5.0 %copy-start.1 = (bf16[512,2048]{1,0:T(8,128)(2,1)S(1)}, bf16[512,2048]{1,0:T(8,128)(2,1)}, u32[]{:S(2)}) copy-start(bf16[512,2048]{1,0:T(8,128)(2,1)} %do.5) | copy-start | bytes 6291460
  0.6 5.0 %copy-start = (bf16[512,2048]{1,0:T(8,128)(2,1)S(1)}, bf16[512,2048]{1,0:T(8,128)(2,1)}, u32[]{:S(2)}) copy-start(bf16[512,2048]{1,0:T(8,128)(2,1)} %v.5) | copy-start | bytes 6291460
  0.7 4.9 %copy-start.3 = (bf16[512,1024]{1,0:T(8,128)(2,1)S(1)}, bf16[512,1024]{1,0:T(8,128)(2,1)}, u32[]{:S(2)}) copy-start(bf16[512,1024]{1,0:T(8,128)(2,1)} %k.5) | copy-start | bytes 3145732
  0.7 4.9 %copy-start.2 = (bf16[512,1024]{1,0:T(8,128)(2,1)S(1)}, bf16[512,1024]{1,0:T(8,128)(2,1)}, u32[]{:S(2)}) copy-start(bf16[512,1024]{1,0:T(8,128)(2,1)} %q.5) | copy-start | bytes 3145732
  2.6 10.7 %collective-permute-start.1 = (f32[4,128,128]{2,1,0:T(8,128)S(1)}, f32[4,128,128]{2,1,0:T(8,128)S(1)}, u32[]{:S(2)}, u32[]{:S(2)}) collective-permute-start(f32[4,128,128]{2,1,0:T(8,128)S(1)} %get-tuple-element.42.refs_0_), channel_id=1, source_target_pairs={{0,1},{1,0},{2,3},{3,2},{4,5},{5,4},{6,7},{7,6},{8,9},{9,8},{10,11... | collective-permute-start | bytes 786440 | tf_op jit(solution)/shard_map/ppermute | solution.py:470
  6.2 8.8 %collective-permute-start = (f32[4,128,128]{2,1,0:T(8,128)S(1)}, f32[4,128,128]{2,1,0:T(8,128)S(1)}, u32[]{:S(2)}, u32[]{:S(2)}) collective-permute-start(f32[4,128,128]{2,1,0:T(8,128)S(1)} %get-tuple-element.38.refs_1_), channel_id=1, source_target_pairs={{0,2},{2,0},{1,3},{3,1},{4,6},{6,4},{5,7},{7,5},{8,10},{10,8},{9,1... | collective-permute-start | bytes 786440 | tf_op jit(solution)/shard_map/ppermute | solution.py:473
  8.9 9.9 %collective-permute-start.4 = (f32[4,128,128]{2,1,0:T(8,128)S(1)}, f32[4,128,128]{2,1,0:T(8,128)S(1)}, u32[]{:S(2)}, u32[]{:S(2)}) collective-permute-start(f32[4,128,128]{2,1,0:T(8,128)S(1)} %mixed.1.refs_6_), channel_id=1, source_target_pairs={{0,1},{1,0},{2,3},{3,2},{4,5},{5,4},{6,7},{7,6},{8,9},{9,8},{10,11... | collective-permute-start | bytes 786440 | tf_op jit(solution)/shard_map/ppermute | solution.py:483
  13.3 8.1 %collective-permute-start.3 = (f32[4,128,128]{2,1,0:T(8,128)S(1)}, f32[4,128,128]{2,1,0:T(8,128)S(1)}, u32[]{:S(2)}, u32[]{:S(2)}) collective-permute-start(f32[4,128,128]{2,1,0:T(8,128)S(1)} %swapped.1.refs_2_), channel_id=1, source_target_pairs={{0,2},{2,0},{1,3},{3,1},{4,6},{6,4},{5,7},{7,5},{8,10},{10,8},{9,1... | collective-permute-start | bytes 786440 | tf_op jit(solution)/shard_map/ppermute | solution.py:486
  14.9 6.5 %collective-permute-start.5 = (f32[2,128,128]{2,1,0:T(8,128)S(1)}, f32[2,128,128]{2,1,0:T(8,128)S(1)}, u32[]{:S(2)}, u32[]{:S(2)}) collective-permute-start(f32[2,128,128]{2,1,0:T(8,128)S(1)} %summed.2.refs_4_.refs_0_), channel_id=1, source_target_pairs={{0,1},{1,0},{2,3},{3,2},{4,5},{5,4},{6,7},{7,6},{8,9},{9,8},{10,11... | collective-permute-start | bytes 393224 | tf_op jit(solution)/shard_map/ppermute | solution.py:495
  18.2 5.1 %collective-permute-start.2 = (f32[2,128,128]{2,1,0:T(8,128)S(1)}, f32[2,128,128]{2,1,0:T(8,128)S(1)}, u32[]{:S(2)}, u32[]{:S(2)}) collective-permute-start(f32[2,128,128]{2,1,0:T(8,128)S(1)} %summed.3.refs_11_), channel_id=1, source_target_pairs={{0,1},{1,0},{2,3},{3,2},{4,5},{5,4},{6,7},{7,6},{8,9},{9,8},{10,11... | collective-permute-start | bytes 393224 | tf_op jit(solution)/shard_map/ppermute | solution.py:499

commit v9 on v7

--- a/solution.py
+++ b/solution.py
@@ -20,7 +20,7 @@
 PIECE = 256
 FIRST = HALF
 EARLY = 0
-LATE = 6
+LATE = 7
 CUT = 2
 ORDER = range(HALF + CUT), range(HALF + CUT, PAIRS)
 VMEM_LIMIT = 12 * 1024 * 1024

time: 24.5 us -> 24.4 us (level)
  starting transfers between devices: 9.63 us -> 9.12 us
  waiting for transfers between devices: 0.6 us -> 1.11 us
    ppermute x1, starting transfers between devices: 1.53 us -> 1.01 us  [local(): got_y2 = swap_y(sum_a)]
    ppermute x1, waiting for transfers between devices: 0.59 us -> 1.01 us  [local(): got_last = [swap_x(last[0])]]
  transfers between devices with their start and end apart: 6 -> 6, of which waited for: 1 -> 2; matrix products, arithmetic and copies ran while one was open for 0% -> 0% of each run, Pallas kernels for 42% -> 42%
where the time goes in v9:
time: 24.4 us; the launch traced here: 24.3 us
  Pallas kernels  13.3 us (55%)
  starting transfers between devices  9.12 us (37%)
  waiting for transfers between devices  1.11 us (5%)
  between operations  0.77 us (3%)
    pallas_call x3, Pallas kernels, cross_terms(): pl.pallas_call(functools.partial(cross_kernel, placed, near, scale_at), i...  4.98 us
    pallas_call x2, Pallas kernels, local_terms(): pl.pallas_call(functools.partial(local_kernel, places), in_specs=[VMEM] *...  4.29 us
    ppermute x1, starting transfers between devices, local(): got_xa = swap_x(fa)  3 us
    pallas_call x1, Pallas kernels, load(): pl.pallas_call(load_kernel, in_specs=[HBM] * 4, out_specs=[VMEM] * 5, out...  1.84 us
    ppermute x1, starting transfers between devices, local(): got_y1 = swap_y(fb)  1.59 us
    ppermute x1, starting transfers between devices, local(): got_last = [swap_x(last[0])]  1.56 us
    ppermute x1, starting transfers between devices, local(): got_xb = swap_x(mixed)  1.35 us
    pallas_call x1, Pallas kernels, g_states(): pl.pallas_call(g_kernel, in_specs=[VMEM] * 5, out_specs=[VMEM] * 4, out_s...  1.04 us
  transfers between devices with their start and end apart: 6, of which 2 were waited for; matrix products, arithmetic and copies ran while one was open for 0% of the time, Pallas kernels for 42%

profile of v9, /device:TPU:0, one launch (start us, length us, event | category | flops | bytes accessed | tf_op | source)
XLA Modules:
  0.0 24.3 jit_solution(6238492581540999362)
XLA Ops:
  0.6 0.0 copy-start.1
  0.6 0.0 copy-start
  0.7 0.0 copy-start.3
  0.7 0.0 copy-start.2
  0.7 1.8 %load.1 = (bf16[512,512]{1,0:T(8,128)(2,1)S(1)}, bf16[512,1024]{1,0:T(8,128)(2,1)S(1)}, f32[512,128]{1,0:T(8,128)S(1)}, f32[512,128]{1,0:T(8,128)S(1)}, f32[4,128,128]{2,1,0:T(8,128)S(1)}) custom-call(bf16[512,1024]{1,0:T(8,128)(2,1)} %q.5, bf16[512,1024]{1,0:T(8,128)(2,1)} %k.5, bf16[512,2048]{1,0:T(8,128)(2,1)} %v.5, bf16[512,2048]{1,0:T(8,128)(2,1)} %do.5), custom_call_target="tpu_custom_call" | custom-call | tf_op jit(solution)/shard_map/load/pallas_call | solution.py:199
  2.5 3.0 %collective-permute-start.1 = (f32[4,128,128]{2,1,0:T(8,128)S(1)}, f32[4,128,128]{2,1,0:T(8,128)S(1)}, u32[]{:S(2)}, u32[]{:S(2)}) collective-permute-start(f32[4,128,128]{2,1,0:T(8,128)S(1)} %get-tuple-element.42.refs_0_), channel_id=1, source_target_pairs={{0,1},{1,0},{2,3},{3,2},{4,5},{5,4},{6,7},{7,6},{8,9},{9,8},{10,11... | collective-permute-start | bytes 786440 | tf_op jit(solution)/shard_map/ppermute | solution.py:471
  5.5 0.0 copy-done.1
  5.5 0.0 copy-done
  5.5 0.0 copy-done.3
  5.5 0.0 copy-done.2
  5.5 0.6 %f_states.1 = (bf16[512,512]{1,0:T(8,128)(2,1)S(1)}, bf16[512,1024]{1,0:T(8,128)(2,1)S(1)}, f32[4,4,128,128]{3,2,1,0:T(8,128)S(1)}, f32[4,128,128]{2,1,0:T(8,128)S(1)}) custom-call(bf16[512,1024]{1,0:T(8,128)(2,1)S(1)} %copy-done.2, bf16[512,1024]{1,0:T(8,128)(2,1)S(1)} %copy-done.3, bf16[512,2048]{1,0:T(8,128)(2,1)S(1)} %copy-done, ...), custom_call_target="tpu_custom_call" | custom-call | tf_op jit(solution)/shard_map/f_states/pallas_call | solution.py:224
  6.1 1.6 %collective-permute-start = (f32[4,128,128]{2,1,0:T(8,128)S(1)}, f32[4,128,128]{2,1,0:T(8,128)S(1)}, u32[]{:S(2)}, u32[]{:S(2)}) collective-permute-start(f32[4,128,128]{2,1,0:T(8,128)S(1)} %get-tuple-element.38.refs_1_), channel_id=1, source_target_pairs={{0,2},{2,0},{1,3},{3,1},{4,6},{6,4},{5,7},{7,5},{8,10},{10,8},{9,1... | collective-permute-start | bytes 786440 | tf_op jit(solution)/shard_map/ppermute | solution.py:474
  7.7 1.0 %g_states.1 = (bf16[512,1024]{1,0:T(8,128)(2,1)S(1)}, bf16[512,2048]{1,0:T(8,128)(2,1)S(1)}, f32[8,4,128,128]{3,2,1,0:T(8,128)S(1)}, f32[8,128,128]{2,1,0:T(8,128)S(1)}) custom-call(bf16[512,1024]{1,0:T(8,128)(2,1)S(1)} %copy-done.2, bf16[512,1024]{1,0:T(8,128)(2,1)S(1)} %copy-done.3, bf16[512,2048]{1,0:T(8,128)(2,1)S(1)} %copy-done, ...), custom_call_target="tpu_custom_call" | custom-call | tf_op jit(solution)/shard_map/g_states/pallas_call | solution.py:254
  8.8 1.4 %collective-permute-start.4 = (f32[4,128,128]{2,1,0:T(8,128)S(1)}, f32[4,128,128]{2,1,0:T(8,128)S(1)}, u32[]{:S(2)}, u32[]{:S(2)}) collective-permute-start(f32[4,128,128]{2,1,0:T(8,128)S(1)} %mixed.1.refs_6_), channel_id=1, source_target_pairs={{0,1},{1,0},{2,3},{3,2},{4,5},{5,4},{6,7},{7,6},{8,9},{9,8},{10,11... | collective-permute-start | bytes 786440 | tf_op jit(solution)/shard_map/ppermute | solution.py:484
  10.1 3.6 %local.2 = (f32[512,1792]{1,0:T(8,128)S(1)}, f32[512,896]{1,0:T(8,128)S(1)}, f32[512,1792]{1,0:T(8,128)S(1)}, f32[512,896]{1,0:T(8,128)S(1)}) custom-call(bf16[512,512]{1,0:T(8,128)(2,1)S(1)} %get-tuple-element.43.refs_0_.x.refs_1_, bf16[512,1024]{1,0:T(8,128)(2,1)S(1)} %get-tuple-element.44.refs_1_.y.refs_2_, ...), custom_call_target="tpu_custom_call" | custom-call | tf_op jit(solution)/shard_map/local/pallas_call | solution.py:365
  13.8 0.0 collective-permute-done.1.refs_1_.refs_4_
  13.8 1.0 %collective-permute-start.3 = (f32[4,128,128]{2,1,0:T(8,128)S(1)}, f32[4,128,128]{2,1,0:T(8,128)S(1)}, u32[]{:S(2)}, u32[]{:S(2)}) collective-permute-start(f32[4,128,128]{2,1,0:T(8,128)S(1)} %swapped.1.refs_2_), channel_id=1, source_target_pairs={{0,2},{2,0},{1,3},{3,1},{4,6},{6,4},{5,7},{7,5},{8,10},{10,8},{9,1... | collective-permute-start | bytes 786440 | tf_op jit(solution)/shard_map/ppermute | solution.py:487
  14.8 0.0 collective-permute-done.refs_0_.refs_10_.refs_4_
  14.9 1.6 %collective-permute-start.5 = (f32[2,128,128]{2,1,0:T(8,128)S(1)}, f32[2,128,128]{2,1,0:T(8,128)S(1)}, u32[]{:S(2)}, u32[]{:S(2)}) collective-permute-start(f32[2,128,128]{2,1,0:T(8,128)S(1)} %summed.2.refs_4_.refs_0_), channel_id=1, source_target_pairs={{0,1},{1,0},{2,3},{3,2},{4,5},{5,4},{6,7},{7,6},{8,9},{9,8},{10,11... | collective-permute-start | bytes 393224 | tf_op jit(solution)/shard_map/ppermute | solution.py:496
  16.4 0.5 %first_steps.1.refs_3_ = f32[4,4,128,128]{3,2,1,0:T(8,128)S(1)} custom-call(bf16[512,512]{1,0:T(8,128)(2,1)S(1)} %get-tuple-element.43.refs_0_.x.refs_1_, bf16[512,1024]{1,0:T(8,128)(2,1)S(1)} %get-tuple-element.44.refs_1_.y.refs_2_, f32[2,128,128]{2,1,0:T(8,128)S(1)} %summed.2.refs_4_.refs_0_), custom_call_target="tpu_custom_call" | custom-call | tf_op jit(solution)/shard_map/first_steps/pallas_call | solution.py:270
  16.9 0.6 %local.3 = (f32[512,256]{1,0:T(8,128)S(1)}, f32[512,128]{1,0:T(8,128)S(1)}, f32[512,256]{1,0:T(8,128)S(1)}, f32[512,128]{1,0:T(8,128)S(1)}) custom-call(bf16[512,512]{1,0:T(8,128)(2,1)S(1)} %get-tuple-element.34.refs_4_.refs_0_.refs_8_.refs_1_, bf16[512,1024]{1,0:T(8,128)(2,1)S(1)} %get-tuple-element.35.refs_5_.refs_1_.refs_9_.refs_2_, ...), custom_call_target="tpu_custom_call" | custom-call | tf_op jit(solution)/shard_map/local/pallas_call | solution.py:365
  17.6 0.6 %collective-permute-start.2 = (f32[2,128,128]{2,1,0:T(8,128)S(1)}, f32[2,128,128]{2,1,0:T(8,128)S(1)}, u32[]{:S(2)}, u32[]{:S(2)}) collective-permute-start(f32[2,128,128]{2,1,0:T(8,128)S(1)} %summed.3.refs_11_), channel_id=1, source_target_pairs={{0,1},{1,0},{2,3},{3,2},{4,5},{5,4},{6,7},{7,6},{8,9},{9,8},{10,11... | collective-permute-start | bytes 393224 | tf_op jit(solution)/shard_map/ppermute | solution.py:500
  18.2 0.1 collective-permute-done.4.refs_8_.refs_5_
  18.3 2.1 %near.1 = (bf16[512,2048]{1,0:T(8,128)(2,1)}, bf16[512,1024]{1,0:T(8,128)(2,1)}, bf16[512,1024]{1,0:T(8,128)(2,1)}, bf16[512,2048]{1,0:T(8,128)(2,1)}) custom-call(f32[512,128]{1,0:T(8,128)S(1)} %get-tuple-element.36.scale.refs_0_, bf16[512,1024]{1,0:T(8,128)(2,1)S(1)} %get-tuple-element.40.refs_2_.refs_1_, ...), custom_call_target="tpu_custom_call" | custom-call | tf_op jit(solution)/shard_map/near/pallas_call | solution.py:437
  20.4 1.0 %collective-permute-done.5.refs_11_ = f32[2,128,128]{2,1,0:T(8,128)S(1)} collective-permute-done((f32[2,128,128]{2,1,0:T(8,128)S(1)}, f32[2,128,128]{2,1,0:T(8,128)S(1)}, u32[]{:S(2)}, u32[]{:S(2)}) %collective-permute-start.5) | collective-permute-done | bytes 131104 | tf_op jit(solution)/shard_map/ppermute | solution.py:496
  21.4 0.0 collective-permute-done.3.refs_4_
  21.4 1.8 %far.2 = (bf16[512,2048]{1,0:T(8,128)(2,1)}, bf16[512,1024]{1,0:T(8,128)(2,1)}, bf16[512,1024]{1,0:T(8,128)(2,1)}, bf16[512,2048]{1,0:T(8,128)(2,1)}) custom-call(f32[512,128]{1,0:T(8,128)S(1)} %get-tuple-element.33.scale.refs_0_, ...), custom_call_target="tpu_custom_call", output_to_operand_aliasing={{0}: (12, {}), {1}: (13, {}), {2}: (14, {}), {3}: (15, {})} | custom-call | tf_op jit(solution)/shard_map/far/pallas_call | solution.py:437
  23.2 0.0 collective-permute-done.2.refs_5_
  23.2 1.1 %far.3 = (bf16[512,2048]{1,0:T(8,128)(2,1)}, bf16[512,1024]{1,0:T(8,128)(2,1)}, bf16[512,1024]{1,0:T(8,128)(2,1)}, bf16[512,2048]{1,0:T(8,128)(2,1)}) custom-call(f32[512,128]{1,0:T(8,128)S(1)} %get-tuple-element.33.scale.refs_0_, ...), custom_call_target="tpu_custom_call", output_to_operand_aliasing={{0}: (10, {}), {1}: (11, {}), {2}: (12, {}), {3}: (13, {})} | custom-call | tf_op jit(solution)/shard_map/far/pallas_call | solution.py:437
  (4 shorter events, 0.1 us)
Async XLA Ops:
  0.6 4.9 %copy-start.1 = (bf16[512,2048]{1,0:T(8,128)(2,1)S(1)}, bf16[512,2048]{1,0:T(8,128)(2,1)}, u32[]{:S(2)}) copy-start(bf16[512,2048]{1,0:T(8,128)(2,1)} %do.5) | copy-start | bytes 6291460
  0.6 4.9 %copy-start = (bf16[512,2048]{1,0:T(8,128)(2,1)S(1)}, bf16[512,2048]{1,0:T(8,128)(2,1)}, u32[]{:S(2)}) copy-start(bf16[512,2048]{1,0:T(8,128)(2,1)} %v.5) | copy-start | bytes 6291460
  0.7 4.9 %copy-start.3 = (bf16[512,1024]{1,0:T(8,128)(2,1)S(1)}, bf16[512,1024]{1,0:T(8,128)(2,1)}, u32[]{:S(2)}) copy-start(bf16[512,1024]{1,0:T(8,128)(2,1)} %k.5) | copy-start | bytes 3145732
  0.7 4.9 %copy-start.2 = (bf16[512,1024]{1,0:T(8,128)(2,1)S(1)}, bf16[512,1024]{1,0:T(8,128)(2,1)}, u32[]{:S(2)}) copy-start(bf16[512,1024]{1,0:T(8,128)(2,1)} %q.5) | copy-start | bytes 3145732
  2.5 11.3 %collective-permute-start.1 = (f32[4,128,128]{2,1,0:T(8,128)S(1)}, f32[4,128,128]{2,1,0:T(8,128)S(1)}, u32[]{:S(2)}, u32[]{:S(2)}) collective-permute-start(f32[4,128,128]{2,1,0:T(8,128)S(1)} %get-tuple-element.42.refs_0_), channel_id=1, source_target_pairs={{0,1},{1,0},{2,3},{3,2},{4,5},{5,4},{6,7},{7,6},{8,9},{9,8},{10,11... | collective-permute-start | bytes 786440 | tf_op jit(solution)/shard_map/ppermute | solution.py:471
  6.1 8.8 %collective-permute-start = (f32[4,128,128]{2,1,0:T(8,128)S(1)}, f32[4,128,128]{2,1,0:T(8,128)S(1)}, u32[]{:S(2)}, u32[]{:S(2)}) collective-permute-start(f32[4,128,128]{2,1,0:T(8,128)S(1)} %get-tuple-element.38.refs_1_), channel_id=1, source_target_pairs={{0,2},{2,0},{1,3},{3,1},{4,6},{6,4},{5,7},{7,5},{8,10},{10,8},{9,1... | collective-permute-start | bytes 786440 | tf_op jit(solution)/shard_map/ppermute | solution.py:474
  8.8 9.5 %collective-permute-start.4 = (f32[4,128,128]{2,1,0:T(8,128)S(1)}, f32[4,128,128]{2,1,0:T(8,128)S(1)}, u32[]{:S(2)}, u32[]{:S(2)}) collective-permute-start(f32[4,128,128]{2,1,0:T(8,128)S(1)} %mixed.1.refs_6_), channel_id=1, source_target_pairs={{0,1},{1,0},{2,3},{3,2},{4,5},{5,4},{6,7},{7,6},{8,9},{9,8},{10,11... | collective-permute-start | bytes 786440 | tf_op jit(solution)/shard_map/ppermute | solution.py:484
  13.8 7.5 %collective-permute-start.3 = (f32[4,128,128]{2,1,0:T(8,128)S(1)}, f32[4,128,128]{2,1,0:T(8,128)S(1)}, u32[]{:S(2)}, u32[]{:S(2)}) collective-permute-start(f32[4,128,128]{2,1,0:T(8,128)S(1)} %swapped.1.refs_2_), channel_id=1, source_target_pairs={{0,2},{2,0},{1,3},{3,1},{4,6},{6,4},{5,7},{7,5},{8,10},{10,8},{9,1... | collective-permute-start | bytes 786440 | tf_op jit(solution)/shard_map/ppermute | solution.py:487
  14.9 6.5 %collective-permute-start.5 = (f32[2,128,128]{2,1,0:T(8,128)S(1)}, f32[2,128,128]{2,1,0:T(8,128)S(1)}, u32[]{:S(2)}, u32[]{:S(2)}) collective-permute-start(f32[2,128,128]{2,1,0:T(8,128)S(1)} %summed.2.refs_4_.refs_0_), channel_id=1, source_target_pairs={{0,1},{1,0},{2,3},{3,2},{4,5},{5,4},{6,7},{7,6},{8,9},{9,8},{10,11... | collective-permute-start | bytes 393224 | tf_op jit(solution)/shard_map/ppermute | solution.py:496
  17.6 5.6 %collective-permute-start.2 = (f32[2,128,128]{2,1,0:T(8,128)S(1)}, f32[2,128,128]{2,1,0:T(8,128)S(1)}, u32[]{:S(2)}, u32[]{:S(2)}) collective-permute-start(f32[2,128,128]{2,1,0:T(8,128)S(1)} %summed.3.refs_11_), channel_id=1, source_target_pairs={{0,1},{1,0},{2,3},{3,2},{4,5},{5,4},{6,7},{7,6},{8,9},{9,8},{10,11... | collective-permute-start | bytes 393224 | tf_op jit(solution)/shard_map/ppermute | solution.py:500
